TPU v7x, 32 devices: a whole 2x2x4 slice. The times are simulated.
32 devices in a mesh: group: 1, expert: 32 (over z, y, x, core).
Axes of the slice: x: 2, y: 2, z: 4, core: 2. Of those that a mesh axis runs over, the one named last changes fastest.
Arguments:
- tokens: bfloat16 [1024, 2048], P(('group', 'expert')), may hold values from -6 to 6
- upstream: bfloat16 [1024, 2048], P(('group', 'expert')), may hold values from -6 to 6
- expert_ids: int32 [1024, 8], P(('group', 'expert')), may hold values from 0 to 15, all different within a row; in each aligned block of 32 rows (0 to 31, 32 to 63, ...) at most 24 rows name the same one
- gate_weights: bfloat16 [1024, 8], P(('group', 'expert')), may hold values from 0.049804688 to 1
- w_gate: bfloat16 [2048, 12288], P('group', 'expert'), may hold values from -0.125 to 0.125
- w_up: bfloat16 [2048, 12288], P('group', 'expert'), may hold values from -0.125 to 0.125
- w_down: bfloat16 [12288, 2048], P('expert', 'group'), may hold values from -0.21875 to 0.21875
Outputs:
- grad_tokens: bfloat16 [1024, 2048], P(('group', 'expert'))
- grad_gates: bfloat16 [1024, 8], P(('group', 'expert'))
- grad_w_gate: bfloat16 [2048, 12288], P('group', 'expert')
- grad_w_up: bfloat16 [2048, 12288], P('group', 'expert')
- grad_w_down: bfloat16 [12288, 2048], P('expert', 'group')
Inputs may be any that keep to these rules, and one draw needn't show every extreme that they name: `expert_ids`: each token names 8 different experts. Within the 32 tokens of one index of expert, no expert is named more than 24 times, a bound that some block reaches.
All inputs are finite; a program needn't handle non-finite values.
Results may differ from a plain program's by a relative error of at most 0.0095.
Values may be sent and summed in bfloat16 or wider, within the bound.
No kernel may reach another device: no remote copies, remote signals or barrier semaphores. Data moves between devices by JAX's collectives and lax.ppermute only.
A program may use at most 128 MiB of HBM per device.

v0:
```python
import jax
import jax.numpy as jnp
from jax import lax
from jax.sharding import PartitionSpec as P


def partner_2(block, axis, apart):
    count = lax.axis_size(axis)
    route = []
    for low in range(count):
        high = low | 1 << apart
        if high != low and high < count:
            route += [(low, high), (high, low)]
    return lax.ppermute(block, axis, route)


def contract(left_side, right_side, left_axis, right_axis):
    return lax.dot_general(
        left_side,
        right_side,
        (((left_axis,), (right_axis,)), ((), ())),
        preferred_element_type=jnp.float32,
    )


def half_terms(inputs, upward, gating, gate_half, up_half, down_half):
    pre_gate = contract(inputs, gate_half, 1, 0)
    pre_up = contract(inputs, up_half, 1, 0)
    logistic = jax.nn.sigmoid(pre_gate)
    activated = pre_gate * logistic
    hidden = (activated * pre_up).astype(jnp.bfloat16)
    backward = contract(upward, down_half, 1, 1)
    gate_part = jnp.sum(hidden.astype(jnp.float32) * backward, axis=1).astype(jnp.bfloat16)
    grad_hidden = gating.astype(jnp.float32)[:, None] * backward
    grad_gate = (grad_hidden * pre_up * logistic * (1.0 + pre_gate * (1.0 - logistic))).astype(
        jnp.bfloat16
    )
    grad_up = (grad_hidden * activated).astype(jnp.bfloat16)
    token_part = (contract(grad_gate, gate_half, 1, 1) + contract(grad_up, up_half, 1, 1)).astype(
        jnp.bfloat16
    )
    return (token_part, gate_part, grad_gate, grad_up, hidden)


def half_grads(inputs, scaled, grad_gate, grad_up, hidden):
    return (
        contract(inputs, grad_gate, 0, 0),
        contract(inputs, grad_up, 0, 0),
        contract(hidden, scaled, 0, 0),
    )


def scale_rows(gating, upward):
    return (gating.astype(jnp.float32)[:, None] * upward.astype(jnp.float32)).astype(jnp.bfloat16)


def local(tokens, upstream, expert_ids, gate_weights, w_gate, w_up, w_down):
    tok_count, model_width = tokens.shape
    top_count = expert_ids.shape[1]
    groups = lax.axis_size("expert")
    experts = groups // 2
    capacity = min(tok_count, 2 * ((tok_count * top_count * 3 + 4 * experts - 1) // (4 * experts)))
    half_slots = capacity // 2
    row_count = groups * half_slots
    flat_ids = expert_ids.reshape(-1)
    onehot = (flat_ids[:, None] == jnp.arange(experts, dtype=jnp.int32)[None, :]).astype(jnp.int32)
    rank_in = jnp.sum((jnp.cumsum(onehot, axis=0) - onehot) * onehot, axis=1)
    slot_index = flat_ids * capacity + rank_in
    pair_index = jnp.arange(tok_count * top_count, dtype=jnp.int32)
    slot_owner = jnp.zeros((experts * capacity,), jnp.int32).at[slot_index].set(pair_index)
    filled = jnp.zeros((experts * capacity,), jnp.bool_).at[slot_index].set(True)
    source = slot_owner // top_count
    sent_rows = jnp.where(filled[:, None], tokens[source], jnp.zeros((), tokens.dtype))
    sent_grads = jnp.where(filled[:, None], upstream[source], jnp.zeros((), upstream.dtype))
    sent_gates = jnp.where(
        filled, gate_weights.reshape(-1)[slot_owner], jnp.zeros((), gate_weights.dtype)
    )
    in_rows, in_grads, in_gates = (
        lax.all_to_all(
            sent_rows.reshape(groups, half_slots, model_width),
            "expert",
            split_axis=0,
            concat_axis=0,
            tiled=True,
        ),
        lax.all_to_all(
            sent_grads.reshape(groups, half_slots, model_width),
            "expert",
            split_axis=0,
            concat_axis=0,
            tiled=True,
        ),
        lax.all_to_all(
            sent_gates.reshape(groups, half_slots),
            "expert",
            split_axis=0,
            concat_axis=0,
            tiled=True,
        ),
    )
    in_rows = in_rows.reshape(row_count, model_width)
    in_grads = in_grads.reshape(row_count, model_width)
    in_gates = in_gates.reshape(row_count)
    partner = partner_2((w_gate, w_up, w_down), "expert", 0)
    own_terms = half_terms(in_rows, in_grads, in_gates, w_gate, w_up, w_down)
    other_terms = half_terms(in_rows, in_grads, in_gates, partner[0], partner[1], partner[2])
    token_sum = (own_terms[0].astype(jnp.float32) + other_terms[0].astype(jnp.float32)).astype(
        jnp.bfloat16
    )
    gate_sum = (own_terms[1].astype(jnp.float32) + other_terms[1].astype(jnp.float32)).astype(
        jnp.bfloat16
    )
    scaled = scale_rows(in_gates, in_grads)
    own_grads = half_grads(in_rows, scaled, own_terms[2], own_terms[3], own_terms[4])
    lent = half_grads(in_rows, scaled, other_terms[2], other_terms[3], other_terms[4])
    returned = partner_2((lent[0], lent[1], lent[2]), "expert", 0)
    grad_w_gate = (own_grads[0] + returned[0]).astype(jnp.bfloat16)
    grad_w_up = (own_grads[1] + returned[1]).astype(jnp.bfloat16)
    grad_w_down = (own_grads[2] + returned[2]).astype(jnp.bfloat16)
    out_tokens, out_gates = (
        lax.all_to_all(
            token_sum.reshape(groups, half_slots, model_width),
            "expert",
            split_axis=0,
            concat_axis=0,
            tiled=True,
        ),
        lax.all_to_all(
            gate_sum.reshape(groups, half_slots), "expert", split_axis=0, concat_axis=0, tiled=True
        ),
    )
    flat_tokens = out_tokens.reshape(experts * capacity, model_width)
    per_pair = flat_tokens[slot_index].reshape(tok_count, top_count, model_width)
    grad_tokens = jnp.sum(per_pair.astype(jnp.float32), axis=1).astype(jnp.bfloat16)
    grad_gates = out_gates.reshape(-1)[slot_index].reshape(tok_count, top_count)
    return (grad_tokens, grad_gates, grad_w_gate, grad_w_up, grad_w_down)


def solution(mesh):
    return jax.shard_map(
        local,
        mesh=mesh,
        in_specs=(
            P(("group", "expert"), None),
            P(("group", "expert"), None),
            P(("group", "expert"), None),
            P(("group", "expert"), None),
            P("group", "expert"),
            P("group", "expert"),
            P("expert", "group"),
        ),
        out_specs=(
            P(("group", "expert"), None),
            P(("group", "expert"), None),
            P("group", "expert"),
            P("group", "expert"),
            P("expert", "group"),
        ),
        check_vma=False,
    )
```

profile of v0, /device:TPU:0, one launch (start us, length us, event | category | flops | bytes accessed | tf_op | source)
XLA Modules:
  0.0 254.2 jit_solution(12310788982249513246)
XLA Ops:
  10.7 7.3 %all-to-all-start = ((bf16[32,1,12]{2,1,0:T(2,128)(2,1)}), bf16[32,1,12]{2,1,0:T(2,128)(2,1)S(1)}, u32[]{:S(2)}, u32[]{:S(2)}) async-start(bf16[32,1,12]{2,1,0:T(2,128)(2,1)} %all_to_all.25), calls=%async_computation | async-start | bytes 32768 | tf_op jit(solution)/shard_map/all_to_all | solution.py:93
  18.1 3.1 %gather_fusion.1 = bf16[384,2048]{1,0:T(8,128)(2,1)} fusion(bf16[32,2048]{1,0:T(8,128)(2,1)S(1)} %copy-done, s32[1024]{0:T(1024)S(1)} %get-tuple-element.27), kind=kCustom, calls=%fused_computation.1 | custom fusion | bytes 3147264 | tf_op jit(solution)/shard_map/gather | solution.py:74
  23.6 3.1 %gather_fusion.2 = bf16[384,2048]{1,0:T(8,128)(2,1)} fusion(bf16[32,2048]{1,0:T(8,128)(2,1)S(1)} %copy-done.2, s32[1024]{0:T(1024)S(1)} %get-tuple-element.27), kind=kCustom, calls=%fused_computation.2 | custom fusion | bytes 3147264 | tf_op jit(solution)/shard_map/gather | solution.py:73
  26.7 3.6 %gather.23 = bf16[32,12,2048]{2,1,0:T(8,128)(2,1)} reshape(bf16[384,2048]{1,0:T(8,128)(2,1)} %gather_fusion.2) | data formatting | bytes 3145728 | tf_op jit(solution)/shard_map/gather | solution.py:73
  30.4 3.9 %broadcast_select_fusion.1 = (bf16[32,12,2048]{2,1,0:T(8,128)(2,1)}, bf16[32,12,2048]{2,1,0:T(8,128)(2,1)}) fusion(bf16[32,12,2048]{2,1,0:T(8,128)(2,1)S(1)} %gather.21, pred[32,12]{1,0:T(8,128)(4,1)S(1)} %broadcast_in_dim.49, bf16[32,12,2048]{2,1,0:T(8,128)(2,1)} %gather.23), kind=kLoop, calls=%fused_computation.15 | loop fusion | flops 1572864 | bytes 6291840 | tf_op jit(solution)/shard_map/jit(_where)/select_n | solution.py:74
  34.2 54.7 %all_to_all.31 = bf16[32,12,2048]{2,1,0:T(8,128)(2,1)} all-to-all(bf16[32,12,2048]{2,1,0:T(8,128)(2,1)} %get-tuple-element.24), channel_id=1, replica_groups=mesh['group'=1,'expert'=32] {'expert'}, dimensions={0} | all-to-all | bytes 3145728 | tf_op jit(solution)/shard_map/all_to_all | solution.py:79
  88.9 4.0 %all-to-all-start.1 = ((bf16[32,12,2048]{2,1,0:T(8,128)(2,1)}), bf16[32,12,2048]{2,1,0:T(8,128)(2,1)}, u32[]{:S(2)}, u32[]{:S(2)}) async-start(bf16[32,12,2048]{2,1,0:T(8,128)(2,1)} %get-tuple-element.23), calls=%async_computation.1 | async-start | bytes 4194304 | tf_op jit(solution)/shard_map/all_to_all | solution.py:86
  96.2 3.3 %fusion.13 = f32[384,384]{0,1:T(8,128)} fusion(bf16[384,2048]{1,0:T(8,128)(2,1)S(1)} %reshape.154, bf16[2048,384]{1,0:T(8,128)(2,1)} %param.12), kind=kOutput, calls=%fused_computation.60 | convolution fusion | flops 603979776 | bytes 3735552 | tf_op jit(solution)/shard_map/dot_general | solution.py:18
  99.4 3.2 %fusion.14 = f32[384,384]{0,1:T(8,128)} fusion(bf16[384,2048]{1,0:T(8,128)(2,1)S(1)} %reshape.154, bf16[2048,384]{1,0:T(8,128)(2,1)} %param.11), kind=kOutput, calls=%fused_computation.61 | convolution fusion | flops 603979776 | bytes 3735552 | tf_op jit(solution)/shard_map/dot_general | solution.py:18
  102.7 38.9 %all-to-all-done.1 = bf16[32,12,2048]{2,1,0:T(8,128)(2,1)} async-done(((bf16[32,12,2048]{2,1,0:T(8,128)(2,1)}), bf16[32,12,2048]{2,1,0:T(8,128)(2,1)}, u32[]{:S(2)}, u32[]{:S(2)}) %all-to-all-start.1) | async-done | bytes 1572896 | tf_op jit(solution)/shard_map/all_to_all | solution.py:86
  144.1 3.0 %fusion.16 = f32[384,384]{0,1:T(8,128)S(1)} fusion(bf16[384,2048]{1,0:T(8,128)(2,1)S(1)} %reshape.154, bf16[2048,384]{1,0:T(8,128)(2,1)} %collective-permute-done.1), kind=kOutput, calls=%fused_computation.63 | convolution fusion | flops 603979776 | bytes 3735552 | tf_op jit(solution)/shard_map/dot_general | solution.py:18
  149.7 3.4 %multiply_reduce_fusion.1 = (bf16[384]{0:T(512)(128)(2,1)S(1)}, bf16[384,384]{0,1:T(8,128)(2,1)}, bf16[384,384]{0,1:T(8,128)(2,1)S(1)}, bf16[384,384]{0,1:T(8,128)(2,1)}) fusion(f32[384,384]{0,1:T(8,128)S(1)} %copy-done.12, f32[384,384]{0,1:T(8,128)S(1)} %copy-done.13, f32[384]{0:T(512)S(1)} %reshape.160, bf16[384,2048]{1,0:T(8,128)(2,1)S(1)} %reshape.153, ...), kind=kOutput, calls=%fused_computation.20 | convolution fusion | flops 606781056 | bytes 5212416 | tf_op jit(solution)/shard_map/dot_general | solution.py:18
  153.2 4.2 %fusion.15 = f32[384,2048]{1,0:T(8,128)} fusion(bf16[384,384]{0,1:T(8,128)(2,1)S(1)} %get-tuple-element.19, bf16[2048,384]{1,0:T(8,128)(2,1)} %param.11), kind=kOutput, calls=%fused_computation.62 | convolution fusion | flops 603979776 | bytes 5013504 | tf_op jit(solution)/shard_map/dot_general | solution.py:18
  157.4 3.5 %multiply_reduce_fusion = (bf16[384]{0:T(512)(128)(2,1)S(1)}, bf16[384,384]{0,1:T(8,128)(2,1)}, bf16[384,384]{0,1:T(8,128)(2,1)}, bf16[384,384]{0,1:T(8,128)(2,1)}) fusion(f32[384,384]{0,1:T(8,128)S(1)} %fusion.16, f32[384,384]{0,1:T(8,128)S(1)} %fusion.17, f32[384]{0:T(512)S(1)} %reshape.160, bf16[384,2048]{1,0:T(8,128)(2,1)S(1)} %reshape.153, ...), kind=kOutput, calls=%fused_computation.18 | convolution fusion | flops 606781056 | bytes 5212416 | tf_op jit(solution)/shard_map/dot_general | solution.py:18
  161.6 4.0 %all-to-all-start.4 = ((bf16[32,1,12]{2,1,0:T(2,128)(2,1)}), bf16[32,1,12]{2,1,0:T(2,128)(2,1)S(1)}, u32[]{:S(2)}, u32[]{:S(2)}) async-start(bf16[32,1,12]{2,1,0:T(2,128)(2,1)} %convert_element_type.166), calls=%async_computation.4 | async-start | bytes 32768 | tf_op jit(solution)/shard_map/all_to_all | solution.py:128
  165.6 3.5 %add_convert_fusion.5 = bf16[384,2048]{1,0:T(8,128)(2,1)S(1)} fusion(f32[384,2048]{1,0:T(8,128)} %fusion.15, bf16[384,384]{0,1:T(8,128)(2,1)} %get-tuple-element.22, bf16[2048,384]{1,0:T(8,128)(2,1)} %param.12), kind=kOutput, calls=%fused_computation.13 | convolution fusion | flops 605552640 | bytes 6586368 | tf_op jit(solution)/shard_map/dot_general | solution.py:18
  171.7 3.6 %add_convert_fusion.3 = bf16[384,2048]{1,0:T(8,128)(2,1)} fusion(bf16[384,2048]{1,0:T(8,128)(2,1)S(1)} %add_convert_fusion.5, f32[384,2048]{1,0:T(8,128)S(1)} %fusion.18, bf16[384,384]{0,1:T(8,128)(2,1)S(1)} %copy-done.9, bf16[2048,384]{1,0:T(8,128)(2,1)} %collective-permute-done.2), kind=kOutput, calls=%fused_computation.11 | convolution fusion | flops 608698368 | bytes 8159232 | tf_op jit(solution)/shard_map/dot_general | solution.py:18
  175.3 3.6 %reshape.155 = bf16[32,12,2048]{2,1,0:T(8,128)(2,1)} reshape(bf16[384,2048]{1,0:T(8,128)(2,1)} %add_convert_fusion.3) | data formatting | bytes 3145728 | tf_op jit(solution)/shard_map/reshape | solution.py:122
  178.9 6.2 %all-to-all-start.3 = ((bf16[32,12,2048]{2,1,0:T(8,128)(2,1)}), bf16[32,12,2048]{2,1,0:T(8,128)(2,1)}, u32[]{:S(2)}, u32[]{:S(2)}) async-start(bf16[32,12,2048]{2,1,0:T(8,128)(2,1)} %reshape.155), calls=%async_computation.3 | async-start | bytes 4194304 | tf_op jit(solution)/shard_map/all_to_all | solution.py:121
  185.1 3.9 %fusion.19 = f32[2048,384]{1,0:T(8,128)} fusion(bf16[384,2048]{1,0:T(8,128)(2,1)S(1)} %reshape.154, bf16[384,384]{0,1:T(8,128)(2,1)} %get-tuple-element.20), kind=kOutput, calls=%fused_computation.66 | convolution fusion | flops 603979776 | bytes 5013504 | tf_op jit(solution)/shard_map/dot_general | solution.py:18
  197.9 35.9 %all-to-all-done.3 = bf16[32,12,2048]{2,1,0:T(8,128)(2,1)} async-done(((bf16[32,12,2048]{2,1,0:T(8,128)(2,1)}), bf16[32,12,2048]{2,1,0:T(8,128)(2,1)}, u32[]{:S(2)}, u32[]{:S(2)}) %all-to-all-start.3) | async-done | bytes 1572896 | tf_op jit(solution)/shard_map/all_to_all | solution.py:121
  241.2 4.4 %add_convert_fusion.2 = bf16[2048,384]{1,0:T(8,128)(2,1)} fusion(f32[2048,384]{1,0:T(8,128)} %collective-permute-done.3, bf16[384,2048]{1,0:T(8,128)(2,1)S(1)} %reshape.154, bf16[384,384]{0,1:T(8,128)(2,1)} %copy-done.6), kind=kOutput, calls=%fused_computation.10 | convolution fusion | flops 605552640 | bytes 6586368 | tf_op jit(solution)/shard_map/dot_general | solution.py:18
  245.6 4.4 %add_convert_fusion.1 = bf16[2048,384]{1,0:T(8,128)(2,1)} fusion(f32[2048,384]{1,0:T(8,128)} %collective-permute-done.4, bf16[384,2048]{1,0:T(8,128)(2,1)S(1)} %reshape.154, bf16[384,384]{0,1:T(8,128)(2,1)S(1)} %copy-done.5), kind=kOutput, calls=%fused_computation.9 | convolution fusion | flops 605552640 | bytes 6586368 | tf_op jit(solution)/shard_map/dot_general | solution.py:18
  250.0 4.2 %add_convert_fusion = bf16[384,2048]{1,0:T(8,128)(2,1)} fusion(f32[384,2048]{1,0:T(8,128)} %collective-permute-done.5, bf16[384,384]{0,1:T(8,128)(2,1)S(1)} %copy-done.11, bf16[384,2048]{1,0:T(8,128)(2,1)S(1)} %copy-done.4, f32[384]{0:T(512)S(1)} %reshape.160), kind=kOutput, calls=%fused_computation.7 | convolution fusion | flops 607911936 | bytes 6587904 | tf_op jit(solution)/shard_map/dot_general | solution.py:18
  (87 shorter events, 40.4 us)
Async XLA Ops:
  0.6 17.5 %copy-start = (bf16[32,2048]{1,0:T(8,128)(2,1)S(1)}, bf16[32,2048]{1,0:T(8,128)(2,1)}, u32[]{:S(2)}) copy-start(bf16[32,2048]{1,0:T(8,128)(2,1)} %param.8) | copy-start | bytes 393220
  10.7 23.5 %all-to-all-start = ((bf16[32,1,12]{2,1,0:T(2,128)(2,1)}), bf16[32,1,12]{2,1,0:T(2,128)(2,1)S(1)}, u32[]{:S(2)}, u32[]{:S(2)}) async-start(bf16[32,1,12]{2,1,0:T(2,128)(2,1)} %all_to_all.25), calls=%async_computation | async-start | bytes 32768 | tf_op jit(solution)/shard_map/all_to_all | solution.py:93
  21.2 2.4 copy-start.2
  88.9 52.7 %all-to-all-start.1 = ((bf16[32,12,2048]{2,1,0:T(8,128)(2,1)}), bf16[32,12,2048]{2,1,0:T(8,128)(2,1)}, u32[]{:S(2)}, u32[]{:S(2)}) async-start(bf16[32,12,2048]{2,1,0:T(8,128)(2,1)} %get-tuple-element.23), calls=%async_computation.1 | async-start | bytes 4194304 | tf_op jit(solution)/shard_map/all_to_all | solution.py:86
  92.9 51.3 %collective-permute-start.1 = (bf16[2048,384]{1,0:T(8,128)(2,1)}, bf16[2048,384]{1,0:T(8,128)(2,1)}, u32[]{:S(2)}, u32[]{:S(2)}) collective-permute-start(bf16[2048,384]{1,0:T(8,128)(2,1)} %param.12), channel_id=1, source_target_pairs={{0,1},{1,0},{2,3},{3,2},{4,5},{5,4},{6,7},{7,6},{8,9},{9,8},{10,11... | collective-permute-start | bytes 4718600 | tf_op jit(solution)/shard_map/ppermute | solution.py:14
  92.9 54.2 %collective-permute-start.2 = (bf16[2048,384]{1,0:T(8,128)(2,1)}, bf16[2048,384]{1,0:T(8,128)(2,1)}, u32[]{:S(2)}, u32[]{:S(2)}) collective-permute-start(bf16[2048,384]{1,0:T(8,128)(2,1)} %param.11), channel_id=1, source_target_pairs={{0,1},{1,0},{2,3},{3,2},{4,5},{5,4},{6,7},{7,6},{8,9},{9,8},{10,11... | collective-permute-start | bytes 4718600 | tf_op jit(solution)/shard_map/ppermute | solution.py:14
  93.4 63.9 %collective-permute-start = (bf16[384,2048]{1,0:T(8,128)(2,1)}, bf16[384,2048]{1,0:T(8,128)(2,1)}, u32[]{:S(2)}, u32[]{:S(2)}) collective-permute-start(bf16[384,2048]{1,0:T(8,128)(2,1)} %param.13), channel_id=1, source_target_pairs={{0,1},{1,0},{2,3},{3,2},{4,5},{5,4},{6,7},{7,6},{8,9},{9,8},{10,11... | collective-permute-start | bytes 4718600 | tf_op jit(solution)/shard_map/ppermute | solution.py:14
  144.1 48.2 %copy-start.3 = (bf16[384,2048]{1,0:T(8,128)(2,1)}, bf16[384,2048]{1,0:T(8,128)(2,1)S(1)}, u32[]{:S(2)}) copy-start(bf16[384,2048]{1,0:T(8,128)(2,1)S(1)} %reshape.153) | copy-start | bytes 4718596
  147.1 2.6 %copy-start.12 = (f32[384,384]{0,1:T(8,128)S(1)}, f32[384,384]{0,1:T(8,128)}, u32[]{:S(2)}) copy-start(f32[384,384]{0,1:T(8,128)} %fusion.13) | copy-start | bytes 1769476
  147.1 2.6 %copy-start.13 = (f32[384,384]{0,1:T(8,128)S(1)}, f32[384,384]{0,1:T(8,128)}, u32[]{:S(2)}) copy-start(f32[384,384]{0,1:T(8,128)} %fusion.14) | copy-start | bytes 1769476
  153.1 4.2 %copy-start.6 = (bf16[384,384]{0,1:T(8,128)(2,1)}, bf16[384,384]{0,1:T(8,128)(2,1)S(1)}, u32[]{:S(2)}) copy-start(bf16[384,384]{0,1:T(8,128)(2,1)S(1)} %get-tuple-element.19) | copy-start | bytes 884740
  161.6 17.3 %all-to-all-start.4 = ((bf16[32,1,12]{2,1,0:T(2,128)(2,1)}), bf16[32,1,12]{2,1,0:T(2,128)(2,1)S(1)}, u32[]{:S(2)}, u32[]{:S(2)}) async-start(bf16[32,1,12]{2,1,0:T(2,128)(2,1)} %convert_element_type.166), calls=%async_computation.4 | async-start | bytes 32768 | tf_op jit(solution)/shard_map/all_to_all | solution.py:128
  165.6 3.5 %copy-start.7 = (bf16[384,384]{0,1:T(8,128)(2,1)S(1)}, bf16[384,384]{0,1:T(8,128)(2,1)}, u32[]{:S(2)}) copy-start(bf16[384,384]{0,1:T(8,128)(2,1)} %get-tuple-element.21) | copy-start | bytes 884740
  169.2 2.5 copy-start.9
  178.9 54.9 %all-to-all-start.3 = ((bf16[32,12,2048]{2,1,0:T(8,128)(2,1)}), bf16[32,12,2048]{2,1,0:T(8,128)(2,1)}, u32[]{:S(2)}, u32[]{:S(2)}) async-start(bf16[32,12,2048]{2,1,0:T(8,128)(2,1)} %reshape.155), calls=%async_computation.3 | async-start | bytes 4194304 | tf_op jit(solution)/shard_map/all_to_all | solution.py:121
  185.1 3.9 %copy-start.8 = (bf16[384,384]{0,1:T(8,128)(2,1)S(1)}, bf16[384,384]{0,1:T(8,128)(2,1)}, u32[]{:S(2)}) copy-start(bf16[384,384]{0,1:T(8,128)(2,1)} %get-tuple-element.21) | copy-start | bytes 884740
  189.0 3.3 %copy-start.10 = (bf16[384,384]{0,1:T(8,128)(2,1)S(1)}, bf16[384,384]{0,1:T(8,128)(2,1)}, u32[]{:S(2)}) copy-start(bf16[384,384]{0,1:T(8,128)(2,1)} %get-tuple-element.18) | copy-start | bytes 884740
  189.0 52.3 %collective-permute-start.3 = (f32[2048,384]{1,0:T(8,128)}, f32[2048,384]{1,0:T(8,128)}, u32[]{:S(2)}, u32[]{:S(2)}) collective-permute-start(f32[2048,384]{1,0:T(8,128)} %fusion.19), channel_id=1, source_target_pairs={{0,1},{1,0},{2,3},{3,2},{4,5},{5,4},{6,7},{7,6},{8,9},{9,8},{10,11... | collective-permute-start | bytes 9437192 | tf_op jit(solution)/shard_map/ppermute | solution.py:14
  191.8 53.8 %collective-permute-start.4 = (f32[2048,384]{1,0:T(8,128)}, f32[2048,384]{1,0:T(8,128)}, u32[]{:S(2)}, u32[]{:S(2)}) collective-permute-start(f32[2048,384]{1,0:T(8,128)} %fusion.20), channel_id=1, source_target_pairs={{0,1},{1,0},{2,3},{3,2},{4,5},{5,4},{6,7},{7,6},{8,9},{9,8},{10,11... | collective-permute-start | bytes 9437192 | tf_op jit(solution)/shard_map/ppermute | solution.py:14
  195.0 54.9 %collective-permute-start.5 = (f32[384,2048]{1,0:T(8,128)}, f32[384,2048]{1,0:T(8,128)}, u32[]{:S(2)}, u32[]{:S(2)}) collective-permute-start(f32[384,2048]{1,0:T(8,128)} %fusion), channel_id=1, source_target_pairs={{0,1},{1,0},{2,3},{3,2},{4,5},{5,4},{6,7},{7,6},{8,9},{9,8},{10,11... | collective-permute-start | bytes 9437192 | tf_op jit(solution)/shard_map/ppermute | solution.py:14
  241.2 4.4 %copy-start.5 = (bf16[384,384]{0,1:T(8,128)(2,1)S(1)}, bf16[384,384]{0,1:T(8,128)(2,1)}, u32[]{:S(2)}) copy-start(bf16[384,384]{0,1:T(8,128)(2,1)} %get-tuple-element.22) | copy-start | bytes 884740
  245.6 4.4 %copy-start.4 = (bf16[384,2048]{1,0:T(8,128)(2,1)S(1)}, bf16[384,2048]{1,0:T(8,128)(2,1)}, u32[]{:S(2)}) copy-start(bf16[384,2048]{1,0:T(8,128)(2,1)} %copy-done.3) | copy-start | bytes 4718596
  245.6 4.4 %copy-start.11 = (bf16[384,384]{0,1:T(8,128)(2,1)S(1)}, bf16[384,384]{0,1:T(8,128)(2,1)}, u32[]{:S(2)}) copy-start(bf16[384,384]{0,1:T(8,128)(2,1)} %get-tuple-element.16) | copy-start | bytes 884740
  250.0 4.2 %copy-start.1 = (bf16[32,2048]{1,0:T(8,128)(2,1)S(1)}, bf16[32,2048]{1,0:T(8,128)(2,1)}, u32[]{:S(2)}) copy-start(bf16[32,2048]{1,0:T(8,128)(2,1)} %param.8) | copy-start | bytes 393220
where the time goes:
time: 255 us; the launch traced here: 254 us
  waiting for transfers between devices  74.8 us (29%)
  matrix products  55.2 us (22%)
  blocking collectives  54.7 us (21%)
  local copies, waits for them, and re-layouts  37.9 us (15%)
  starting transfers between devices  22.6 us (9%)
  other arithmetic  8.06 us (3%)
    dot_general x16, matrix products, contract(): lax.dot_general(left_side, right_side, (((left_axis,), (right_axis,)), ((...  55.2 us
    all_to_all x1, blocking collectives, local(): lax.all_to_all(sent_rows.reshape(groups, half_slots, model_width), 'exper...  54.7 us
    all_to_all x1, waiting for transfers between devices, local(): lax.all_to_all(sent_grads.reshape(groups, half_slots, model_width), 'expe...  38.9 us
    all_to_all x1, waiting for transfers between devices, local(): lax.all_to_all(token_sum.reshape(groups, half_slots, model_width), 'exper...  35.9 us
    all_to_all x1, starting transfers between devices, local(): lax.all_to_all(sent_gates.reshape(groups, half_slots), 'expert', split_ax...  7.3 us
    gather x2, local copies, waits for them, and re-layouts, local(): tokens[source]  6.72 us
    all_to_all x1, starting transfers between devices, local(): lax.all_to_all(token_sum.reshape(groups, half_slots, model_width), 'exper...  6.18 us
    gather x2, local copies, waits for them, and re-layouts, local(): upstream[source]  5.51 us
  transfers between devices with their start and end apart: 10, of which 2 were waited for; matrix products, arithmetic and copies ran while one was open for 33% of the time, Pallas kernels for 0%

commit v1 on v0

v1 whole, which is shorter than its diff:
```python
import functools

import jax
import jax.numpy as jnp
from jax import lax
from jax.experimental import pallas as pl
from jax.experimental.pallas import tpu as pltpu
from jax.sharding import PartitionSpec as P

LANES = 128
PLANE = 4
VMEM_LIMIT = 56 * 1024 * 1024
F32 = jnp.float32
BF16 = jnp.bfloat16


def dot(left, right, left_axis, right_axis):
    return lax.dot_general(
        left, right, (((left_axis,), (right_axis,)), ((), ())), preferred_element_type=F32
    )


def split_index(index):
    return index >> 3, index >> 2 & 1, index >> 1 & 1, index & 1


def join_index(level, u, v, core):
    return ((level * 2 + u) * 2 + v) * 2 + core


def route(count, target):
    return [(index, join_index(*target(*split_index(index)))) for index in range(count)]


def core_route(count):
    return route(count, lambda level, u, v, core: (level, u, v, 1 - core))


def first_route(count):
    return route(
        count,
        lambda level, u, v, core: (level, u, 1 - v, core) if core == 0 else (level, 1 - u, v, core),
    )


def second_route(count):
    return route(
        count,
        lambda level, u, v, core: (level, 1 - u, v, core) if core == 0 else (level, u, 1 - v, core),
    )


def level_route(count, shift):
    levels = count // (2 * PLANE)
    return route(count, lambda level, u, v, core: ((level + shift) % levels, u, v, core))


def send(block, pairs):
    return lax.ppermute(block, "expert", pairs)


def gate_column(gates, expert):
    lane = lax.broadcasted_iota(jnp.int32, gates.shape, 1)
    return jnp.sum(jnp.where(lane == expert, gates.astype(F32), 0.0), axis=1, keepdims=True)


def terms_body(count, width, half, expert_ref, *refs):
    blocks, refs = refs[:count], refs[count:]
    weights, refs = refs[:6], refs[6:]
    parts, refs = refs[:count], refs[count:]
    hidden_ref, own_ref, other_ref, gate_w, up_w, down_w, sems = refs
    copies = []
    for side in range(2):
        span = pl.ds(side * half, half)
        copies.append(
            [
                pltpu.make_async_copy(source, place, sems.at[side * 3 + i])
                for i, (source, place) in enumerate(
                    (
                        (weights[side * 3], gate_w.at[:, span]),
                        (weights[side * 3 + 1], up_w.at[:, span]),
                        (weights[side * 3 + 2], down_w.at[span, :]),
                    )
                )
            ]
        )
    for side in copies:
        for copy in side:
            copy.start()
    expert = expert_ref[0]
    rows = jnp.concatenate([block[:, :width] for block in blocks], axis=0)
    grads = jnp.concatenate([block[:, width : 2 * width] for block in blocks], axis=0)
    gates = jnp.concatenate([block[:, 2 * width :] for block in blocks], axis=0)
    gating = gate_column(gates, expert)
    full = 2 * half
    step = 256 if full % 256 == 0 else LANES
    sums = [0.0, 0.0]
    for low in range(0, full, step):
        if low == 0:
            for copy in copies[0]:
                copy.wait()
        if low < half + step and low + step > half and low <= half:
            for copy in copies[1]:
                copy.wait()
        span = slice(low, low + step)
        pre_gate = dot(rows, gate_w[:, span], 1, 0)
        pre_up = dot(rows, up_w[:, span], 1, 0)
        backward = dot(grads, down_w[span, :], 1, 1)
        logistic = jax.nn.sigmoid(pre_gate)
        activated = pre_gate * logistic
        hidden = (activated * pre_up).astype(BF16)
        terms = hidden.astype(F32) * backward
        for part in range(0, step, LANES):
            side = 0 if low + part < half else 1
            sums[side] = sums[side] + terms[:, part : part + LANES]
        grad_hidden = gating * backward
        grad_gate = (
            grad_hidden * pre_up * logistic * (1.0 + pre_gate * (1.0 - logistic))
        ).astype(BF16)
        grad_up = (grad_hidden * activated).astype(BF16)
        hidden_ref[:, span] = hidden
        for part in range(0, step, LANES):
            at = low + part
            target, at = (own_ref, at) if at < half else (other_ref, at - half)
            target[:, at : at + LANES] = grad_gate[:, part : part + LANES]
            target[:, half + at : half + at + LANES] = grad_up[:, part : part + LANES]
    gate_grad = [jnp.sum(total, axis=1, keepdims=True).astype(BF16).astype(F32) for total in sums]
    gate_grad = gate_grad[0] + gate_grad[1]
    lane = lax.broadcasted_iota(jnp.int32, gates.shape, 1)
    gate_lanes = jnp.where(lane == expert, gate_grad, 0.0).astype(BF16)
    grad_gate = jnp.concatenate([own_ref[:, :half], other_ref[:, :half]], axis=1)
    grad_up = jnp.concatenate([own_ref[:, half:], other_ref[:, half:]], axis=1)
    start = 0
    for part in parts:
        stop = start + part.shape[0]
        part[:, width:] = gate_lanes[start:stop]
        start = stop
    wide = 512 if width % 512 == 0 else width
    for low in range(0, width, wide):
        span = slice(low, low + wide)
        token = dot(grad_gate, gate_w[span, :], 1, 1) + dot(grad_up, up_w[span, :], 1, 1)
        token = token.astype(BF16)
        start = 0
        for part in parts:
            stop = start + part.shape[0]
            part[:, span] = token[start:stop]
            start = stop


def expert_terms(blocks, weights, expert):
    width, half = weights[0].shape
    total = sum(block.shape[0] for block in blocks)
    whole = pl.BlockSpec(memory_space=pltpu.VMEM)
    count = len(blocks)
    out_shape = [jax.ShapeDtypeStruct((block.shape[0], width + LANES), BF16) for block in blocks]
    out_shape += [jax.ShapeDtypeStruct((total, 2 * half), BF16)] * 3
    results = pl.pallas_call(
        functools.partial(terms_body, count, width, half),
        out_shape=out_shape,
        in_specs=[pl.BlockSpec(memory_space=pltpu.SMEM)]
        + [whole] * count
        + [pl.BlockSpec(memory_space=pl.ANY)] * 6,
        out_specs=[whole] * len(out_shape),
        scratch_shapes=[
            pltpu.VMEM((width, 2 * half), BF16),
            pltpu.VMEM((width, 2 * half), BF16),
            pltpu.VMEM((2 * half, width), BF16),
            pltpu.SemaphoreType.DMA((6,)),
        ],
        compiler_params=pltpu.CompilerParams(vmem_limit_bytes=VMEM_LIMIT),
        cost_estimate=pl.CostEstimate(
            flops=2 * 5 * total * width * 2 * half,
            bytes_accessed=12 * width * half + 12 * total * width,
            transcendentals=total * 2 * half,
        ),
        name="expert_terms",
    )(expert, *blocks, *weights)
    return results[:count], results[count], results[count + 1], results[count + 2]


def grads_body(count, groups, half, received, expert_ref, *refs):
    rows, refs = refs[:count], refs[count:]
    grads, refs = refs[:count], refs[count:]
    gates, refs = refs[:count], refs[count:]
    hidden, refs = refs[:groups], refs[groups:]
    pairs, refs = refs[:groups], refs[groups:]
    if received:
        lent, refs = refs[:3], refs[3:]
    gate_out, up_out, down_out = refs
    join = lambda parts: jnp.concatenate([part[...] for part in parts], axis=0)
    gating = gate_column(join(gates), expert_ref[0])
    scaled = (gating * join(grads).astype(F32)).astype(BF16)
    both = dot(join(rows), join(pairs), 0, 0)
    down = dot(join(hidden), scaled, 0, 0)
    gate, up = both[:, :half], both[:, half:]
    if received:
        gate = gate + lent[0][...].astype(F32)
        up = up + lent[1][...].astype(F32)
        down = down + lent[2][...].astype(F32)
    gate_out[...] = gate.astype(BF16)
    up_out[...] = up.astype(BF16)
    down_out[...] = down.astype(BF16)


def weight_grads(blocks, hidden, pairs, side, lent, expert, width, half):
    tile = 512 if width % 512 == 0 else width
    steps = width // tile
    count, groups = len(blocks), len(hidden)
    total = sum(block.shape[0] for block in blocks)
    in_specs = [pl.BlockSpec(memory_space=pltpu.SMEM)]
    in_specs += [pl.BlockSpec((b.shape[0], tile), lambda i: (0, i)) for b in blocks]
    in_specs += [pl.BlockSpec((b.shape[0], tile), lambda i: (0, steps + i)) for b in blocks]
    in_specs += [
        pl.BlockSpec((b.shape[0], LANES), lambda i: (0, 2 * width // LANES)) for b in blocks
    ]
    in_specs += [pl.BlockSpec((h.shape[0], half), lambda i: (0, side)) for h in hidden]
    in_specs += [pl.BlockSpec((p.shape[0], 2 * half), lambda i: (0, 0)) for p in pairs]
    weight_specs = [
        pl.BlockSpec((tile, half), lambda i: (i, 0)),
        pl.BlockSpec((tile, half), lambda i: (i, 0)),
        pl.BlockSpec((half, tile), lambda i: (0, i)),
    ]
    if lent:
        in_specs += weight_specs
    return pl.pallas_call(
        functools.partial(grads_body, count, groups, half, bool(lent)),
        grid=(steps,),
        out_shape=[
            jax.ShapeDtypeStruct((width, half), BF16),
            jax.ShapeDtypeStruct((width, half), BF16),
            jax.ShapeDtypeStruct((half, width), BF16),
        ],
        in_specs=in_specs,
        out_specs=weight_specs,
        compiler_params=pltpu.CompilerParams(vmem_limit_bytes=VMEM_LIMIT),
        cost_estimate=pl.CostEstimate(
            flops=2 * 3 * total * width * half,
            bytes_accessed=4 * total * width + 6 * width * half,
            transcendentals=0,
        ),
        name="weight_grads",
    )(expert, *blocks, *blocks, *blocks, *hidden, *pairs, *lent)


def add(left, right):
    return (left.astype(F32) + right.astype(F32)).astype(BF16)


def local(tokens, upstream, expert_ids, gate_weights, w_gate, w_up, w_down):
    tok_count, width = tokens.shape
    half = w_gate.shape[1]
    count = lax.axis_size("expert")
    levels = count // (2 * PLANE)
    expert = (lax.axis_index("expert") // 2).astype(jnp.int32)[None]
    chosen = expert_ids[:, :, None] == jnp.arange(LANES, dtype=jnp.int32)[None, None, :]
    gates = jnp.sum(jnp.where(chosen, gate_weights.astype(F32)[:, :, None], 0.0), axis=1)
    home = jnp.concatenate([tokens, upstream, gates.astype(BF16)], axis=1)

    own = (w_gate, w_up, w_down)
    other = tuple(send(weight, core_route(count)) for weight in own)

    groups = [(0,)]
    for shift in range(1, levels // 2 + 1):
        groups.append((shift, levels - shift) if shift != levels - shift else (shift,))
    first, second = first_route(count), second_route(count)

    blocks_of = []
    for group in groups:
        if group == (0,):
            mine = home
        else:
            mine = [send(home, level_route(count, shift)) for shift in group]
            mine = mine[0] if len(mine) == 1 else jnp.concatenate(mine, axis=0)
        near = send(mine, first)
        beside = send(mine, second)
        across = send(beside, first)
        blocks_of.append((mine, near, beside, across))

    all_hidden, own_pairs, other_pairs, arrived = [], [], [], []
    for group, blocks in zip(groups, blocks_of):
        parts, hidden, own_pair, other_pair = expert_terms(blocks, own + other, expert)
        all_hidden.append(hidden)
        own_pairs.append(own_pair)
        other_pairs.append(other_pair)
        beside = add(parts[2], send(parts[3], first))
        near_back = send(parts[1], first)
        beside_back = send(beside, second)
        plane = parts[0].astype(F32) + near_back.astype(F32) + beside_back.astype(F32)
        plane = plane.astype(BF16)
        if group == (0,):
            arrived.append(plane)
        else:
            for i, shift in enumerate(group):
                piece = plane[i * tok_count : (i + 1) * tok_count]
                arrived.append(send(piece, level_route(count, levels - shift)))

    blocks = [block for group in blocks_of for block in group]
    lent = weight_grads(blocks, all_hidden, other_pairs, 1, (), expert, width, half)
    lent = [send(part, core_route(count)) for part in lent]
    grads = weight_grads(blocks, all_hidden, own_pairs, 0, lent, expert, width, half)

    total = sum(piece.astype(F32) for piece in arrived)
    grad_tokens = total[:, :width].astype(BF16)
    gate_sums = total[:, width:]
    grad_gates = jnp.sum(jnp.where(chosen, gate_sums[:, None, :], 0.0), axis=2).astype(BF16)
    return (grad_tokens, grad_gates, *grads)


def solution(mesh):
    rows = P(("group", "expert"), None)
    return jax.shard_map(
        local,
        mesh=mesh,
        in_specs=(rows, rows, rows, rows, P("group", "expert"), P("group", "expert"), P("expert", "group")),
        out_specs=(rows, rows, P("group", "expert"), P("group", "expert"), P("expert", "group")),
        check_vma=False,
    )
```

time: 255 us -> 152 us (0.60)
  matrix products: 55.2 us -> 0 us
  blocking collectives: 54.7 us -> 0 us
  Pallas kernels: 0 us -> 43.7 us
  local copies, waits for them, and re-layouts: 37.9 us -> 7.67 us
  waiting for transfers between devices: 74.8 us -> 53.2 us
  starting transfers between devices: 22.6 us -> 43.8 us
  other arithmetic: 8.06 us -> 1.74 us
    all_to_all x4 -> x0, waiting for transfers between devices: 74.8 us -> none  [the longest x1 38.9 us: local(): lax.all_to_all(sent_grads.reshape(groups, half_slots, model_width), 'expe...]
    dot_general x16 -> x0, matrix products: 55.2 us -> none  [contract(): lax.dot_general(left_side, right_side, (((left_axis,), (right_axis,)), ((...]
    all_to_all x1 -> x0, blocking collectives: 54.7 us -> none  [local(): lax.all_to_all(sent_rows.reshape(groups, half_slots, model_width), 'exper...]
    ppermute x6 -> x30, waiting for transfers between devices: 0.02 us -> 53.2 us  [send(): return lax.ppermute(block, 'expert', pairs)]
    pallas_call x0 -> x5, Pallas kernels: none -> 43.7 us  [the longest x3 28.5 us: expert_terms(): pl.pallas_call(functools.partial(terms_body, count, width, half), out_sha...]
    ppermute x6 -> x30, starting transfers between devices: 1.16 us -> 43.8 us  [send(): return lax.ppermute(block, 'expert', pairs)]
    all_to_all x4 -> x0, starting transfers between devices: 21.4 us -> none  [the longest x1 7.3 us: local(): lax.all_to_all(sent_gates.reshape(groups, half_slots), 'expert', split_ax...]
    gather x7 -> x0, local copies, waits for them, and re-layouts: 19.2 us -> none  [the longest x2 6.72 us: local(): tokens[source]]
  transfers between devices with their start and end apart: 10 -> 30, of which waited for: 2 -> 12; matrix products, arithmetic and copies ran while one was open for 33% -> 1% of each run, Pallas kernels for 0% -> 24%
where the time goes in v1:
time: 152 us; the launch traced here: 151 us
  waiting for transfers between devices  53.2 us (35%)
  starting transfers between devices  43.8 us (29%)
  Pallas kernels  43.7 us (29%)
  local copies, waits for them, and re-layouts  7.67 us (5%)
  other arithmetic  1.74 us (1%)
    ppermute x30, waiting for transfers between devices, send(): return lax.ppermute(block, 'expert', pairs)  53.2 us
    ppermute x30, starting transfers between devices, send(): return lax.ppermute(block, 'expert', pairs)  43.8 us
    pallas_call x3, Pallas kernels, expert_terms(): pl.pallas_call(functools.partial(terms_body, count, width, half), out_sha...  28.5 us
    pallas_call x2, Pallas kernels, weight_grads(): pl.pallas_call(functools.partial(grads_body, count, groups, half, bool(le...  15.2 us
    unnamed x43, local copies, waits for them, and re-layouts  6.2 us
  transfers between devices with their start and end apart: 30, of which 12 were waited for; matrix products, arithmetic and copies ran while one was open for 1% of the time, Pallas kernels for 24%

profile of v1, /device:TPU:0, one launch (start us, length us, event | category | flops | bytes accessed | tf_op | source)
XLA Modules:
  0.0 151.1 jit_solution(7578848054947621566)
XLA Ops:
  3.3 4.1 %collective-permute-start.19 = (bf16[32,4224]{1,0:T(8,128)(2,1)S(1)}, bf16[32,4224]{1,0:T(8,128)(2,1)S(1)}, u32[]{:S(2)}, u32[]{:S(2)}) collective-permute-start(bf16[32,4224]{1,0:T(8,128)(2,1)S(1)} %pad_maximum_fusion.refs_0_.refs_12_.refs_24_), channel_id=1, source_target_pairs={{0,16},{1,17},{2,18},{3,19},{4,20},{5,21},{6,22},{7,23},{8,24},{9,... | collective-permute-start | bytes 811016 | tf_op jit(solution)/shard_map/ppermute | solution.py:59
  9.0 2.2 %collective-permute-start.10 = (bf16[32,4224]{1,0:T(8,128)(2,1)S(1)}, bf16[32,4224]{1,0:T(8,128)(2,1)S(1)}, u32[]{:S(2)}, u32[]{:S(2)}) collective-permute-start(bf16[32,4224]{1,0:T(8,128)(2,1)S(1)} %pad_maximum_fusion.refs_0_.refs_12_.refs_24_), channel_id=1, source_target_pairs={{0,24},{1,25},{2,26},{3,27},{4,28},{5,29},{6,30},{7,31},{8,0},{9,1... | collective-permute-start | bytes 811016 | tf_op jit(solution)/shard_map/ppermute | solution.py:59
  12.8 13.6 %collective-permute-done.19.refs_0_.refs_8_.refs_20_.refs_32_ = bf16[32,4224]{1,0:T(8,128)(2,1)S(1)} collective-permute-done((bf16[32,4224]{1,0:T(8,128)(2,1)S(1)}, bf16[32,4224]{1,0:T(8,128)(2,1)S(1)}, u32[]{:S(2)}, u32[]{:S(2)}) %collective-permute-start.19) | collective-permute-done | bytes 270368 | tf_op jit(solution)/shard_map/ppermute | solution.py:59
  27.1 1.8 %collective-permute-start.21 = (bf16[32,4224]{1,0:T(8,128)(2,1)S(1)}, bf16[32,4224]{1,0:T(8,128)(2,1)S(1)}, u32[]{:S(2)}, u32[]{:S(2)}) collective-permute-start(bf16[32,4224]{1,0:T(8,128)(2,1)S(1)} %collective-permute-done.19.refs_0_.refs_8_.refs_20_.refs_32_), channel_id=1, source_target_pairs={{0,4},{1,3},{2,6},{3,1},{4,0},{5,7},{6,2},{7,5},{8,12},{9,11},{10,... | collective-permute-start | bytes 811016 | tf_op jit(solution)/shard_map/ppermute | solution.py:59
  30.4 5.6 %collective-permute-done.21.refs_2_.refs_10_.refs_22_.refs_34_ = bf16[32,4224]{1,0:T(8,128)(2,1)S(1)} collective-permute-done((bf16[32,4224]{1,0:T(8,128)(2,1)S(1)}, bf16[32,4224]{1,0:T(8,128)(2,1)S(1)}, u32[]{:S(2)}, u32[]{:S(2)}) %collective-permute-start.21) | collective-permute-done | bytes 270368 | tf_op jit(solution)/shard_map/ppermute | solution.py:59
  35.9 1.9 %collective-permute-start.12 = (bf16[64,4224]{1,0:T(8,128)(2,1)S(1)}, bf16[64,4224]{1,0:T(8,128)(2,1)S(1)}, u32[]{:S(2)}, u32[]{:S(2)}) collective-permute-start(bf16[64,4224]{1,0:T(8,128)(2,1)S(1)} %constant_dynamic-update-slice_fusion.refs_0_.refs_4_.refs_16_.refs_28_), channel_id=1, source_target_pairs={{0,4},{1,3},{2,6},{3,1},{4,0},{5,7},{6,2},{7,5},{8,12},{9,11},{10,... | collective-permute-start | bytes 1622024 | tf_op jit(solution)/shard_map/ppermute | solution.py:59
  39.1 5.5 %collective-permute-done.22.refs_3_.refs_11_.refs_23_.refs_35_ = bf16[32,4224]{1,0:T(8,128)(2,1)} collective-permute-done((bf16[32,4224]{1,0:T(8,128)(2,1)S(1)}, bf16[32,4224]{1,0:T(8,128)(2,1)}, u32[]{:S(2)}, u32[]{:S(2)}) %collective-permute-start.22) | collective-permute-done | bytes 270368 | tf_op jit(solution)/shard_map/ppermute | solution.py:59
  44.5 1.7 %collective-permute-start.11 = (bf16[64,4224]{1,0:T(8,128)(2,1)S(1)}, bf16[64,4224]{1,0:T(8,128)(2,1)S(1)}, u32[]{:S(2)}, u32[]{:S(2)}) collective-permute-start(bf16[64,4224]{1,0:T(8,128)(2,1)S(1)} %constant_dynamic-update-slice_fusion.refs_0_.refs_4_.refs_16_.refs_28_), channel_id=1, source_target_pairs={{0,2},{1,5},{2,0},{3,7},{4,6},{5,1},{6,4},{7,3},{8,10},{9,13},{10,... | collective-permute-start | bytes 1622024 | tf_op jit(solution)/shard_map/ppermute | solution.py:59
  46.3 1.9 %collective-permute-done.12.refs_2_.refs_6_.refs_18_.refs_30_ = bf16[64,4224]{1,0:T(8,128)(2,1)S(1)} collective-permute-done((bf16[64,4224]{1,0:T(8,128)(2,1)S(1)}, bf16[64,4224]{1,0:T(8,128)(2,1)S(1)}, u32[]{:S(2)}, u32[]{:S(2)}) %collective-permute-start.12) | collective-permute-done | bytes 540704 | tf_op jit(solution)/shard_map/ppermute | solution.py:59
  52.8 9.3 %expert_terms.5 = (bf16[32,2176]{1,0:T(8,128)(2,1)}, bf16[32,2176]{1,0:T(8,128)(2,1)}, bf16[32,2176]{1,0:T(8,128)(2,1)}, bf16[32,2176]{1,0:T(8,128)(2,1)}, bf16[...) custom-call(s32[1]{0:T(128)} %bitcast.expert_ref, bf16[32,4224]{1,0:T(8,128)(2,1)} %copy-done.5, ...), custom_call_target="tpu_custom_call" | custom-call | flops 2013265920 | bytes 12582912 | tf_op jit(solution)/shard_map/expert_terms/pallas_call | solution.py:157
  65.6 9.3 %expert_terms.3 = (bf16[32,2176]{1,0:T(8,128)(2,1)}, bf16[32,2176]{1,0:T(8,128)(2,1)}, bf16[32,2176]{1,0:T(8,128)(2,1)}, bf16[32,2176]{1,0:T(8,128)(2,1)}, bf16[...) custom-call(s32[1]{0:T(128)} %bitcast.expert_ref, bf16[32,4224]{1,0:T(8,128)(2,1)} %copy-done.4, ...), custom_call_target="tpu_custom_call" | custom-call | flops 2013265920 | bytes 12582912 | tf_op jit(solution)/shard_map/expert_terms/pallas_call | solution.py:157
  74.9 1.8 %collective-permute-start.6 = (bf16[32,2176]{1,0:T(8,128)(2,1)}, bf16[32,2176]{1,0:T(8,128)(2,1)S(1)}, u32[]{:S(2)}, u32[]{:S(2)}) collective-permute-start(bf16[32,2176]{1,0:T(8,128)(2,1)} %get-tuple-element.33), channel_id=1, source_target_pairs={{0,2},{1,5},{2,0},{3,7},{4,6},{5,1},{6,4},{7,3},{8,10},{9,13},{10,... | collective-permute-start | bytes 417800 | tf_op jit(solution)/shard_map/ppermute | solution.py:59
  78.3 10.0 %expert_terms.4 = (bf16[64,2176]{1,0:T(8,128)(2,1)}, bf16[64,2176]{1,0:T(8,128)(2,1)}, bf16[64,2176]{1,0:T(8,128)(2,1)}, bf16[64,2176]{1,0:T(8,128)(2,1)}, bf16[...) custom-call(s32[1]{0:T(128)} %bitcast.expert_ref, bf16[64,4224]{1,0:T(8,128)(2,1)} %copy-done, ...), custom_call_target="tpu_custom_call" | custom-call | flops 4026531840 | bytes 15728640 | tf_op jit(solution)/shard_map/expert_terms/pallas_call | solution.py:157
  89.6 7.3 %weight_grads.2 = (bf16[2048,384]{1,0:T(8,128)(2,1)}, bf16[2048,384]{1,0:T(8,128)(2,1)}, bf16[384,2048]{1,0:T(8,128)(2,1)}) custom-call(s32[1]{0:T(128)} %bitcast.expert_ref, bf16[32,4224]{1,0:T(8,128)(2,1)} %copy-done.4, bf16[32,4224]{1,0:T(8,128)(2,1)} %collective-permute-done.refs_1_.refs_13_.refs_25_, bf16[32,4224]{1,0:T(8,128)(2,1)} %copy-done.6, ...), custom_call_target="tpu_custom_call" | custom-call | flops 2415919104 | bytes 8912896 | tf_op jit(solution)/shard_map/weight_grads/pallas_call | solution.py:225
  97.9 5.6 %collective-permute-done.15 = bf16[64,2176]{1,0:T(8,128)(2,1)S(1)} collective-permute-done((bf16[64,2176]{1,0:T(8,128)(2,1)S(1)}, bf16[64,2176]{1,0:T(8,128)(2,1)S(1)}, u32[]{:S(2)}, u32[]{:S(2)}) %collective-permute-start.15) | collective-permute-done | bytes 278560 | tf_op jit(solution)/shard_map/ppermute | solution.py:59
  103.5 3.8 %collective-permute-start.25 = (bf16[32,2176]{1,0:T(8,128)(2,1)S(1)}, bf16[32,2176]{1,0:T(8,128)(2,1)S(1)}, u32[]{:S(2)}, u32[]{:S(2)}) collective-permute-start(bf16[32,2176]{1,0:T(8,128)(2,1)S(1)} %add_convert_fusion.3), channel_id=1, source_target_pairs={{0,4},{1,3},{2,6},{3,1},{4,0},{5,7},{6,2},{7,5},{8,12},{9,11},{10,... | collective-permute-start | bytes 417800 | tf_op jit(solution)/shard_map/ppermute | solution.py:59
  107.5 2.9 %collective-permute-done.25 = bf16[32,2176]{1,0:T(8,128)(2,1)S(1)} collective-permute-done((bf16[32,2176]{1,0:T(8,128)(2,1)S(1)}, bf16[32,2176]{1,0:T(8,128)(2,1)S(1)}, u32[]{:S(2)}, u32[]{:S(2)}) %collective-permute-start.25) | collective-permute-done | bytes 139296 | tf_op jit(solution)/shard_map/ppermute | solution.py:59
  110.3 2.0 %collective-permute-start.16 = (bf16[64,2176]{1,0:T(8,128)(2,1)S(1)}, bf16[64,2176]{1,0:T(8,128)(2,1)S(1)}, u32[]{:S(2)}, u32[]{:S(2)}) collective-permute-start(bf16[64,2176]{1,0:T(8,128)(2,1)S(1)} %add_convert_fusion.1), channel_id=1, source_target_pairs={{0,4},{1,3},{2,6},{3,1},{4,0},{5,7},{6,2},{7,5},{8,12},{9,11},{10,... | collective-permute-start | bytes 835592 | tf_op jit(solution)/shard_map/ppermute | solution.py:59
  112.5 4.4 %collective-permute-done.16 = bf16[64,2176]{1,0:T(8,128)(2,1)S(1)} collective-permute-done((bf16[64,2176]{1,0:T(8,128)(2,1)S(1)}, bf16[64,2176]{1,0:T(8,128)(2,1)S(1)}, u32[]{:S(2)}, u32[]{:S(2)}) %collective-permute-start.16) | collective-permute-done | bytes 278560 | tf_op jit(solution)/shard_map/ppermute | solution.py:59
  116.9 2.0 %collective-permute-start.8 = (bf16[32,2176]{1,0:T(8,128)(2,1)S(1)}, bf16[32,2176]{1,0:T(8,128)(2,1)S(1)}, u32[]{:S(2)}, u32[]{:S(2)}) collective-permute-start(bf16[32,2176]{1,0:T(8,128)(2,1)S(1)} %add_convert_fusion.5), channel_id=1, source_target_pairs={{0,4},{1,3},{2,6},{3,1},{4,0},{5,7},{6,2},{7,5},{8,12},{9,11},{10,... | collective-permute-start | bytes 417800 | tf_op jit(solution)/shard_map/ppermute | solution.py:59
  119.0 7.7 %collective-permute-start.26 = (bf16[32,2176]{1,0:T(8,128)(2,1)S(1)}, bf16[32,2176]{1,0:T(8,128)(2,1)S(1)}, u32[]{:S(2)}, u32[]{:S(2)}) collective-permute-start(bf16[32,2176]{1,0:T(8,128)(2,1)S(1)} %add_convert_fusion.2), channel_id=1, source_target_pairs={{0,16},{1,17},{2,18},{3,19},{4,20},{5,21},{6,22},{7,23},{8,24},{9,... | collective-permute-start | bytes 417800 | tf_op jit(solution)/shard_map/ppermute | solution.py:59
  127.3 5.6 %collective-permute-done.26 = bf16[32,2176]{1,0:T(8,128)(2,1)S(1)} collective-permute-done((bf16[32,2176]{1,0:T(8,128)(2,1)S(1)}, bf16[32,2176]{1,0:T(8,128)(2,1)S(1)}, u32[]{:S(2)}, u32[]{:S(2)}) %collective-permute-start.26) | collective-permute-done | bytes 139296 | tf_op jit(solution)/shard_map/ppermute | solution.py:59
  134.0 5.7 %collective-permute-done.18 = bf16[32,2176]{1,0:T(8,128)(2,1)S(1)} collective-permute-done((bf16[32,2176]{1,0:T(8,128)(2,1)S(1)}, bf16[32,2176]{1,0:T(8,128)(2,1)S(1)}, u32[]{:S(2)}, u32[]{:S(2)}) %collective-permute-start.18) | collective-permute-done | bytes 139296 | tf_op jit(solution)/shard_map/ppermute | solution.py:59
  143.0 7.9 %weight_grads.3 = (bf16[2048,384]{1,0:T(8,128)(2,1)}, bf16[2048,384]{1,0:T(8,128)(2,1)}, bf16[384,2048]{1,0:T(8,128)(2,1)}) custom-call(s32[1]{0:T(128)} %bitcast.expert_ref, bf16[32,4224]{1,0:T(8,128)(2,1)} %copy-done.4, bf16[32,4224]{1,0:T(8,128)(2,1)} %collective-permute-done.refs_1_.refs_13_.refs_25_, bf16[32,4224]{1,0:T(8,128)(2,1)} %copy-done.6, ...), custom_call_target="tpu_custom_call" | custom-call | flops 2415919104 | bytes 8912896 | tf_op jit(solution)/shard_map/weight_grads/pallas_call | solution.py:225
  (98 shorter events, 26.5 us)
Async XLA Ops:
  3.3 23.0 %collective-permute-start.19 = (bf16[32,4224]{1,0:T(8,128)(2,1)S(1)}, bf16[32,4224]{1,0:T(8,128)(2,1)S(1)}, u32[]{:S(2)}, u32[]{:S(2)}) collective-permute-start(bf16[32,4224]{1,0:T(8,128)(2,1)S(1)} %pad_maximum_fusion.refs_0_.refs_12_.refs_24_), channel_id=1, source_target_pairs={{0,16},{1,17},{2,18},{3,19},{4,20},{5,21},{6,22},{7,23},{8,24},{9,... | collective-permute-start | bytes 811016 | tf_op jit(solution)/shard_map/ppermute | solution.py:59
  7.4 19.0 %collective-permute-start.9 = (bf16[32,4224]{1,0:T(8,128)(2,1)S(1)}, bf16[32,4224]{1,0:T(8,128)(2,1)S(1)}, u32[]{:S(2)}, u32[]{:S(2)}) collective-permute-start(bf16[32,4224]{1,0:T(8,128)(2,1)S(1)} %pad_maximum_fusion.refs_0_.refs_12_.refs_24_), channel_id=1, source_target_pairs={{0,8},{1,9},{2,10},{3,11},{4,12},{5,13},{6,14},{7,15},{8,16},{9,17... | collective-permute-start | bytes 811016 | tf_op jit(solution)/shard_map/ppermute | solution.py:59
  9.0 18.1 %collective-permute-start.10 = (bf16[32,4224]{1,0:T(8,128)(2,1)S(1)}, bf16[32,4224]{1,0:T(8,128)(2,1)S(1)}, u32[]{:S(2)}, u32[]{:S(2)}) collective-permute-start(bf16[32,4224]{1,0:T(8,128)(2,1)S(1)} %pad_maximum_fusion.refs_0_.refs_12_.refs_24_), channel_id=1, source_target_pairs={{0,24},{1,25},{2,26},{3,27},{4,28},{5,29},{6,30},{7,31},{8,0},{9,1... | collective-permute-start | bytes 811016 | tf_op jit(solution)/shard_map/ppermute | solution.py:59
  11.2 17.6 %collective-permute-start.1 = (bf16[32,4224]{1,0:T(8,128)(2,1)S(1)}, bf16[32,4224]{1,0:T(8,128)(2,1)S(1)}, u32[]{:S(2)}, u32[]{:S(2)}) collective-permute-start(bf16[32,4224]{1,0:T(8,128)(2,1)S(1)} %pad_maximum_fusion.refs_0_.refs_12_.refs_24_), channel_id=1, source_target_pairs={{0,4},{1,3},{2,6},{3,1},{4,0},{5,7},{6,2},{7,5},{8,12},{9,11},{10,... | collective-permute-start | bytes 811016 | tf_op jit(solution)/shard_map/ppermute | solution.py:59
  12.8 36.9 %collective-permute-start.3 = (bf16[2048,384]{1,0:T(8,128)(2,1)}, bf16[2048,384]{1,0:T(8,128)(2,1)S(1)}, u32[]{:S(2)}, u32[]{:S(2)}) collective-permute-start(bf16[2048,384]{1,0:T(8,128)(2,1)} %refs_4_.5), channel_id=1, source_target_pairs={{0,1},{1,0},{2,3},{3,2},{4,5},{5,4},{6,7},{7,6},{8,9},{9,8},{10,11... | collective-permute-start | bytes 4718600 | tf_op jit(solution)/shard_map/ppermute | solution.py:59
  26.4 24.4 %collective-permute-start.4 = (bf16[2048,384]{1,0:T(8,128)(2,1)}, bf16[2048,384]{1,0:T(8,128)(2,1)S(1)}, u32[]{:S(2)}, u32[]{:S(2)}) collective-permute-start(bf16[2048,384]{1,0:T(8,128)(2,1)} %refs_5_.5), channel_id=1, source_target_pairs={{0,1},{1,0},{2,3},{3,2},{4,5},{5,4},{6,7},{7,6},{8,9},{9,8},{10,11... | collective-permute-start | bytes 4718600 | tf_op jit(solution)/shard_map/ppermute | solution.py:59
  26.4 26.5 %collective-permute-start.5 = (bf16[384,2048]{1,0:T(8,128)(2,1)}, bf16[384,2048]{1,0:T(8,128)(2,1)}, u32[]{:S(2)}, u32[]{:S(2)}) collective-permute-start(bf16[384,2048]{1,0:T(8,128)(2,1)} %refs_6_.5), channel_id=1, source_target_pairs={{0,1},{1,0},{2,3},{3,2},{4,5},{5,4},{6,7},{7,6},{8,9},{9,8},{10,11... | collective-permute-start | bytes 4718600 | tf_op jit(solution)/shard_map/ppermute | solution.py:59
  27.1 8.9 %collective-permute-start.21 = (bf16[32,4224]{1,0:T(8,128)(2,1)S(1)}, bf16[32,4224]{1,0:T(8,128)(2,1)S(1)}, u32[]{:S(2)}, u32[]{:S(2)}) collective-permute-start(bf16[32,4224]{1,0:T(8,128)(2,1)S(1)} %collective-permute-done.19.refs_0_.refs_8_.refs_20_.refs_32_), channel_id=1, source_target_pairs={{0,4},{1,3},{2,6},{3,1},{4,0},{5,7},{6,2},{7,5},{8,12},{9,11},{10,... | collective-permute-start | bytes 811016 | tf_op jit(solution)/shard_map/ppermute | solution.py:59
  28.8 9.0 %collective-permute-start.20 = (bf16[32,4224]{1,0:T(8,128)(2,1)S(1)}, bf16[32,4224]{1,0:T(8,128)(2,1)S(1)}, u32[]{:S(2)}, u32[]{:S(2)}) collective-permute-start(bf16[32,4224]{1,0:T(8,128)(2,1)S(1)} %collective-permute-done.19.refs_0_.refs_8_.refs_20_.refs_32_), channel_id=1, source_target_pairs={{0,2},{1,5},{2,0},{3,7},{4,6},{5,1},{6,4},{7,3},{8,10},{9,13},{10,... | collective-permute-start | bytes 811016 | tf_op jit(solution)/shard_map/ppermute | solution.py:59
  35.9 12.2 %collective-permute-start.12 = (bf16[64,4224]{1,0:T(8,128)(2,1)S(1)}, bf16[64,4224]{1,0:T(8,128)(2,1)S(1)}, u32[]{:S(2)}, u32[]{:S(2)}) collective-permute-start(bf16[64,4224]{1,0:T(8,128)(2,1)S(1)} %constant_dynamic-update-slice_fusion.refs_0_.refs_4_.refs_16_.refs_28_), channel_id=1, source_target_pairs={{0,4},{1,3},{2,6},{3,1},{4,0},{5,7},{6,2},{7,5},{8,12},{9,11},{10,... | collective-permute-start | bytes 1622024 | tf_op jit(solution)/shard_map/ppermute | solution.py:59
  44.5 32.1 %collective-permute-start.11 = (bf16[64,4224]{1,0:T(8,128)(2,1)S(1)}, bf16[64,4224]{1,0:T(8,128)(2,1)S(1)}, u32[]{:S(2)}, u32[]{:S(2)}) collective-permute-start(bf16[64,4224]{1,0:T(8,128)(2,1)S(1)} %constant_dynamic-update-slice_fusion.refs_0_.refs_4_.refs_16_.refs_28_), channel_id=1, source_target_pairs={{0,2},{1,5},{2,0},{3,7},{4,6},{5,1},{6,4},{7,3},{8,10},{9,13},{10,... | collective-permute-start | bytes 1622024 | tf_op jit(solution)/shard_map/ppermute | solution.py:59
  48.2 28.8 %collective-permute-start.13 = (bf16[64,4224]{1,0:T(8,128)(2,1)S(1)}, bf16[64,4224]{1,0:T(8,128)(2,1)S(1)}, u32[]{:S(2)}, u32[]{:S(2)}) collective-permute-start(bf16[64,4224]{1,0:T(8,128)(2,1)S(1)} %collective-permute-done.12.refs_2_.refs_6_.refs_18_.refs_30_), channel_id=1, source_target_pairs={{0,2},{1,5},{2,0},{3,7},{4,6},{5,1},{6,4},{7,3},{8,10},{9,13},{10,... | collective-permute-start | bytes 1622024 | tf_op jit(solution)/shard_map/ppermute | solution.py:59
  49.6 13.7 %collective-permute-start = (bf16[32,4224]{1,0:T(8,128)(2,1)S(1)}, bf16[32,4224]{1,0:T(8,128)(2,1)}, u32[]{:S(2)}, u32[]{:S(2)}) collective-permute-start(bf16[32,4224]{1,0:T(8,128)(2,1)S(1)} %pad_maximum_fusion.refs_0_.refs_12_.refs_24_), channel_id=1, source_target_pairs={{0,2},{1,5},{2,0},{3,7},{4,6},{5,1},{6,4},{7,3},{8,10},{9,13},{10,... | collective-permute-start | bytes 811016 | tf_op jit(solution)/shard_map/ppermute | solution.py:59
  51.9 13.7 %collective-permute-start.2 = (bf16[32,4224]{1,0:T(8,128)(2,1)S(1)}, bf16[32,4224]{1,0:T(8,128)(2,1)}, u32[]{:S(2)}, u32[]{:S(2)}) collective-permute-start(bf16[32,4224]{1,0:T(8,128)(2,1)S(1)} %collective-permute-done.1.refs_2_.refs_14_.refs_26_), channel_id=1, source_target_pairs={{0,2},{1,5},{2,0},{3,7},{4,6},{5,1},{6,4},{7,3},{8,10},{9,13},{10,... | collective-permute-start | bytes 811016 | tf_op jit(solution)/shard_map/ppermute | solution.py:59
  62.1 45.2 %collective-permute-start.23 = (bf16[32,2176]{1,0:T(8,128)(2,1)}, bf16[32,2176]{1,0:T(8,128)(2,1)S(1)}, u32[]{:S(2)}, u32[]{:S(2)}) collective-permute-start(bf16[32,2176]{1,0:T(8,128)(2,1)} %get-tuple-element.41), channel_id=1, source_target_pairs={{0,2},{1,5},{2,0},{3,7},{4,6},{5,1},{6,4},{7,3},{8,10},{9,13},{10,... | collective-permute-start | bytes 417800 | tf_op jit(solution)/shard_map/ppermute | solution.py:59
  63.3 33.5 %collective-permute-start.24 = (bf16[32,2176]{1,0:T(8,128)(2,1)}, bf16[32,2176]{1,0:T(8,128)(2,1)S(1)}, u32[]{:S(2)}, u32[]{:S(2)}) collective-permute-start(bf16[32,2176]{1,0:T(8,128)(2,1)} %get-tuple-element.43), channel_id=1, source_target_pairs={{0,2},{1,5},{2,0},{3,7},{4,6},{5,1},{6,4},{7,3},{8,10},{9,13},{10,... | collective-permute-start | bytes 417800 | tf_op jit(solution)/shard_map/ppermute | solution.py:59
  74.9 44.2 %collective-permute-start.6 = (bf16[32,2176]{1,0:T(8,128)(2,1)}, bf16[32,2176]{1,0:T(8,128)(2,1)S(1)}, u32[]{:S(2)}, u32[]{:S(2)}) collective-permute-start(bf16[32,2176]{1,0:T(8,128)(2,1)} %get-tuple-element.33), channel_id=1, source_target_pairs={{0,2},{1,5},{2,0},{3,7},{4,6},{5,1},{6,4},{7,3},{8,10},{9,13},{10,... | collective-permute-start | bytes 417800 | tf_op jit(solution)/shard_map/ppermute | solution.py:59
  76.7 21.1 %collective-permute-start.7 = (bf16[32,2176]{1,0:T(8,128)(2,1)}, bf16[32,2176]{1,0:T(8,128)(2,1)S(1)}, u32[]{:S(2)}, u32[]{:S(2)}) collective-permute-start(bf16[32,2176]{1,0:T(8,128)(2,1)} %get-tuple-element.35), channel_id=1, source_target_pairs={{0,2},{1,5},{2,0},{3,7},{4,6},{5,1},{6,4},{7,3},{8,10},{9,13},{10,... | collective-permute-start | bytes 417800 | tf_op jit(solution)/shard_map/ppermute | solution.py:59
  88.3 24.1 %collective-permute-start.14 = (bf16[64,2176]{1,0:T(8,128)(2,1)}, bf16[64,2176]{1,0:T(8,128)(2,1)S(1)}, u32[]{:S(2)}, u32[]{:S(2)}) collective-permute-start(bf16[64,2176]{1,0:T(8,128)(2,1)} %get-tuple-element.37), channel_id=1, source_target_pairs={{0,2},{1,5},{2,0},{3,7},{4,6},{5,1},{6,4},{7,3},{8,10},{9,13},{10,... | collective-permute-start | bytes 835592 | tf_op jit(solution)/shard_map/ppermute | solution.py:59
  97.8 43.6 %collective-permute-start.27 = (bf16[2048,384]{1,0:T(8,128)(2,1)}, bf16[2048,384]{1,0:T(8,128)(2,1)S(1)}, u32[]{:S(2)}, u32[]{:S(2)}) collective-permute-start(bf16[2048,384]{1,0:T(8,128)(2,1)} %get-tuple-element.53), channel_id=1, source_target_pairs={{0,1},{1,0},{2,3},{3,2},{4,5},{5,4},{6,7},{7,6},{8,9},{9,8},{10,11... | collective-permute-start | bytes 4718600 | tf_op jit(solution)/shard_map/ppermute | solution.py:59
  107.4 34.0 %collective-permute-start.28 = (bf16[2048,384]{1,0:T(8,128)(2,1)}, bf16[2048,384]{1,0:T(8,128)(2,1)S(1)}, u32[]{:S(2)}, u32[]{:S(2)}) collective-permute-start(bf16[2048,384]{1,0:T(8,128)(2,1)} %get-tuple-element.54), channel_id=1, source_target_pairs={{0,1},{1,0},{2,3},{3,2},{4,5},{5,4},{6,7},{7,6},{8,9},{9,8},{10,11... | collective-permute-start | bytes 4718600 | tf_op jit(solution)/shard_map/ppermute | solution.py:59
  112.4 29.0 %collective-permute-start.29 = (bf16[384,2048]{1,0:T(8,128)(2,1)}, bf16[384,2048]{1,0:T(8,128)(2,1)}, u32[]{:S(2)}, u32[]{:S(2)}) collective-permute-start(bf16[384,2048]{1,0:T(8,128)(2,1)} %get-tuple-element.55), channel_id=1, source_target_pairs={{0,1},{1,0},{2,3},{3,2},{4,5},{5,4},{6,7},{7,6},{8,9},{9,8},{10,11... | collective-permute-start | bytes 4718600 | tf_op jit(solution)/shard_map/ppermute | solution.py:59
  116.9 9.9 %collective-permute-start.8 = (bf16[32,2176]{1,0:T(8,128)(2,1)S(1)}, bf16[32,2176]{1,0:T(8,128)(2,1)S(1)}, u32[]{:S(2)}, u32[]{:S(2)}) collective-permute-start(bf16[32,2176]{1,0:T(8,128)(2,1)S(1)} %add_convert_fusion.5), channel_id=1, source_target_pairs={{0,4},{1,3},{2,6},{3,1},{4,0},{5,7},{6,2},{7,5},{8,12},{9,11},{10,... | collective-permute-start | bytes 417800 | tf_op jit(solution)/shard_map/ppermute | solution.py:59
  119.0 13.8 %collective-permute-start.26 = (bf16[32,2176]{1,0:T(8,128)(2,1)S(1)}, bf16[32,2176]{1,0:T(8,128)(2,1)S(1)}, u32[]{:S(2)}, u32[]{:S(2)}) collective-permute-start(bf16[32,2176]{1,0:T(8,128)(2,1)S(1)} %add_convert_fusion.2), channel_id=1, source_target_pairs={{0,16},{1,17},{2,18},{3,19},{4,20},{5,21},{6,22},{7,23},{8,24},{9,... | collective-permute-start | bytes 417800 | tf_op jit(solution)/shard_map/ppermute | solution.py:59
  (26 other events, 364.3 us)

commit v2 on v1

v2 whole, which is shorter than its diff:
```python
import functools

import jax
import jax.numpy as jnp
from jax import lax
from jax.experimental import pallas as pl
from jax.experimental.pallas import tpu as pltpu
from jax.sharding import PartitionSpec as P

LANES = 128
PLANE = 4
TERMS_VMEM = 32 * 1024 * 1024
GRADS_VMEM = 40 * 1024 * 1024
F32 = jnp.float32
BF16 = jnp.bfloat16


def dot(left, right, left_axis, right_axis):
    return lax.dot_general(
        left, right, (((left_axis,), (right_axis,)), ((), ())), preferred_element_type=F32
    )


def split_index(index):
    return index >> 3, index >> 2 & 1, index >> 1 & 1, index & 1


def join_index(level, u, v, core):
    return ((level * 2 + u) * 2 + v) * 2 + core


def route(count, target):
    return [(index, join_index(*target(*split_index(index)))) for index in range(count)]


def core_route(count):
    return route(count, lambda level, u, v, core: (level, u, v, 1 - core))


def first_route(count):
    return route(
        count,
        lambda level, u, v, core: (level, u, 1 - v, core) if core == 0 else (level, 1 - u, v, core),
    )


def second_route(count):
    return route(
        count,
        lambda level, u, v, core: (level, 1 - u, v, core) if core == 0 else (level, u, 1 - v, core),
    )


def level_route(count, shift):
    levels = count // (2 * PLANE)
    return route(count, lambda level, u, v, core: ((level + shift) % levels, u, v, core))


def send(block, pairs):
    return lax.ppermute(block, "expert", pairs)


def gate_column(gates, expert):
    lane = lax.broadcasted_iota(jnp.int32, gates.shape, 1)
    return jnp.sum(jnp.where(lane == expert, gates.astype(F32), 0.0), axis=1, keepdims=True)


def terms_body(count, width, half, expert_ref, *refs):
    blocks, refs = refs[:count], refs[count:]
    gate_in, up_in, down_w, *refs = refs
    parts, refs = refs[:count], refs[count:]
    hidden_ref, pair_ref, both_w, pre_ref, sems = refs
    copies = [
        pltpu.make_async_copy(source, both_w.at[:, pl.ds(i * half, half)], sems.at[i])
        for i, source in enumerate((gate_in, up_in))
    ]
    for copy in copies:
        copy.start()
    expert = expert_ref[0]
    rows = jnp.concatenate([block[:, :width] for block in blocks], axis=0)
    grads = jnp.concatenate([block[:, width : 2 * width] for block in blocks], axis=0)
    gates = jnp.concatenate([block[:, 2 * width :] for block in blocks], axis=0)
    gating = gate_column(gates, expert)
    backward = dot(grads, down_w[...], 1, 1)
    for copy in copies:
        copy.wait()
    pre_ref[...] = dot(rows, both_w[...], 1, 0)
    total = 0.0
    for low in range(0, half, LANES):
        span = slice(low, low + LANES)
        pre_gate = pre_ref[:, span]
        pre_up = pre_ref[:, half + low : half + low + LANES]
        back = backward[:, span]
        logistic = jax.nn.sigmoid(pre_gate)
        activated = pre_gate * logistic
        hidden = (activated * pre_up).astype(BF16)
        total = total + hidden.astype(F32) * back
        grad_hidden = gating * back
        grad_gate = grad_hidden * pre_up * logistic * (1.0 + pre_gate * (1.0 - logistic))
        grad_up = grad_hidden * activated
        hidden_ref[:, span] = (gating * (activated * pre_up)).astype(BF16)
        pair_ref[:, span] = grad_gate.astype(BF16)
        pair_ref[:, half + low : half + low + LANES] = grad_up.astype(BF16)
    gate_grad = jnp.sum(total, axis=1, keepdims=True)
    lane = lax.broadcasted_iota(jnp.int32, gates.shape, 1)
    gate_lanes = jnp.where(lane == expert, gate_grad, 0.0).astype(BF16)
    scatter(gate_lanes, parts, slice(width, None))
    tile = 512 if width % 512 == 0 else width
    for low in range(0, width, tile):
        span = slice(low, low + tile)
        scatter(dot(pair_ref[...], both_w[span, :], 1, 1).astype(BF16), parts, span)


def scatter(value, parts, span):
    start = 0
    for part in parts:
        stop = start + part.shape[0]
        part[:, span] = value[start:stop]
        start = stop


def expert_terms(blocks, weights, expert):
    width, half = weights[0].shape
    total = sum(block.shape[0] for block in blocks)
    whole = pl.BlockSpec(memory_space=pltpu.VMEM)
    apart = pl.BlockSpec(memory_space=pl.ANY)
    count = len(blocks)
    out_shape = [jax.ShapeDtypeStruct((block.shape[0], width + LANES), BF16) for block in blocks]
    out_shape.append(jax.ShapeDtypeStruct((total, half), BF16))
    out_shape.append(jax.ShapeDtypeStruct((total, 2 * half), BF16))
    results = pl.pallas_call(
        functools.partial(terms_body, count, width, half),
        out_shape=out_shape,
        in_specs=[pl.BlockSpec(memory_space=pltpu.SMEM)] + [whole] * count + [apart, apart, whole],
        out_specs=[whole] * len(out_shape),
        scratch_shapes=[
            pltpu.VMEM((width, 2 * half), BF16),
            pltpu.VMEM((total, 2 * half), F32),
            pltpu.SemaphoreType.DMA((2,)),
        ],
        compiler_params=pltpu.CompilerParams(vmem_limit_bytes=TERMS_VMEM),
        cost_estimate=pl.CostEstimate(
            flops=2 * 5 * total * width * half,
            bytes_accessed=6 * width * half + 6 * total * width,
            transcendentals=total * half,
        ),
        name="expert_terms",
    )(expert, *blocks, *weights)
    return results[:count], results[count], results[count + 1]


def grads_body(count, groups, width, half, *refs):
    blocks, refs = refs[:count], refs[count:]
    hidden, refs = refs[:groups], refs[groups:]
    pairs, refs = refs[:groups], refs[groups:]
    gate_out, up_out, down_out, held, sems = refs
    tile = gate_out.shape[0]
    step, steps = pl.program_id(0), pl.num_programs(0)

    def copies(at, slot):
        start = 0
        for i, block in enumerate(blocks):
            size = block.shape[0]
            for side in range(2):
                source = pl.ds(pl.multiple_of(side * width + at * tile, LANES), tile)
                yield pltpu.make_async_copy(
                    block.at[:, source],
                    held.at[slot, side, pl.ds(start, size), :],
                    sems.at[slot, side, i],
                )
            start += size

    @pl.when(step == 0)
    def _():
        for copy in copies(0, 0):
            copy.start()

    @pl.when(step + 1 < steps)
    def _():
        for copy in copies(step + 1, (step + 1) % 2):
            copy.start()

    slot = step % 2
    for copy in copies(step, slot):
        copy.wait()
    join = lambda parts: jnp.concatenate([part[...] for part in parts], axis=0)
    rows, grads = held[slot, 0], held[slot, 1]
    both = dot(rows, join(pairs), 0, 0).astype(BF16)
    gate_out[...] = both[:, :half]
    up_out[...] = both[:, half:]
    down_out[...] = dot(join(hidden), grads, 0, 0).astype(BF16)


def weight_grads(blocks, hidden, pairs, width, half):
    count, groups = len(blocks), len(hidden)
    total = sum(block.shape[0] for block in blocks)
    tile = width // 2 if total <= 1024 else width // 8
    return pl.pallas_call(
        functools.partial(grads_body, count, groups, width, half),
        grid=(width // tile,),
        out_shape=[
            jax.ShapeDtypeStruct((width, half), BF16),
            jax.ShapeDtypeStruct((width, half), BF16),
            jax.ShapeDtypeStruct((half, width), BF16),
        ],
        in_specs=[pl.BlockSpec(memory_space=pl.ANY)] * count
        + [pl.BlockSpec(part.shape, lambda i: (0, 0)) for part in hidden + pairs],
        out_specs=[
            pl.BlockSpec((tile, half), lambda i: (i, 0)),
            pl.BlockSpec((tile, half), lambda i: (i, 0)),
            pl.BlockSpec((half, tile), lambda i: (0, i)),
        ],
        scratch_shapes=[
            pltpu.VMEM((2, 2, total, tile), BF16),
            pltpu.SemaphoreType.DMA((2, 2, count)),
        ],
        compiler_params=pltpu.CompilerParams(vmem_limit_bytes=GRADS_VMEM),
        cost_estimate=pl.CostEstimate(
            flops=2 * 3 * total * width * half,
            bytes_accessed=4 * total * width + 6 * width * half,
            transcendentals=0,
        ),
        name="weight_grads",
    )(*blocks, *hidden, *pairs)


def add(left, right):
    return (left.astype(F32) + right.astype(F32)).astype(BF16)


def local(tokens, upstream, expert_ids, gate_weights, w_gate, w_up, w_down):
    tok_count, width = tokens.shape
    half = w_gate.shape[1]
    count = lax.axis_size("expert")
    levels = count // (2 * PLANE)
    expert = (lax.axis_index("expert") // 2).astype(jnp.int32)[None]
    chosen = expert_ids[:, :, None] == jnp.arange(LANES, dtype=jnp.int32)[None, None, :]
    gates = jnp.sum(jnp.where(chosen, gate_weights.astype(F32)[:, :, None], 0.0), axis=1)
    home = jnp.concatenate([tokens, upstream, gates.astype(BF16)], axis=1)

    weights = (w_gate, w_up, w_down)
    groups = [(0,)]
    for shift in range(1, levels // 2 + 1):
        groups.append((shift, levels - shift) if shift != levels - shift else (shift,))
    first, second, swap = first_route(count), second_route(count), core_route(count)

    blocks_of = []
    for group in groups:
        if group == (0,):
            mine = home
        else:
            mine = [send(home, level_route(count, shift)) for shift in group]
            mine = mine[0] if len(mine) == 1 else jnp.concatenate(mine, axis=0)
        near = send(mine, first)
        beside = send(mine, second)
        across = send(beside, first)
        kept = [mine, near, beside, across]
        blocks_of.append(kept + [send(block, swap) for block in kept])

    all_hidden, all_pairs, arrived = [], [], []
    for group, blocks in zip(groups, blocks_of):
        parts, hidden, pair = expert_terms(blocks, weights, expert)
        all_hidden.append(hidden)
        all_pairs.append(pair)
        mine, near, beside, across = [
            add(part, send(lent, swap)) for part, lent in zip(parts[:4], parts[4:])
        ]
        beside = add(beside, send(across, first))
        near_back = send(near, first)
        beside_back = send(beside, second)
        plane = mine.astype(F32) + near_back.astype(F32) + beside_back.astype(F32)
        plane = plane.astype(BF16)
        if group == (0,):
            arrived.append(plane)
        else:
            for i, shift in enumerate(group):
                piece = plane[i * tok_count : (i + 1) * tok_count]
                arrived.append(send(piece, level_route(count, levels - shift)))

    blocks = [block for group in blocks_of for block in group]
    grads = weight_grads(blocks, all_hidden, all_pairs, width, w_gate.shape[1])

    total = sum(piece.astype(F32) for piece in arrived)
    grad_tokens = total[:, :width].astype(BF16)
    gate_sums = total[:, width:]
    grad_gates = jnp.sum(jnp.where(chosen, gate_sums[:, None, :], 0.0), axis=2).astype(BF16)
    return (grad_tokens, grad_gates, *grads)


def solution(mesh):
    rows = P(("group", "expert"), None)
    return jax.shard_map(
        local,
        mesh=mesh,
        in_specs=(rows, rows, rows, rows, P("group", "expert"), P("group", "expert"), P("expert", "group")),
        out_specs=(rows, rows, P("group", "expert"), P("group", "expert"), P("expert", "group")),
        check_vma=False,
    )
```

time: 152 us -> 122 us (0.80)
  Pallas kernels: 43.7 us -> 23.5 us
  waiting for transfers between devices: 53.2 us -> 44.3 us
    pallas_call x3, Pallas kernels: 28.5 us -> 13.8 us  [expert_terms(): pl.pallas_call(functools.partial(terms_body, count, width, half), out_sha...]
    ppermute x30 -> x48, waiting for transfers between devices: 53.2 us -> 44.3 us  [send(): return lax.ppermute(block, 'expert', pairs)]
    pallas_call x2 -> x1, Pallas kernels: 15.2 us -> 9.62 us  [weight_grads(): pl.pallas_call(functools.partial(grads_body, count, groups, width, half),...]
    unnamed x43 -> x13, local copies, waits for them, and re-layouts: 6.2 us -> 5.67 us
    ppermute x30 -> x48, starting transfers between devices: 43.8 us -> 43.9 us  [send(): return lax.ppermute(block, 'expert', pairs)]
  transfers between devices with their start and end apart: 30 -> 48, of which waited for: 12 -> 17; matrix products, arithmetic and copies ran while one was open for 1% -> 1% of each run, Pallas kernels for 24% -> 19%
where the time goes in v2:
time: 122 us
  waiting for transfers between devices  44.3 us (36%)
  starting transfers between devices  43.9 us (36%)
  Pallas kernels  23.5 us (19%)
  local copies, waits for them, and re-layouts  7.15 us (6%)
  other arithmetic  2.16 us (2%)
    ppermute x48, waiting for transfers between devices, send(): return lax.ppermute(block, 'expert', pairs)  44.3 us
    ppermute x48, starting transfers between devices, send(): return lax.ppermute(block, 'expert', pairs)  43.9 us
    pallas_call x3, Pallas kernels, expert_terms(): pl.pallas_call(functools.partial(terms_body, count, width, half), out_sha...  13.8 us
    pallas_call x1, Pallas kernels, weight_grads(): pl.pallas_call(functools.partial(grads_body, count, groups, width, half),...  9.62 us
    unnamed x13, local copies, waits for them, and re-layouts  5.67 us
  transfers between devices with their start and end apart: 48, of which 17 were waited for; matrix products, arithmetic and copies ran while one was open for 1% of the time, Pallas kernels for 19%

profile of v2, /device:TPU:0, one launch (start us, length us, event | category | flops | bytes accessed | tf_op | source)
XLA Modules:
  0.0 121.9 jit_solution(11211980673830871548)
XLA Ops:
  3.3 3.0 %collective-permute-start.1 = (bf16[32,4224]{1,0:T(8,128)(2,1)S(1)}, bf16[32,4224]{1,0:T(8,128)(2,1)S(1)}, u32[]{:S(2)}, u32[]{:S(2)}) collective-permute-start(bf16[32,4224]{1,0:T(8,128)(2,1)S(1)} %pad_maximum_fusion.refs_0_), channel_id=1, source_target_pairs={{0,4},{1,3},{2,6},{3,1},{4,0},{5,7},{6,2},{7,5},{8,12},{9,11},{10,... | collective-permute-start | bytes 811016 | tf_op jit(solution)/shard_map/ppermute | solution.py:60
  6.3 2.6 %collective-permute-start.32 = (bf16[32,4224]{1,0:T(8,128)(2,1)S(1)}, bf16[32,4224]{1,0:T(8,128)(2,1)S(1)}, u32[]{:S(2)}, u32[]{:S(2)}) collective-permute-start(bf16[32,4224]{1,0:T(8,128)(2,1)S(1)} %pad_maximum_fusion.refs_0_), channel_id=1, source_target_pairs={{0,16},{1,17},{2,18},{3,19},{4,20},{5,21},{6,22},{7,23},{8,24},{9,... | collective-permute-start | bytes 811016 | tf_op jit(solution)/shard_map/ppermute | solution.py:60
  8.9 1.6 %collective-permute-start.14 = (bf16[32,4224]{1,0:T(8,128)(2,1)S(1)}, bf16[32,4224]{1,0:T(8,128)(2,1)S(1)}, u32[]{:S(2)}, u32[]{:S(2)}) collective-permute-start(bf16[32,4224]{1,0:T(8,128)(2,1)S(1)} %pad_maximum_fusion.refs_0_), channel_id=1, source_target_pairs={{0,8},{1,9},{2,10},{3,11},{4,12},{5,13},{6,14},{7,15},{8,16},{9,17... | collective-permute-start | bytes 811016 | tf_op jit(solution)/shard_map/ppermute | solution.py:60
  10.5 1.5 %collective-permute-start = (bf16[32,4224]{1,0:T(8,128)(2,1)S(1)}, bf16[32,4224]{1,0:T(8,128)(2,1)S(1)}, u32[]{:S(2)}, u32[]{:S(2)}) collective-permute-start(bf16[32,4224]{1,0:T(8,128)(2,1)S(1)} %pad_maximum_fusion.refs_0_), channel_id=1, source_target_pairs={{0,2},{1,5},{2,0},{3,7},{4,6},{5,1},{6,4},{7,3},{8,10},{9,13},{10,... | collective-permute-start | bytes 811016 | tf_op jit(solution)/shard_map/ppermute | solution.py:60
  12.9 5.0 %collective-permute-start.15 = (bf16[32,4224]{1,0:T(8,128)(2,1)S(1)}, bf16[32,4224]{1,0:T(8,128)(2,1)S(1)}, u32[]{:S(2)}, u32[]{:S(2)}) collective-permute-start(bf16[32,4224]{1,0:T(8,128)(2,1)S(1)} %pad_maximum_fusion.refs_0_), channel_id=1, source_target_pairs={{0,24},{1,25},{2,26},{3,27},{4,28},{5,29},{6,30},{7,31},{8,0},{9,1... | collective-permute-start | bytes 811016 | tf_op jit(solution)/shard_map/ppermute | solution.py:60
  17.8 10.1 %collective-permute-done.32.refs_0_.refs_16_ = bf16[32,4224]{1,0:T(8,128)(2,1)S(1)} collective-permute-done((bf16[32,4224]{1,0:T(8,128)(2,1)S(1)}, bf16[32,4224]{1,0:T(8,128)(2,1)S(1)}, u32[]{:S(2)}, u32[]{:S(2)}) %collective-permute-start.32) | collective-permute-done | bytes 270368 | tf_op jit(solution)/shard_map/ppermute | solution.py:60
  30.7 1.4 %copy-done = bf16[2048,384]{1,0:T(8,128)(2,1)S(1)} copy-done((bf16[2048,384]{1,0:T(8,128)(2,1)S(1)}, bf16[2048,384]{1,0:T(8,128)(2,1)}, u32[]{:S(2)}) %copy-start) | copy-done | bytes 1572888
  32.1 1.4 %copy-done.2 = bf16[2048,384]{1,0:T(8,128)(2,1)S(1)} copy-done((bf16[2048,384]{1,0:T(8,128)(2,1)S(1)}, bf16[2048,384]{1,0:T(8,128)(2,1)}, u32[]{:S(2)}) %copy-start.2) | copy-done | bytes 1572888
  33.5 1.4 %copy-done.4 = bf16[384,2048]{1,0:T(8,128)(2,1)S(1)} copy-done((bf16[384,2048]{1,0:T(8,128)(2,1)S(1)}, bf16[384,2048]{1,0:T(8,128)(2,1)}, u32[]{:S(2)}) %copy-start.4) | copy-done | bytes 1572888
  34.9 3.6 %expert_terms.3 = (bf16[32,2176]{1,0:T(8,128)(2,1)S(1)}, bf16[32,2176]{1,0:T(8,128)(2,1)S(1)}, bf16[32,2176]{1,0:T(8,128)(2,1)S(1)}, bf16[32,2176]{1,0:T(8,128)(...) custom-call(s32[1]{0:T(128)} %bitcast.expert_ref, ...), custom_call_target="tpu_custom_call" | custom-call | flops 2013265920 | bytes 7864320 | tf_op jit(solution)/shard_map/expert_terms/pallas_call | solution.py:131
  41.9 7.1 %collective-permute-done.33.refs_1_.refs_17_ = bf16[32,4224]{1,0:T(8,128)(2,1)S(1)} collective-permute-done((bf16[32,4224]{1,0:T(8,128)(2,1)S(1)}, bf16[32,4224]{1,0:T(8,128)(2,1)S(1)}, u32[]{:S(2)}, u32[]{:S(2)}) %collective-permute-start.33) | collective-permute-done | bytes 270368 | tf_op jit(solution)/shard_map/ppermute | solution.py:60
  49.0 4.4 %collective-permute-done.35.refs_3_.refs_19_ = bf16[32,4224]{1,0:T(8,128)(2,1)S(1)} collective-permute-done((bf16[32,4224]{1,0:T(8,128)(2,1)S(1)}, bf16[32,4224]{1,0:T(8,128)(2,1)S(1)}, u32[]{:S(2)}, u32[]{:S(2)}) %collective-permute-start.35) | collective-permute-done | bytes 270368 | tf_op jit(solution)/shard_map/ppermute | solution.py:60
  56.7 3.6 %expert_terms.5 = (bf16[32,2176]{1,0:T(8,128)(2,1)S(1)}, bf16[32,2176]{1,0:T(8,128)(2,1)S(1)}, bf16[32,2176]{1,0:T(8,128)(2,1)S(1)}, bf16[32,2176]{1,0:T(8,128)(...) custom-call(s32[1]{0:T(128)} %bitcast.expert_ref, ...), custom_call_target="tpu_custom_call" | custom-call | flops 2013265920 | bytes 7864320 | tf_op jit(solution)/shard_map/expert_terms/pallas_call | solution.py:131
  61.6 3.4 %collective-permute-done.12 = bf16[32,2176]{1,0:T(8,128)(2,1)S(1)} collective-permute-done((bf16[32,2176]{1,0:T(8,128)(2,1)S(1)}, bf16[32,2176]{1,0:T(8,128)(2,1)S(1)}, u32[]{:S(2)}, u32[]{:S(2)}) %collective-permute-start.12) | collective-permute-done | bytes 139296 | tf_op jit(solution)/shard_map/ppermute | solution.py:60
  67.9 2.9 %collective-permute-done.18.refs_3_.refs_11_ = bf16[64,4224]{1,0:T(8,128)(2,1)S(1)} collective-permute-done((bf16[64,4224]{1,0:T(8,128)(2,1)S(1)}, bf16[64,4224]{1,0:T(8,128)(2,1)S(1)}, u32[]{:S(2)}, u32[]{:S(2)}) %collective-permute-start.18) | collective-permute-done | bytes 540704 | tf_op jit(solution)/shard_map/ppermute | solution.py:60
  73.5 6.6 %expert_terms.4 = (bf16[64,2176]{1,0:T(8,128)(2,1)S(1)}, bf16[64,2176]{1,0:T(8,128)(2,1)S(1)}, bf16[64,2176]{1,0:T(8,128)(2,1)S(1)}, bf16[64,2176]{1,0:T(8,128)(...) custom-call(s32[1]{0:T(128)} %bitcast.expert_ref, ...), custom_call_target="tpu_custom_call" | custom-call | flops 4026531840 | bytes 11010048 | tf_op jit(solution)/shard_map/expert_terms/pallas_call | solution.py:131
  81.9 1.3 %collective-permute-done.24 = bf16[64,2176]{1,0:T(8,128)(2,1)S(1)} collective-permute-done((bf16[64,2176]{1,0:T(8,128)(2,1)S(1)}, bf16[64,2176]{1,0:T(8,128)(2,1)S(1)}, u32[]{:S(2)}, u32[]{:S(2)}) %collective-permute-start.24) | collective-permute-done | bytes 278560 | tf_op jit(solution)/shard_map/ppermute | solution.py:60
  85.4 4.4 %collective-permute-done.28 = bf16[64,2176]{1,0:T(8,128)(2,1)S(1)} collective-permute-done((bf16[64,2176]{1,0:T(8,128)(2,1)S(1)}, bf16[64,2176]{1,0:T(8,128)(2,1)S(1)}, u32[]{:S(2)}, u32[]{:S(2)}) %collective-permute-start.28) | collective-permute-done | bytes 278560 | tf_op jit(solution)/shard_map/ppermute | solution.py:60
  92.6 2.7 %collective-permute-done.46 = bf16[32,2176]{1,0:T(8,128)(2,1)S(1)} collective-permute-done((bf16[32,2176]{1,0:T(8,128)(2,1)S(1)}, bf16[32,2176]{1,0:T(8,128)(2,1)S(1)}, u32[]{:S(2)}, u32[]{:S(2)}) %collective-permute-start.46) | collective-permute-done | bytes 139296 | tf_op jit(solution)/shard_map/ppermute | solution.py:60
  95.3 2.0 %collective-permute-start.29 = (bf16[64,2176]{1,0:T(8,128)(2,1)S(1)}, bf16[64,2176]{1,0:T(8,128)(2,1)S(1)}, u32[]{:S(2)}, u32[]{:S(2)}) collective-permute-start(bf16[64,2176]{1,0:T(8,128)(2,1)S(1)} %add_convert_fusion.1), channel_id=1, source_target_pairs={{0,4},{1,3},{2,6},{3,1},{4,0},{5,7},{6,2},{7,5},{8,12},{9,11},{10,... | collective-permute-start | bytes 835592 | tf_op jit(solution)/shard_map/ppermute | solution.py:60
  97.5 2.8 %collective-permute-done.25 = bf16[64,2176]{1,0:T(8,128)(2,1)S(1)} collective-permute-done((bf16[64,2176]{1,0:T(8,128)(2,1)S(1)}, bf16[64,2176]{1,0:T(8,128)(2,1)S(1)}, u32[]{:S(2)}, u32[]{:S(2)}) %collective-permute-start.25) | collective-permute-done | bytes 278560 | tf_op jit(solution)/shard_map/ppermute | solution.py:60
  100.3 6.2 %collective-permute-start.47 = (bf16[32,2176]{1,0:T(8,128)(2,1)S(1)}, bf16[32,2176]{1,0:T(8,128)(2,1)S(1)}, u32[]{:S(2)}, u32[]{:S(2)}) collective-permute-start(bf16[32,2176]{1,0:T(8,128)(2,1)S(1)} %add_convert_fusion.6), channel_id=1, source_target_pairs={{0,16},{1,17},{2,18},{3,19},{4,20},{5,21},{6,22},{7,23},{8,24},{9,... | collective-permute-start | bytes 417800 | tf_op jit(solution)/shard_map/ppermute | solution.py:60
  107.2 3.4 %collective-permute-start.30 = (bf16[32,2176]{1,0:T(8,128)(2,1)S(1)}, bf16[32,2176]{1,0:T(8,128)(2,1)S(1)}, u32[]{:S(2)}, u32[]{:S(2)}) collective-permute-start(bf16[32,2176]{1,0:T(8,128)(2,1)S(1)} %get-tuple-element.76), channel_id=1, source_target_pairs={{0,24},{1,25},{2,26},{3,27},{4,28},{5,29},{6,30},{7,31},{8,0},{9,1... | collective-permute-start | bytes 417800 | tf_op jit(solution)/shard_map/ppermute | solution.py:60
  110.6 9.6 %weight_grads.1 = (bf16[2048,384]{1,0:T(8,128)(2,1)}, bf16[2048,384]{1,0:T(8,128)(2,1)}, bf16[384,2048]{1,0:T(8,128)(2,1)}) custom-call(bf16[32,4224]{1,0:T(8,128)(2,1)S(1)} %pad_maximum_fusion.refs_0_, bf16[32,4224]{1,0:T(8,128)(2,1)S(1)} %collective-permute-done.refs_1_, bf16[32,4224]{1,0:T(8,128)(2,1)S(1)} %collective-permute-done.1.refs_2_, ...), custom_call_target="tpu_custom_call" | custom-call | flops 4831838208 | bytes 13107200 | tf_op jit(solution)/shard_map/weight_grads/pallas_call | solution.py:198
  (109 shorter events, 28.9 us)
Async XLA Ops:
  6.3 21.6 %collective-permute-start.32 = (bf16[32,4224]{1,0:T(8,128)(2,1)S(1)}, bf16[32,4224]{1,0:T(8,128)(2,1)S(1)}, u32[]{:S(2)}, u32[]{:S(2)}) collective-permute-start(bf16[32,4224]{1,0:T(8,128)(2,1)S(1)} %pad_maximum_fusion.refs_0_), channel_id=1, source_target_pairs={{0,16},{1,17},{2,18},{3,19},{4,20},{5,21},{6,22},{7,23},{8,24},{9,... | collective-permute-start | bytes 811016 | tf_op jit(solution)/shard_map/ppermute | solution.py:60
  8.9 19.0 %collective-permute-start.14 = (bf16[32,4224]{1,0:T(8,128)(2,1)S(1)}, bf16[32,4224]{1,0:T(8,128)(2,1)S(1)}, u32[]{:S(2)}, u32[]{:S(2)}) collective-permute-start(bf16[32,4224]{1,0:T(8,128)(2,1)S(1)} %pad_maximum_fusion.refs_0_), channel_id=1, source_target_pairs={{0,8},{1,9},{2,10},{3,11},{4,12},{5,13},{6,14},{7,15},{8,16},{9,17... | collective-permute-start | bytes 811016 | tf_op jit(solution)/shard_map/ppermute | solution.py:60
  10.5 18.0 %collective-permute-start = (bf16[32,4224]{1,0:T(8,128)(2,1)S(1)}, bf16[32,4224]{1,0:T(8,128)(2,1)S(1)}, u32[]{:S(2)}, u32[]{:S(2)}) collective-permute-start(bf16[32,4224]{1,0:T(8,128)(2,1)S(1)} %pad_maximum_fusion.refs_0_), channel_id=1, source_target_pairs={{0,2},{1,5},{2,0},{3,7},{4,6},{5,1},{6,4},{7,3},{8,10},{9,13},{10,... | collective-permute-start | bytes 811016 | tf_op jit(solution)/shard_map/ppermute | solution.py:60
  12.0 16.5 %collective-permute-start.2 = (bf16[32,4224]{1,0:T(8,128)(2,1)S(1)}, bf16[32,4224]{1,0:T(8,128)(2,1)S(1)}, u32[]{:S(2)}, u32[]{:S(2)}) collective-permute-start(bf16[32,4224]{1,0:T(8,128)(2,1)S(1)} %collective-permute-done.1.refs_2_), channel_id=1, source_target_pairs={{0,2},{1,5},{2,0},{3,7},{4,6},{5,1},{6,4},{7,3},{8,10},{9,13},{10,... | collective-permute-start | bytes 811016 | tf_op jit(solution)/shard_map/ppermute | solution.py:60
  12.9 25.8 %collective-permute-start.15 = (bf16[32,4224]{1,0:T(8,128)(2,1)S(1)}, bf16[32,4224]{1,0:T(8,128)(2,1)S(1)}, u32[]{:S(2)}, u32[]{:S(2)}) collective-permute-start(bf16[32,4224]{1,0:T(8,128)(2,1)S(1)} %pad_maximum_fusion.refs_0_), channel_id=1, source_target_pairs={{0,24},{1,25},{2,26},{3,27},{4,28},{5,29},{6,30},{7,31},{8,0},{9,1... | collective-permute-start | bytes 811016 | tf_op jit(solution)/shard_map/ppermute | solution.py:60
  29.5 11.4 %collective-permute-start.34 = (bf16[32,4224]{1,0:T(8,128)(2,1)S(1)}, bf16[32,4224]{1,0:T(8,128)(2,1)S(1)}, u32[]{:S(2)}, u32[]{:S(2)}) collective-permute-start(bf16[32,4224]{1,0:T(8,128)(2,1)S(1)} %collective-permute-done.32.refs_0_.refs_16_), channel_id=1, source_target_pairs={{0,4},{1,3},{2,6},{3,1},{4,0},{5,7},{6,2},{7,5},{8,12},{9,11},{10,... | collective-permute-start | bytes 811016 | tf_op jit(solution)/shard_map/ppermute | solution.py:60
  38.7 21.6 %collective-permute-start.17 = (bf16[64,4224]{1,0:T(8,128)(2,1)S(1)}, bf16[64,4224]{1,0:T(8,128)(2,1)S(1)}, u32[]{:S(2)}, u32[]{:S(2)}) collective-permute-start(bf16[64,4224]{1,0:T(8,128)(2,1)S(1)} %constant_dynamic-update-slice_fusion.refs_0_.refs_8_), channel_id=1, source_target_pairs={{0,4},{1,3},{2,6},{3,1},{4,0},{5,7},{6,2},{7,5},{8,12},{9,11},{10,... | collective-permute-start | bytes 1622024 | tf_op jit(solution)/shard_map/ppermute | solution.py:60
  39.6 9.4 %collective-permute-start.33 = (bf16[32,4224]{1,0:T(8,128)(2,1)S(1)}, bf16[32,4224]{1,0:T(8,128)(2,1)S(1)}, u32[]{:S(2)}, u32[]{:S(2)}) collective-permute-start(bf16[32,4224]{1,0:T(8,128)(2,1)S(1)} %collective-permute-done.32.refs_0_.refs_16_), channel_id=1, source_target_pairs={{0,2},{1,5},{2,0},{3,7},{4,6},{5,1},{6,4},{7,3},{8,10},{9,13},{10,... | collective-permute-start | bytes 811016 | tf_op jit(solution)/shard_map/ppermute | solution.py:60
  40.8 13.2 %collective-permute-start.36 = (bf16[32,4224]{1,0:T(8,128)(2,1)S(1)}, bf16[32,4224]{1,0:T(8,128)(2,1)S(1)}, u32[]{:S(2)}, u32[]{:S(2)}) collective-permute-start(bf16[32,4224]{1,0:T(8,128)(2,1)S(1)} %collective-permute-done.32.refs_0_.refs_16_), channel_id=1, source_target_pairs={{0,1},{1,0},{2,3},{3,2},{4,5},{5,4},{6,7},{7,6},{8,9},{9,8},{10,11... | collective-permute-start | bytes 811016 | tf_op jit(solution)/shard_map/ppermute | solution.py:60
  40.9 12.5 %collective-permute-start.35 = (bf16[32,4224]{1,0:T(8,128)(2,1)S(1)}, bf16[32,4224]{1,0:T(8,128)(2,1)S(1)}, u32[]{:S(2)}, u32[]{:S(2)}) collective-permute-start(bf16[32,4224]{1,0:T(8,128)(2,1)S(1)} %collective-permute-done.34.refs_2_.refs_18_), channel_id=1, source_target_pairs={{0,2},{1,5},{2,0},{3,7},{4,6},{5,1},{6,4},{7,3},{8,10},{9,13},{10,... | collective-permute-start | bytes 811016 | tf_op jit(solution)/shard_map/ppermute | solution.py:60
  41.6 12.4 %collective-permute-start.8 = (bf16[32,2176]{1,0:T(8,128)(2,1)S(1)}, bf16[32,2176]{1,0:T(8,128)(2,1)S(1)}, u32[]{:S(2)}, u32[]{:S(2)}) collective-permute-start(bf16[32,2176]{1,0:T(8,128)(2,1)S(1)} %get-tuple-element.41), channel_id=1, source_target_pairs={{0,1},{1,0},{2,3},{3,2},{4,5},{5,4},{6,7},{7,6},{8,9},{9,8},{10,11... | collective-permute-start | bytes 417800 | tf_op jit(solution)/shard_map/ppermute | solution.py:60
  54.1 12.5 %collective-permute-start.16 = (bf16[64,4224]{1,0:T(8,128)(2,1)S(1)}, bf16[64,4224]{1,0:T(8,128)(2,1)S(1)}, u32[]{:S(2)}, u32[]{:S(2)}) collective-permute-start(bf16[64,4224]{1,0:T(8,128)(2,1)S(1)} %constant_dynamic-update-slice_fusion.refs_0_.refs_8_), channel_id=1, source_target_pairs={{0,2},{1,5},{2,0},{3,7},{4,6},{5,1},{6,4},{7,3},{8,10},{9,13},{10,... | collective-permute-start | bytes 1622024 | tf_op jit(solution)/shard_map/ppermute | solution.py:60
  55.2 15.6 %collective-permute-start.19 = (bf16[64,4224]{1,0:T(8,128)(2,1)S(1)}, bf16[64,4224]{1,0:T(8,128)(2,1)S(1)}, u32[]{:S(2)}, u32[]{:S(2)}) collective-permute-start(bf16[64,4224]{1,0:T(8,128)(2,1)S(1)} %constant_dynamic-update-slice_fusion.refs_0_.refs_8_), channel_id=1, source_target_pairs={{0,1},{1,0},{2,3},{3,2},{4,5},{5,4},{6,7},{7,6},{8,9},{9,8},{10,11... | collective-permute-start | bytes 1622024 | tf_op jit(solution)/shard_map/ppermute | solution.py:60
  55.7 9.3 %collective-permute-start.12 = (bf16[32,2176]{1,0:T(8,128)(2,1)S(1)}, bf16[32,2176]{1,0:T(8,128)(2,1)S(1)}, u32[]{:S(2)}, u32[]{:S(2)}) collective-permute-start(bf16[32,2176]{1,0:T(8,128)(2,1)S(1)} %add_convert_fusion.14), channel_id=1, source_target_pairs={{0,2},{1,5},{2,0},{3,7},{4,6},{5,1},{6,4},{7,3},{8,10},{9,13},{10,... | collective-permute-start | bytes 417800 | tf_op jit(solution)/shard_map/ppermute | solution.py:60
  60.3 46.8 %collective-permute-start.7 = (bf16[32,2176]{1,0:T(8,128)(2,1)S(1)}, bf16[32,2176]{1,0:T(8,128)(2,1)S(1)}, u32[]{:S(2)}, u32[]{:S(2)}) collective-permute-start(bf16[32,2176]{1,0:T(8,128)(2,1)S(1)} %get-tuple-element.39), channel_id=1, source_target_pairs={{0,1},{1,0},{2,3},{3,2},{4,5},{5,4},{6,7},{7,6},{8,9},{9,8},{10,11... | collective-permute-start | bytes 417800 | tf_op jit(solution)/shard_map/ppermute | solution.py:60
  60.4 10.4 %collective-permute-start.18 = (bf16[64,4224]{1,0:T(8,128)(2,1)S(1)}, bf16[64,4224]{1,0:T(8,128)(2,1)S(1)}, u32[]{:S(2)}, u32[]{:S(2)}) collective-permute-start(bf16[64,4224]{1,0:T(8,128)(2,1)S(1)} %collective-permute-done.17.refs_2_.refs_10_), channel_id=1, source_target_pairs={{0,2},{1,5},{2,0},{3,7},{4,6},{5,1},{6,4},{7,3},{8,10},{9,13},{10,... | collective-permute-start | bytes 1622024 | tf_op jit(solution)/shard_map/ppermute | solution.py:60
  70.8 49.3 %collective-permute-start.9 = (bf16[32,2176]{1,0:T(8,128)(2,1)S(1)}, bf16[32,2176]{1,0:T(8,128)(2,1)S(1)}, u32[]{:S(2)}, u32[]{:S(2)}) collective-permute-start(bf16[32,2176]{1,0:T(8,128)(2,1)S(1)} %add_convert_fusion.16), channel_id=1, source_target_pairs={{0,2},{1,5},{2,0},{3,7},{4,6},{5,1},{6,4},{7,3},{8,10},{9,13},{10,... | collective-permute-start | bytes 417800 | tf_op jit(solution)/shard_map/ppermute | solution.py:60
  71.9 19.4 %collective-permute-start.40 = (bf16[32,2176]{1,0:T(8,128)(2,1)S(1)}, bf16[32,2176]{1,0:T(8,128)(2,1)S(1)}, u32[]{:S(2)}, u32[]{:S(2)}) collective-permute-start(bf16[32,2176]{1,0:T(8,128)(2,1)S(1)} %get-tuple-element.55), channel_id=1, source_target_pairs={{0,1},{1,0},{2,3},{3,2},{4,5},{5,4},{6,7},{7,6},{8,9},{9,8},{10,11... | collective-permute-start | bytes 417800 | tf_op jit(solution)/shard_map/ppermute | solution.py:60
  91.3 9.0 %collective-permute-start.25 = (bf16[64,2176]{1,0:T(8,128)(2,1)S(1)}, bf16[64,2176]{1,0:T(8,128)(2,1)S(1)}, u32[]{:S(2)}, u32[]{:S(2)}) collective-permute-start(bf16[64,2176]{1,0:T(8,128)(2,1)S(1)} %add_convert_fusion.4), channel_id=1, source_target_pairs={{0,2},{1,5},{2,0},{3,7},{4,6},{5,1},{6,4},{7,3},{8,10},{9,13},{10,... | collective-permute-start | bytes 835592 | tf_op jit(solution)/shard_map/ppermute | solution.py:60
  95.3 11.2 %collective-permute-start.29 = (bf16[64,2176]{1,0:T(8,128)(2,1)S(1)}, bf16[64,2176]{1,0:T(8,128)(2,1)S(1)}, u32[]{:S(2)}, u32[]{:S(2)}) collective-permute-start(bf16[64,2176]{1,0:T(8,128)(2,1)S(1)} %add_convert_fusion.1), channel_id=1, source_target_pairs={{0,4},{1,3},{2,6},{3,1},{4,0},{5,7},{6,2},{7,5},{8,12},{9,11},{10,... | collective-permute-start | bytes 835592 | tf_op jit(solution)/shard_map/ppermute | solution.py:60
  97.4 22.8 %collective-permute-start.13 = (bf16[32,2176]{1,0:T(8,128)(2,1)S(1)}, bf16[32,2176]{1,0:T(8,128)(2,1)S(1)}, u32[]{:S(2)}, u32[]{:S(2)}) collective-permute-start(bf16[32,2176]{1,0:T(8,128)(2,1)S(1)} %add_convert_fusion.13), channel_id=1, source_target_pairs={{0,4},{1,3},{2,6},{3,1},{4,0},{5,7},{6,2},{7,5},{8,12},{9,11},{10,... | collective-permute-start | bytes 417800 | tf_op jit(solution)/shard_map/ppermute | solution.py:60
  100.3 19.9 %collective-permute-start.47 = (bf16[32,2176]{1,0:T(8,128)(2,1)S(1)}, bf16[32,2176]{1,0:T(8,128)(2,1)S(1)}, u32[]{:S(2)}, u32[]{:S(2)}) collective-permute-start(bf16[32,2176]{1,0:T(8,128)(2,1)S(1)} %add_convert_fusion.6), channel_id=1, source_target_pairs={{0,16},{1,17},{2,18},{3,19},{4,20},{5,21},{6,22},{7,23},{8,24},{9,... | collective-permute-start | bytes 417800 | tf_op jit(solution)/shard_map/ppermute | solution.py:60
  106.7 13.5 %collective-permute-start.31 = (bf16[32,2176]{1,0:T(8,128)(2,1)S(1)}, bf16[32,2176]{1,0:T(8,128)(2,1)S(1)}, u32[]{:S(2)}, u32[]{:S(2)}) collective-permute-start(bf16[32,2176]{1,0:T(8,128)(2,1)S(1)} %get-tuple-element.77), channel_id=1, source_target_pairs={{0,8},{1,9},{2,10},{3,11},{4,12},{5,13},{6,14},{7,15},{8,16},{9,17... | collective-permute-start | bytes 417800 | tf_op jit(solution)/shard_map/ppermute | solution.py:60
  107.2 13.1 %collective-permute-start.30 = (bf16[32,2176]{1,0:T(8,128)(2,1)S(1)}, bf16[32,2176]{1,0:T(8,128)(2,1)S(1)}, u32[]{:S(2)}, u32[]{:S(2)}) collective-permute-start(bf16[32,2176]{1,0:T(8,128)(2,1)S(1)} %get-tuple-element.76), channel_id=1, source_target_pairs={{0,24},{1,25},{2,26},{3,27},{4,28},{5,29},{6,30},{7,31},{8,0},{9,1... | collective-permute-start | bytes 417800 | tf_op jit(solution)/shard_map/ppermute | solution.py:60
  (29 other events, 144.7 us)

commit v3 on v2

v3 whole, which is shorter than its diff:
```python
import functools

import jax
import jax.numpy as jnp
from jax import lax
from jax.experimental import pallas as pl
from jax.experimental.pallas import tpu as pltpu
from jax.sharding import PartitionSpec as P

LANES = 128
PLANE = 4
MIB = 1024 * 1024
PACK_VMEM = 56
F32 = jnp.float32
BF16 = jnp.bfloat16


def dot(left, right, left_axis, right_axis):
    return lax.dot_general(
        left, right, (((left_axis,), (right_axis,)), ((), ())), preferred_element_type=F32
    )


def split_index(index):
    return index >> 3, index >> 2 & 1, index >> 1 & 1, index & 1


def join_index(level, u, v, core):
    return ((level * 2 + u) * 2 + v) * 2 + core


def route(count, target):
    return [(index, join_index(*target(*split_index(index)))) for index in range(count)]


def core_route(count):
    return route(count, lambda level, u, v, core: (level, u, v, 1 - core))


def first_route(count):
    return route(
        count,
        lambda level, u, v, core: (level, u, 1 - v, core) if core == 0 else (level, 1 - u, v, core),
    )


def second_route(count):
    return route(
        count,
        lambda level, u, v, core: (level, 1 - u, v, core) if core == 0 else (level, u, 1 - v, core),
    )


def corner_route(count):
    return route(count, lambda level, u, v, core: (level, 1 - u, 1 - v, core))


def level_route(count, shift):
    levels = count // (2 * PLANE)
    return route(
        count,
        lambda level, u, v, core: ((level + (-shift if core else shift)) % levels, u, v, core),
    )


def send(block, pairs):
    return lax.ppermute(block, "expert", pairs)


def after(value, *earlier):
    return lax.optimization_barrier((value, *earlier))[0]


def gate_column(gates, expert):
    lane = lax.broadcasted_iota(jnp.int32, gates.shape, 1)
    return jnp.sum(jnp.where(lane == expert, gates.astype(F32), 0.0), axis=1, keepdims=True)


def terms_body(spans, arrays, width, half, expert_ref, *refs):
    held, refs = refs[:arrays], refs[arrays:]
    weights, refs = refs[:4], refs[4:]
    *parts, own_ref, kept_ref, pre_ref = refs
    pick = lambda low, high: jnp.concatenate(
        [held[i][start : start + size, low:high] for i, start, size in spans], axis=0
    )
    expert = expert_ref[0]
    rows, grads = pick(0, width), pick(width, 2 * width)
    gates = pick(2 * width, 2 * width + LANES)
    gating = gate_column(gates, expert)
    kept_ref[:, 3 * half : 3 * half + width] = rows
    kept_ref[:, 3 * half + width :] = grads
    outs = own_ref, kept_ref
    gate_grad = 0.0
    for side in range(2):
        both_w, down_w = weights[2 * side : 2 * side + 2]
        backward = dot(grads, down_w[...], 1, 1)
        pre_ref[...] = dot(rows, both_w[...], 1, 0)
        total = 0.0
        for low in range(0, half, LANES):
            span = slice(low, low + LANES)
            pre_gate = pre_ref[:, span]
            pre_up = pre_ref[:, half + low : half + low + LANES]
            back = backward[:, span]
            logistic = jax.nn.sigmoid(pre_gate)
            activated = pre_gate * logistic
            hidden = (activated * pre_up).astype(BF16)
            total = total + hidden.astype(F32) * back
            grad_hidden = gating * back
            grad_gate = grad_hidden * pre_up * logistic * (1.0 + pre_gate * (1.0 - logistic))
            grad_up = grad_hidden * activated
            out = outs[side]
            out[:, span] = grad_gate.astype(BF16)
            out[:, half + low : half + low + LANES] = grad_up.astype(BF16)
            scaled = gating * (activated * pre_up)
            out[:, 2 * half + low : 2 * half + low + LANES] = scaled.astype(BF16)
        gate_grad += jnp.sum(total, axis=1, keepdims=True).astype(BF16).astype(F32)
    lane = lax.broadcasted_iota(jnp.int32, gates.shape, 1)
    gate_lanes = jnp.where(lane == expert, gate_grad, 0.0).astype(BF16)
    scatter(gate_lanes, parts, slice(width, None))
    tile = 512 if width % 512 == 0 else width
    for low in range(0, width, tile):
        span = slice(low, low + tile)
        token = 0.0
        for both_w, out in zip(weights[::2], outs):
            token += dot(out[:, : 2 * half], both_w[span, :], 1, 1)
        scatter(token.astype(BF16), parts, span)


def scatter(value, parts, span):
    start = 0
    for part in parts:
        stop = start + part.shape[0]
        part[:, span] = value[start:stop]
        start = stop


def expert_terms(blocks, weights, expert):
    half, width = weights[1].shape
    arrays = []
    for place in blocks:
        for array, _, _ in place:
            if not any(array is known for known in arrays):
                arrays.append(array)
    number = lambda array: [array is known for known in arrays].index(True)
    spans = [(number(array), start, size) for place in blocks for array, start, size in place]
    sizes = [sum(size for _, _, size in place) for place in blocks]
    total = sum(sizes)
    whole = pl.BlockSpec(memory_space=pltpu.VMEM)
    out_shape = [jax.ShapeDtypeStruct((size, width + LANES), BF16) for size in sizes]
    out_shape.append(jax.ShapeDtypeStruct((total, 3 * half), BF16))
    out_shape.append(jax.ShapeDtypeStruct((total, 2 * width + 3 * half), BF16))
    *parts, own, kept = pl.pallas_call(
        functools.partial(terms_body, spans, len(arrays), width, half),
        out_shape=out_shape,
        in_specs=[pl.BlockSpec(memory_space=pltpu.SMEM)] + [whole] * (len(arrays) + 4),
        out_specs=[whole] * len(out_shape),
        scratch_shapes=[pltpu.VMEM((total, 2 * half), F32)],
        compiler_params=pltpu.CompilerParams(vmem_limit_bytes=16 * MIB),
        cost_estimate=pl.CostEstimate(
            flops=total * width, bytes_accessed=total * width, transcendentals=0
        ),
        name="expert_terms",
    )(expert, *arrays, *weights)
    return parts, own, kept


def stack_body(sizes, *refs):
    blocks = list(refs[: sum(sizes)])
    for size, out in zip(sizes, refs[sum(sizes) :]):
        start = 0
        for _ in range(size):
            block = blocks.pop(0)
            out[start : start + block.shape[0], :] = block[...]
            start += block.shape[0]


def stacks(*lists):
    return pl.pallas_call(
        functools.partial(stack_body, [len(blocks) for blocks in lists]),
        out_shape=[
            jax.ShapeDtypeStruct((sum(b.shape[0] for b in blocks), blocks[0].shape[1]), BF16)
            for blocks in lists
        ],
        compiler_params=pltpu.CompilerParams(vmem_limit_bytes=8 * MIB),
        name="stacks",
    )(*(block for blocks in lists for block in blocks))


def grads_body(groups, width, half, *refs):
    rows, refs = refs[:groups], refs[groups:]
    terms, refs = refs[:groups], refs[groups:]
    gate_out, up_out, down_out, held, sems = refs
    tile = gate_out.shape[0]
    step, steps = pl.program_id(0), pl.num_programs(0)

    def copies(at, slot):
        start = 0
        for i, block in enumerate(rows):
            size = block.shape[0]
            for side in range(2):
                source = pl.ds(pl.multiple_of(3 * half + side * width + at * tile, LANES), tile)
                yield pltpu.make_async_copy(
                    block.at[:, source],
                    held.at[slot, side, pl.ds(start, size), :],
                    sems.at[slot, side, i],
                )
            start += size

    @pl.when(step == 0)
    def _():
        for copy in copies(0, 0):
            copy.start()

    @pl.when(step + 1 < steps)
    def _():
        for copy in copies(step + 1, (step + 1) % 2):
            copy.start()

    slot = step % 2
    for copy in copies(step, slot):
        copy.wait()
    pairs = jnp.concatenate([term[:, : 2 * half] for term in terms], axis=0)
    hidden = jnp.concatenate([term[:, 2 * half :] for term in terms], axis=0)
    both = dot(held[slot, 0], pairs, 0, 0).astype(BF16)
    gate_out[...] = both[:, :half]
    up_out[...] = both[:, half:]
    down_out[...] = dot(hidden, held[slot, 1], 0, 0).astype(BF16)


def weight_grads(rows, terms, width, half):
    groups = len(rows)
    total = sum(block.shape[0] for block in rows)
    tile = width // 2 if total <= 1024 else width // 8
    column = pl.BlockSpec((tile, half), lambda i: (i, 0))
    return pl.pallas_call(
        functools.partial(grads_body, groups, width, half),
        grid=(width // tile,),
        out_shape=[jax.ShapeDtypeStruct((width, half), BF16)] * 2
        + [jax.ShapeDtypeStruct((half, width), BF16)],
        in_specs=[pl.BlockSpec(memory_space=pl.ANY)] * groups
        + [pl.BlockSpec((term.shape[0], 3 * half), lambda i: (0, 0)) for term in terms],
        out_specs=[column, column, pl.BlockSpec((half, tile), lambda i: (0, i))],
        scratch_shapes=[
            pltpu.VMEM((2, 2, total, tile), BF16),
            pltpu.SemaphoreType.DMA((2, 2, groups)),
        ],
        compiler_params=pltpu.CompilerParams(vmem_limit_bytes=(28 if total <= 1024 else 48) * MIB),
        cost_estimate=pl.CostEstimate(
            flops=2 * 3 * total * width * half,
            bytes_accessed=4 * total * width + 6 * width * half,
            transcendentals=0,
        ),
        name="weight_grads",
    )(*rows, *terms)


def add(left, right):
    return (left.astype(F32) + right.astype(F32)).astype(BF16)


def local(tokens, upstream, expert_ids, gate_weights, w_gate, w_up, w_down):
    tok_count, width = tokens.shape
    half = w_gate.shape[1]
    count = lax.axis_size("expert")
    levels = count // (2 * PLANE)
    expert = (lax.axis_index("expert") // 2).astype(jnp.int32)[None]
    chosen = expert_ids[:, :, None] == jnp.arange(LANES, dtype=jnp.int32)[None, None, :]
    gates = jnp.sum(jnp.where(chosen, gate_weights.astype(F32)[:, :, None], 0.0), axis=1)
    home = jnp.concatenate([tokens, upstream, gates.astype(BF16)], axis=1)

    first, second, corner = first_route(count), second_route(count), corner_route(count)
    swap = core_route(count)
    onward, backward = level_route(count, 1), level_route(count, -1)
    both = jnp.concatenate([w_gate, w_up], axis=1)
    weights = [both, w_down, send(both, swap)]
    last = levels // 2

    ways = {1: (home, None), -1: (home, None)}
    units, results, planes, arrived, rows, terms = [], [], {}, [], [], []
    done = ()
    for step in range(last + 4):
        ready, done, sent = done, [], ()

        def pass_on(block, pairs):
            result = send(after(block, *ready) if ready else block, pairs)
            done.append(result)
            return result

        if step <= last:
            here = [way for way in (1, -1) if step and ways[way][0] is not None]
            lists = [[ways[way][0] for way in here]]
            for way in here:
                if step + 1 < last or (way == 1 and step < last):
                    lists.append(list(ways[way]))
            lists = [blocks for blocks in lists if len(blocks) > 1]
            stacked = list(stacks(*lists)) if lists else []
            mine = home if step == 0 else stacked.pop(0) if len(here) > 1 else ways[1][0]
            new, corners = {1: (None, None), -1: (None, None)}, []
            for way in (1, -1):
                goes_on = step < last if way == 1 else step + 1 < last
                pairs = level_route(count, way)
                if step == 0:
                    if goes_on:
                        new[way] = (pass_on(home, pairs), None)
                elif way in here:
                    got = pass_on(stacked.pop(0) if goes_on else ways[way][1], pairs)
                    corner_at = tok_count if goes_on else 0
                    corners.append((got, corner_at, tok_count))
                    if goes_on:
                        new[way] = (got[:tok_count], got[tok_count:])
                    else:
                        new[way] = (None, got)
            sent = (mine,)
            near, beside = pass_on(mine, first), pass_on(mine, second)
            if step == 0:
                across = send(beside, first)
                done.append(across)
                corners = [(across, 0, tok_count)]
                new = {way: (new[way][0], across) for way in new}
            if step == 1:
                weights.append(send(after(w_down, *ready), swap))
            units.append([[(block, 0, block.shape[0])] for block in (mine, near, beside)] + [corners])
            ways = new
        if 1 <= step - 2 <= last:
            at = step - 3
            beside_back = pass_on(add(results[at][2], across_back), second)
            planes[at] = [results[at][0], near_back, beside_back]
        if 0 <= step - 2 <= last:
            at = step - 2
            if at < last:
                across_back, near_back = pass_on(results[at][3], first), pass_on(results[at][1], first)
            else:
                pieces = [pass_on(part, pairs) for part, pairs in zip(results[at][1:], (first, second, corner))]
                planes[at] = [results[at][0], *pieces]
            pass_on(rows[2 * at], swap)
            rows[2 * at + 1] = terms[2 * at + 1] = done[-1]
        if 0 <= step - 1 <= last:
            unit = units[step - 1]
            block, *span = unit[0][0]
            unit[0][0] = (after(block, *ready, *sent), *span)
            parts, own, kept = expert_terms(unit, weights, expert)
            done.append(parts[0])
            results.append(parts)
            rows += [kept, None]
            terms += [own, None]
        back_home = [at for at in planes if planes[at] and (at < last - 1 or step == last + 3)]
        if step >= 3:
            for at in back_home:
                plane = sum(piece.astype(F32) for piece in planes[at]).astype(BF16)
                planes[at] = None
                if at == 0:
                    arrived.append(plane)
                else:
                    arrived.append(pass_on(plane[:tok_count], level_route(count, -at)))
                if plane.shape[0] > tok_count:
                    arrived.append(pass_on(plane[tok_count:], level_route(count, at)))

    grads = weight_grads(rows, terms, width, half)
    arrived[-1] = after(arrived[-1], *grads)

    grad_tokens = sum(piece[:, :width].astype(F32) for piece in arrived).astype(BF16)
    gate_sums = sum(piece[:, width:].astype(F32) for piece in arrived)
    grad_gates = jnp.sum(jnp.where(chosen, gate_sums[:, None, :], 0.0), axis=2).astype(BF16)
    return (grad_tokens, grad_gates, *grads)


def solution(mesh):
    rows = P(("group", "expert"), None)
    return jax.shard_map(
        local,
        mesh=mesh,
        in_specs=(rows, rows, rows, rows, P("group", "expert"), P("group", "expert"), P("expert", "group")),
        out_specs=(rows, rows, P("group", "expert"), P("group", "expert"), P("expert", "group")),
        check_vma=False,
    )
```

time: 122 us -> 105 us (0.86)
  waiting for transfers between devices: 44.3 us -> 28.6 us
  starting transfers between devices: 43.9 us -> 32.3 us
  Pallas kernels: 23.5 us -> 29 us
  local copies, waits for them, and re-layouts: 7.15 us -> 11.4 us
    ppermute x48 -> x29, waiting for transfers between devices: 44.3 us -> 28.6 us  [send(): return lax.ppermute(block, 'expert', pairs)]
    ppermute x48 -> x29, starting transfers between devices: 43.9 us -> 32.3 us  [send(): return lax.ppermute(block, 'expert', pairs)]
    pallas_call x4 -> x5, Pallas kernels: 23.5 us -> 29 us  [the longest x3 19.6 us: expert_terms(): pl.pallas_call(functools.partial(terms_body, spans, len(arrays), width, h...]
    unnamed x13 -> x27, local copies, waits for them, and re-layouts: 5.67 us -> 9.93 us
  transfers between devices with their start and end apart: 48 -> 29, of which waited for: 17 -> 12; matrix products, arithmetic and copies ran while one was open for 1% -> 3% of each run, Pallas kernels for 19% -> 28%
where the time goes in v3:
time: 105 us
  starting transfers between devices  32.3 us (31%)
  Pallas kernels  29 us (28%)
  waiting for transfers between devices  28.6 us (27%)
  local copies, waits for them, and re-layouts  11.4 us (11%)
  other arithmetic  2.41 us (2%)
    ppermute x29, starting transfers between devices, send(): return lax.ppermute(block, 'expert', pairs)  32.3 us
    ppermute x29, waiting for transfers between devices, send(): return lax.ppermute(block, 'expert', pairs)  28.6 us
    pallas_call x3, Pallas kernels, expert_terms(): pl.pallas_call(functools.partial(terms_body, spans, len(arrays), width, h...  19.6 us
    unnamed x27, local copies, waits for them, and re-layouts  9.93 us
    pallas_call x1, Pallas kernels, weight_grads(): pl.pallas_call(functools.partial(grads_body, groups, width, half), grid=(...  7.42 us
  transfers between devices with their start and end apart: 29, of which 12 were waited for; matrix products, arithmetic and copies ran while one was open for 3% of the time, Pallas kernels for 28%

profile of v3, /device:TPU:0, one launch (start us, length us, event | category | flops | bytes accessed | tf_op | source)
XLA Modules:
  0.0 104.5 jit_solution(5105103110829945514)
XLA Ops:
  0.6 1.7 %constant_dynamic-update-slice_fusion.1 = bf16[2048,768]{1,0:T(8,128)(2,1)S(1)} fusion(bf16[2048,384]{1,0:T(8,128)(2,1)} %param.11), kind=kLoop, calls=%fused_computation.12 | loop fusion | bytes 3145728
  4.7 2.9 %collective-permute-start.3 = (bf16[32,4224]{1,0:T(8,128)(2,1)S(1)}, bf16[32,4224]{1,0:T(8,128)(2,1)S(1)}, u32[]{:S(2)}, u32[]{:S(2)}) collective-permute-start(bf16[32,4224]{1,0:T(8,128)(2,1)S(1)} %pad_maximum_fusion.refs_0_), channel_id=1, source_target_pairs={{0,4},{1,3},{2,6},{3,1},{4,0},{5,7},{6,2},{7,5},{8,12},{9,11},{10,... | collective-permute-start | bytes 811016 | tf_op jit(solution)/shard_map/ppermute | solution.py:67
  7.5 1.5 %collective-permute-start.2 = (bf16[32,4224]{1,0:T(8,128)(2,1)S(1)}, bf16[32,4224]{1,0:T(8,128)(2,1)S(1)}, u32[]{:S(2)}, u32[]{:S(2)}) collective-permute-start(bf16[32,4224]{1,0:T(8,128)(2,1)S(1)} %pad_maximum_fusion.refs_0_), channel_id=1, source_target_pairs={{0,2},{1,5},{2,0},{3,7},{4,6},{5,1},{6,4},{7,3},{8,10},{9,13},{10,... | collective-permute-start | bytes 811016 | tf_op jit(solution)/shard_map/ppermute | solution.py:67
  9.0 3.6 %collective-permute-start.1 = (bf16[32,4224]{1,0:T(8,128)(2,1)S(1)}, bf16[32,4224]{1,0:T(8,128)(2,1)S(1)}, u32[]{:S(2)}, u32[]{:S(2)}) collective-permute-start(bf16[32,4224]{1,0:T(8,128)(2,1)S(1)} %pad_maximum_fusion.refs_0_), channel_id=1, source_target_pairs={{0,24},{1,9},{2,26},{3,11},{4,28},{5,13},{6,30},{7,15},{8,0},{9,17... | collective-permute-start | bytes 811016 | tf_op jit(solution)/shard_map/ppermute | solution.py:67
  14.0 2.2 %collective-permute-start.4 = (bf16[32,4224]{1,0:T(8,128)(2,1)S(1)}, bf16[32,4224]{1,0:T(8,128)(2,1)}, u32[]{:S(2)}, u32[]{:S(2)}) collective-permute-start(bf16[32,4224]{1,0:T(8,128)(2,1)S(1)} %collective-permute-done.3.refs_2_), channel_id=1, source_target_pairs={{0,2},{1,5},{2,0},{3,7},{4,6},{5,1},{6,4},{7,3},{8,10},{9,13},{10,... | collective-permute-start | bytes 811016 | tf_op jit(solution)/shard_map/ppermute | solution.py:67
  17.6 4.4 %collective-permute-done.1.refs_1_ = bf16[32,4224]{1,0:T(8,128)(2,1)S(1)} collective-permute-done((bf16[32,4224]{1,0:T(8,128)(2,1)S(1)}, bf16[32,4224]{1,0:T(8,128)(2,1)S(1)}, u32[]{:S(2)}, u32[]{:S(2)}) %collective-permute-start.1) | collective-permute-done | bytes 270368 | tf_op jit(solution)/shard_map/ppermute | solution.py:67
  22.0 2.7 %collective-permute-done.refs_0_.refs_2_ = bf16[32,4224]{1,0:T(8,128)(2,1)S(1)} collective-permute-done((bf16[32,4224]{1,0:T(8,128)(2,1)S(1)}, bf16[32,4224]{1,0:T(8,128)(2,1)S(1)}, u32[]{:S(2)}, u32[]{:S(2)}) %collective-permute-start) | collective-permute-done | bytes 270368 | tf_op jit(solution)/shard_map/ppermute | solution.py:67
  24.7 2.0 %stacks.1 = (bf16[64,4224]{1,0:T(8,128)(2,1)}, bf16[64,4224]{1,0:T(8,128)(2,1)}) custom-call(bf16[32,4224]{1,0:T(8,128)(2,1)S(1)} %collective-permute-done.refs_0_.refs_2_, bf16[32,4224]{1,0:T(8,128)(2,1)S(1)} %collective-permute-done.1.refs_1_, bf16[32,4224]{1,0:T(8,128)(2,1)S(1)} %collective-permute-done.refs_0_.refs_2_, ...), custom_call_target="tpu_custom_call" | custom-call | tf_op jit(solution)/shard_map/stacks/pallas_call | solution.py:178
  29.5 3.2 %collective-permute-start.8 = (bf16[32,4224]{1,0:T(8,128)(2,1)}, bf16[32,4224]{1,0:T(8,128)(2,1)}, u32[]{:S(2)}, u32[]{:S(2)}) collective-permute-start(bf16[32,4224]{1,0:T(8,128)(2,1)} %collective-permute-done.4.refs_3_), channel_id=1, source_target_pairs={{0,24},{1,9},{2,26},{3,11},{4,28},{5,13},{6,30},{7,15},{8,0},{9,17... | collective-permute-start | bytes 811016 | tf_op jit(solution)/shard_map/ppermute | solution.py:67
  32.7 1.4 %copy-done = bf16[384,2048]{1,0:T(8,128)(2,1)S(1)} copy-done((bf16[384,2048]{1,0:T(8,128)(2,1)S(1)}, bf16[384,2048]{1,0:T(8,128)(2,1)}, u32[]{:S(2)}) %copy-start) | copy-done | bytes 1572888
  37.5 6.2 %expert_terms.3 = (bf16[32,2176]{1,0:T(8,128)(2,1)S(1)}, bf16[32,2176]{1,0:T(8,128)(2,1)S(1)}, bf16[32,2176]{1,0:T(8,128)(2,1)S(1)}, bf16[32,2176]{1,0:T(8,128)(...) custom-call(s32[1]{0:T(128)} %bitcast.expert_ref, bf16[32,4224]{1,0:T(8,128)(2,1)S(1)} %pad_maximum_fusion.refs_0_, ...), custom_call_target="tpu_custom_call" | custom-call | flops 262144 | bytes 262144 | tf_op jit(solution)/shard_map/expert_terms/pallas_call | solution.py:152
  43.6 4.3 %collective-permute-done.8.refs_4_ = bf16[32,4224]{1,0:T(8,128)(2,1)} collective-permute-done((bf16[32,4224]{1,0:T(8,128)(2,1)}, bf16[32,4224]{1,0:T(8,128)(2,1)}, u32[]{:S(2)}, u32[]{:S(2)}) %collective-permute-start.8) | collective-permute-done | bytes 270368 | tf_op jit(solution)/shard_map/ppermute | solution.py:67
  54.3 7.5 %expert_terms.4 = (bf16[64,2176]{1,0:T(8,128)(2,1)S(1)}, bf16[64,2176]{1,0:T(8,128)(2,1)S(1)}, bf16[64,2176]{1,0:T(8,128)(2,1)S(1)}, bf16[64,2176]{1,0:T(8,128)(...) custom-call(s32[1]{0:T(128)} %bitcast.expert_ref, bf16[64,4224]{1,0:T(8,128)(2,1)} %get-tuple-element.70.refs_0_, ...), custom_call_target="tpu_custom_call" | custom-call | flops 524288 | bytes 524288 | tf_op jit(solution)/shard_map/expert_terms/pallas_call | solution.py:152
  64.8 1.5 %collective-permute-start.19 = (bf16[64,2176]{1,0:T(8,128)(2,1)S(1)}, bf16[64,2176]{1,0:T(8,128)(2,1)S(1)}, u32[]{:S(2)}, u32[]{:S(2)}) collective-permute-start(bf16[64,2176]{1,0:T(8,128)(2,1)S(1)} %get-tuple-element.77), channel_id=1, source_target_pairs={{0,2},{1,5},{2,0},{3,7},{4,6},{5,1},{6,4},{7,3},{8,10},{9,13},{10,... | collective-permute-start | bytes 835592 | tf_op jit(solution)/shard_map/ppermute | solution.py:67
  66.8 5.9 %expert_terms.5 = (bf16[32,2176]{1,0:T(8,128)(2,1)S(1)}, bf16[32,2176]{1,0:T(8,128)(2,1)S(1)}, bf16[32,2176]{1,0:T(8,128)(2,1)S(1)}, bf16[32,2176]{1,0:T(8,128)(...) custom-call(s32[1]{0:T(128)} %bitcast.expert_ref, ...), custom_call_target="tpu_custom_call" | custom-call | flops 262144 | bytes 262144 | tf_op jit(solution)/shard_map/expert_terms/pallas_call | solution.py:152
  72.8 1.5 %collective-permute-done.18 = bf16[64,2176]{1,0:T(8,128)(2,1)S(1)} collective-permute-done((bf16[64,2176]{1,0:T(8,128)(2,1)S(1)}, bf16[64,2176]{1,0:T(8,128)(2,1)S(1)}, u32[]{:S(2)}, u32[]{:S(2)}) %collective-permute-start.18) | collective-permute-done | bytes 278560 | tf_op jit(solution)/shard_map/ppermute | solution.py:67
  74.3 1.5 %collective-permute-start.22 = (bf16[32,2176]{1,0:T(8,128)(2,1)S(1)}, bf16[32,2176]{1,0:T(8,128)(2,1)S(1)}, u32[]{:S(2)}, u32[]{:S(2)}) collective-permute-start(bf16[32,2176]{1,0:T(8,128)(2,1)S(1)} %get-tuple-element.84), channel_id=1, source_target_pairs={{0,2},{1,5},{2,0},{3,7},{4,6},{5,1},{6,4},{7,3},{8,10},{9,13},{10,... | collective-permute-start | bytes 417800 | tf_op jit(solution)/shard_map/ppermute | solution.py:67
  79.0 1.8 %collective-permute-done.22 = bf16[32,2176]{1,0:T(8,128)(2,1)S(1)} collective-permute-done((bf16[32,2176]{1,0:T(8,128)(2,1)S(1)}, bf16[32,2176]{1,0:T(8,128)(2,1)S(1)}, u32[]{:S(2)}, u32[]{:S(2)}) %collective-permute-start.22) | collective-permute-done | bytes 139296 | tf_op jit(solution)/shard_map/ppermute | solution.py:67
  80.9 3.5 %collective-permute-done.24 = bf16[32,2176]{1,0:T(8,128)(2,1)S(1)} collective-permute-done((bf16[32,2176]{1,0:T(8,128)(2,1)S(1)}, bf16[32,2176]{1,0:T(8,128)(2,1)S(1)}, u32[]{:S(2)}, u32[]{:S(2)}) %collective-permute-start.24) | collective-permute-done | bytes 139296 | tf_op jit(solution)/shard_map/ppermute | solution.py:67
  84.5 2.8 %collective-permute-done.21 = bf16[64,2176]{1,0:T(8,128)(2,1)S(1)} collective-permute-done((bf16[64,2176]{1,0:T(8,128)(2,1)S(1)}, bf16[64,2176]{1,0:T(8,128)(2,1)S(1)}, u32[]{:S(2)}, u32[]{:S(2)}) %collective-permute-start.21) | collective-permute-done | bytes 278560 | tf_op jit(solution)/shard_map/ppermute | solution.py:67
  87.5 1.7 %collective-permute-start.26 = (bf16[32,2176]{1,0:T(8,128)(2,1)S(1)}, bf16[32,2176]{1,0:T(8,128)(2,1)S(1)}, u32[]{:S(2)}, u32[]{:S(2)}) collective-permute-start(bf16[32,2176]{1,0:T(8,128)(2,1)S(1)} %get-tuple-element.91), channel_id=1, source_target_pairs={{0,24},{1,9},{2,26},{3,11},{4,28},{5,13},{6,30},{7,15},{8,0},{9,17... | collective-permute-start | bytes 417800 | tf_op jit(solution)/shard_map/ppermute | solution.py:67
  89.5 1.5 %collective-permute-start.28 = (bf16[32,2176]{1,0:T(8,128)(2,1)S(1)}, bf16[32,2176]{1,0:T(8,128)(2,1)S(1)}, u32[]{:S(2)}, u32[]{:S(2)}) collective-permute-start(bf16[32,2176]{1,0:T(8,128)(2,1)S(1)} %add_convert_fusion.2), channel_id=1, source_target_pairs={{0,16},{1,17},{2,18},{3,19},{4,20},{5,21},{6,22},{7,23},{8,24},{9,... | collective-permute-start | bytes 417800 | tf_op jit(solution)/shard_map/ppermute | solution.py:67
  91.1 7.4 %weight_grads.1 = (bf16[2048,384]{1,0:T(8,128)(2,1)}, bf16[2048,384]{1,0:T(8,128)(2,1)}, bf16[384,2048]{1,0:T(8,128)(2,1)}) custom-call(bf16[128,5248]{1,0:T(8,128)(2,1)S(1)} %get-tuple-element.69.refs_0_, bf16[128,5248]{1,0:T(8,128)(2,1)S(1)} %collective-permute-done.16.refs_1_.refs_7_, bf16[256,5248]{1,0:T(8,128)(2,1)S(1)} %get-tuple-element.79.refs_2_, ...), custom_call_target="tpu_custom_call" | custom-call | flops 4831838208 | bytes 13107200 | tf_op jit(solution)/shard_map/weight_grads/pallas_call | solution.py:235
  98.5 4.5 %collective-permute-done.28 = bf16[32,2176]{1,0:T(8,128)(2,1)S(1)} collective-permute-done((bf16[32,2176]{1,0:T(8,128)(2,1)S(1)}, bf16[32,2176]{1,0:T(8,128)(2,1)S(1)}, u32[]{:S(2)}, u32[]{:S(2)}) %collective-permute-start.28) | collective-permute-done | bytes 139296 | tf_op jit(solution)/shard_map/ppermute | solution.py:67
  (80 shorter events, 26.6 us)
Async XLA Ops:
  2.8 29.9 %collective-permute-start.5 = (bf16[2048,768]{1,0:T(8,128)(2,1)S(1)}, bf16[2048,768]{1,0:T(8,128)(2,1)}, u32[]{:S(2)}, u32[]{:S(2)}) collective-permute-start(bf16[2048,768]{1,0:T(8,128)(2,1)S(1)} %constant_dynamic-update-slice_fusion.refs_4_.refs_5_), channel_id=1, source_target_pairs={{0,1},{1,0},{2,3},{3,2},{4,5},{5,4},{6,7},{7,6},{8,9},{9,8},{10,11... | collective-permute-start | bytes 9437192 | tf_op jit(solution)/shard_map/ppermute | solution.py:67
  4.7 9.4 %collective-permute-start.3 = (bf16[32,4224]{1,0:T(8,128)(2,1)S(1)}, bf16[32,4224]{1,0:T(8,128)(2,1)S(1)}, u32[]{:S(2)}, u32[]{:S(2)}) collective-permute-start(bf16[32,4224]{1,0:T(8,128)(2,1)S(1)} %pad_maximum_fusion.refs_0_), channel_id=1, source_target_pairs={{0,4},{1,3},{2,6},{3,1},{4,0},{5,7},{6,2},{7,5},{8,12},{9,11},{10,... | collective-permute-start | bytes 811016 | tf_op jit(solution)/shard_map/ppermute | solution.py:67
  7.5 9.4 %collective-permute-start.2 = (bf16[32,4224]{1,0:T(8,128)(2,1)S(1)}, bf16[32,4224]{1,0:T(8,128)(2,1)S(1)}, u32[]{:S(2)}, u32[]{:S(2)}) collective-permute-start(bf16[32,4224]{1,0:T(8,128)(2,1)S(1)} %pad_maximum_fusion.refs_0_), channel_id=1, source_target_pairs={{0,2},{1,5},{2,0},{3,7},{4,6},{5,1},{6,4},{7,3},{8,10},{9,13},{10,... | collective-permute-start | bytes 811016 | tf_op jit(solution)/shard_map/ppermute | solution.py:67
  9.0 13.0 %collective-permute-start.1 = (bf16[32,4224]{1,0:T(8,128)(2,1)S(1)}, bf16[32,4224]{1,0:T(8,128)(2,1)S(1)}, u32[]{:S(2)}, u32[]{:S(2)}) collective-permute-start(bf16[32,4224]{1,0:T(8,128)(2,1)S(1)} %pad_maximum_fusion.refs_0_), channel_id=1, source_target_pairs={{0,24},{1,9},{2,26},{3,11},{4,28},{5,13},{6,30},{7,15},{8,0},{9,17... | collective-permute-start | bytes 811016 | tf_op jit(solution)/shard_map/ppermute | solution.py:67
  12.6 12.1 %collective-permute-start = (bf16[32,4224]{1,0:T(8,128)(2,1)S(1)}, bf16[32,4224]{1,0:T(8,128)(2,1)S(1)}, u32[]{:S(2)}, u32[]{:S(2)}) collective-permute-start(bf16[32,4224]{1,0:T(8,128)(2,1)S(1)} %pad_maximum_fusion.refs_0_), channel_id=1, source_target_pairs={{0,8},{1,25},{2,10},{3,27},{4,12},{5,29},{6,14},{7,31},{8,16},{9,1... | collective-permute-start | bytes 811016 | tf_op jit(solution)/shard_map/ppermute | solution.py:67
  14.0 10.7 %collective-permute-start.4 = (bf16[32,4224]{1,0:T(8,128)(2,1)S(1)}, bf16[32,4224]{1,0:T(8,128)(2,1)}, u32[]{:S(2)}, u32[]{:S(2)}) collective-permute-start(bf16[32,4224]{1,0:T(8,128)(2,1)S(1)} %collective-permute-done.3.refs_2_), channel_id=1, source_target_pairs={{0,2},{1,5},{2,0},{3,7},{4,6},{5,1},{6,4},{7,3},{8,10},{9,13},{10,... | collective-permute-start | bytes 811016 | tf_op jit(solution)/shard_map/ppermute | solution.py:67
  26.7 21.2 %collective-permute-start.10 = (bf16[64,4224]{1,0:T(8,128)(2,1)}, bf16[64,4224]{1,0:T(8,128)(2,1)}, u32[]{:S(2)}, u32[]{:S(2)}) collective-permute-start(bf16[64,4224]{1,0:T(8,128)(2,1)} %get-tuple-element.70.refs_0_), channel_id=1, source_target_pairs={{0,4},{1,3},{2,6},{3,1},{4,0},{5,7},{6,2},{7,5},{8,12},{9,11},{10,... | collective-permute-start | bytes 1622024 | tf_op jit(solution)/shard_map/ppermute | solution.py:67
  27.2 20.7 %collective-permute-start.9 = (bf16[64,4224]{1,0:T(8,128)(2,1)}, bf16[64,4224]{1,0:T(8,128)(2,1)}, u32[]{:S(2)}, u32[]{:S(2)}) collective-permute-start(bf16[64,4224]{1,0:T(8,128)(2,1)} %get-tuple-element.70.refs_0_), channel_id=1, source_target_pairs={{0,2},{1,5},{2,0},{3,7},{4,6},{5,1},{6,4},{7,3},{8,10},{9,13},{10,... | collective-permute-start | bytes 1622024 | tf_op jit(solution)/shard_map/ppermute | solution.py:67
  27.8 20.2 %collective-permute-start.7 = (bf16[64,4224]{1,0:T(8,128)(2,1)}, bf16[64,4224]{1,0:T(8,128)(2,1)}, u32[]{:S(2)}, u32[]{:S(2)}) collective-permute-start(bf16[64,4224]{1,0:T(8,128)(2,1)} %get-tuple-element.59), channel_id=1, source_target_pairs={{0,8},{1,25},{2,10},{3,27},{4,12},{5,29},{6,14},{7,31},{8,16},{9,1... | collective-permute-start | bytes 1622024 | tf_op jit(solution)/shard_map/ppermute | solution.py:67
  29.5 18.4 %collective-permute-start.8 = (bf16[32,4224]{1,0:T(8,128)(2,1)}, bf16[32,4224]{1,0:T(8,128)(2,1)}, u32[]{:S(2)}, u32[]{:S(2)}) collective-permute-start(bf16[32,4224]{1,0:T(8,128)(2,1)} %collective-permute-done.4.refs_3_), channel_id=1, source_target_pairs={{0,24},{1,9},{2,26},{3,11},{4,28},{5,13},{6,30},{7,15},{8,0},{9,17... | collective-permute-start | bytes 811016 | tf_op jit(solution)/shard_map/ppermute | solution.py:67
  48.9 14.2 %collective-permute-start.16 = (bf16[128,5248]{1,0:T(8,128)(2,1)S(1)}, bf16[128,5248]{1,0:T(8,128)(2,1)S(1)}, u32[]{:S(2)}, u32[]{:S(2)}) collective-permute-start(bf16[128,5248]{1,0:T(8,128)(2,1)S(1)} %get-tuple-element.69.refs_0_), channel_id=1, source_target_pairs={{0,1},{1,0},{2,3},{3,2},{4,5},{5,4},{6,7},{7,6},{8,9},{9,8},{10,11... | collective-permute-start | bytes 4030472 | tf_op jit(solution)/shard_map/ppermute | solution.py:67
  50.1 13.0 %collective-permute-start.13 = (bf16[32,4224]{1,0:T(8,128)(2,1)S(1)}, bf16[32,4224]{1,0:T(8,128)(2,1)S(1)}, u32[]{:S(2)}, u32[]{:S(2)}) collective-permute-start(bf16[32,4224]{1,0:T(8,128)(2,1)S(1)} %get-tuple-element.66), channel_id=1, source_target_pairs={{0,8},{1,25},{2,10},{3,27},{4,12},{5,29},{6,14},{7,31},{8,16},{9,1... | collective-permute-start | bytes 811016 | tf_op jit(solution)/shard_map/ppermute | solution.py:67
  51.5 11.7 %collective-permute-start.15 = (bf16[32,4224]{1,0:T(8,128)(2,1)S(1)}, bf16[32,4224]{1,0:T(8,128)(2,1)S(1)}, u32[]{:S(2)}, u32[]{:S(2)}) collective-permute-start(bf16[32,4224]{1,0:T(8,128)(2,1)S(1)} %get-tuple-element.80.refs_0_), channel_id=1, source_target_pairs={{0,4},{1,3},{2,6},{3,1},{4,0},{5,7},{6,2},{7,5},{8,12},{9,11},{10,... | collective-permute-start | bytes 811016 | tf_op jit(solution)/shard_map/ppermute | solution.py:67
  52.3 10.9 %collective-permute-start.14 = (bf16[32,4224]{1,0:T(8,128)(2,1)S(1)}, bf16[32,4224]{1,0:T(8,128)(2,1)S(1)}, u32[]{:S(2)}, u32[]{:S(2)}) collective-permute-start(bf16[32,4224]{1,0:T(8,128)(2,1)S(1)} %get-tuple-element.80.refs_0_), channel_id=1, source_target_pairs={{0,2},{1,5},{2,0},{3,7},{4,6},{5,1},{6,4},{7,3},{8,10},{9,13},{10,... | collective-permute-start | bytes 811016 | tf_op jit(solution)/shard_map/ppermute | solution.py:67
  53.5 9.7 %collective-permute-start.11 = (bf16[32,2176]{1,0:T(8,128)(2,1)S(1)}, bf16[32,2176]{1,0:T(8,128)(2,1)S(1)}, u32[]{:S(2)}, u32[]{:S(2)}) collective-permute-start(bf16[32,2176]{1,0:T(8,128)(2,1)S(1)} %get-tuple-element.62), channel_id=1, source_target_pairs={{0,2},{1,5},{2,0},{3,7},{4,6},{5,1},{6,4},{7,3},{8,10},{9,13},{10,... | collective-permute-start | bytes 417800 | tf_op jit(solution)/shard_map/ppermute | solution.py:67
  63.2 11.2 %collective-permute-start.20 = (bf16[256,5248]{1,0:T(8,128)(2,1)S(1)}, bf16[256,5248]{1,0:T(8,128)(2,1)S(1)}, u32[]{:S(2)}, u32[]{:S(2)}) collective-permute-start(bf16[256,5248]{1,0:T(8,128)(2,1)S(1)} %get-tuple-element.79.refs_2_), channel_id=1, source_target_pairs={{0,1},{1,0},{2,3},{3,2},{4,5},{5,4},{6,7},{7,6},{8,9},{9,8},{10,11... | collective-permute-start | bytes 8060936 | tf_op jit(solution)/shard_map/ppermute | solution.py:67
  63.7 9.0 %collective-permute-start.17 = (bf16[32,2176]{1,0:T(8,128)(2,1)S(1)}, bf16[32,2176]{1,0:T(8,128)(2,1)S(1)}, u32[]{:S(2)}, u32[]{:S(2)}) collective-permute-start(bf16[32,2176]{1,0:T(8,128)(2,1)S(1)} %add_convert_fusion.4), channel_id=1, source_target_pairs={{0,4},{1,3},{2,6},{3,1},{4,0},{5,7},{6,2},{7,5},{8,12},{9,11},{10,... | collective-permute-start | bytes 417800 | tf_op jit(solution)/shard_map/ppermute | solution.py:67
  64.8 8.0 %collective-permute-start.19 = (bf16[64,2176]{1,0:T(8,128)(2,1)S(1)}, bf16[64,2176]{1,0:T(8,128)(2,1)S(1)}, u32[]{:S(2)}, u32[]{:S(2)}) collective-permute-start(bf16[64,2176]{1,0:T(8,128)(2,1)S(1)} %get-tuple-element.77), channel_id=1, source_target_pairs={{0,2},{1,5},{2,0},{3,7},{4,6},{5,1},{6,4},{7,3},{8,10},{9,13},{10,... | collective-permute-start | bytes 835592 | tf_op jit(solution)/shard_map/ppermute | solution.py:67
  66.3 8.0 %collective-permute-start.18 = (bf16[64,2176]{1,0:T(8,128)(2,1)S(1)}, bf16[64,2176]{1,0:T(8,128)(2,1)S(1)}, u32[]{:S(2)}, u32[]{:S(2)}) collective-permute-start(bf16[64,2176]{1,0:T(8,128)(2,1)S(1)} %get-tuple-element.74), channel_id=1, source_target_pairs={{0,2},{1,5},{2,0},{3,7},{4,6},{5,1},{6,4},{7,3},{8,10},{9,13},{10,... | collective-permute-start | bytes 835592 | tf_op jit(solution)/shard_map/ppermute | solution.py:67
  77.9 9.4 %collective-permute-start.21 = (bf16[64,2176]{1,0:T(8,128)(2,1)S(1)}, bf16[64,2176]{1,0:T(8,128)(2,1)S(1)}, u32[]{:S(2)}, u32[]{:S(2)}) collective-permute-start(bf16[64,2176]{1,0:T(8,128)(2,1)S(1)} %add_convert_fusion.1), channel_id=1, source_target_pairs={{0,4},{1,3},{2,6},{3,1},{4,0},{5,7},{6,2},{7,5},{8,12},{9,11},{10,... | collective-permute-start | bytes 835592 | tf_op jit(solution)/shard_map/ppermute | solution.py:67
  79.0 8.5 %collective-permute-start.25 = (bf16[128,5248]{1,0:T(8,128)(2,1)S(1)}, bf16[128,5248]{1,0:T(8,128)(2,1)S(1)}, u32[]{:S(2)}, u32[]{:S(2)}) collective-permute-start(bf16[128,5248]{1,0:T(8,128)(2,1)S(1)} %get-tuple-element.90.refs_4_), channel_id=1, source_target_pairs={{0,1},{1,0},{2,3},{3,2},{4,5},{5,4},{6,7},{7,6},{8,9},{9,8},{10,11... | collective-permute-start | bytes 4030472 | tf_op jit(solution)/shard_map/ppermute | solution.py:67
  87.5 15.5 %collective-permute-start.26 = (bf16[32,2176]{1,0:T(8,128)(2,1)S(1)}, bf16[32,2176]{1,0:T(8,128)(2,1)S(1)}, u32[]{:S(2)}, u32[]{:S(2)}) collective-permute-start(bf16[32,2176]{1,0:T(8,128)(2,1)S(1)} %get-tuple-element.91), channel_id=1, source_target_pairs={{0,24},{1,9},{2,26},{3,11},{4,28},{5,13},{6,30},{7,15},{8,0},{9,17... | collective-permute-start | bytes 417800 | tf_op jit(solution)/shard_map/ppermute | solution.py:67
  89.2 13.8 %collective-permute-start.27 = (bf16[32,2176]{1,0:T(8,128)(2,1)S(1)}, bf16[32,2176]{1,0:T(8,128)(2,1)S(1)}, u32[]{:S(2)}, u32[]{:S(2)}) collective-permute-start(bf16[32,2176]{1,0:T(8,128)(2,1)S(1)} %get-tuple-element.92), channel_id=1, source_target_pairs={{0,8},{1,25},{2,10},{3,27},{4,12},{5,29},{6,14},{7,31},{8,16},{9,1... | collective-permute-start | bytes 417800 | tf_op jit(solution)/shard_map/ppermute | solution.py:67
  89.5 13.4 %collective-permute-start.28 = (bf16[32,2176]{1,0:T(8,128)(2,1)S(1)}, bf16[32,2176]{1,0:T(8,128)(2,1)S(1)}, u32[]{:S(2)}, u32[]{:S(2)}) collective-permute-start(bf16[32,2176]{1,0:T(8,128)(2,1)S(1)} %add_convert_fusion.2), channel_id=1, source_target_pairs={{0,16},{1,17},{2,18},{3,19},{4,20},{5,21},{6,22},{7,23},{8,24},{9,... | collective-permute-start | bytes 417800 | tf_op jit(solution)/shard_map/ppermute | solution.py:67
  (17 other events, 73.3 us)

commit v4 on v3

--- a/solution.py
+++ b/solution.py
@@ -155,7 +155,7 @@
         in_specs=[pl.BlockSpec(memory_space=pltpu.SMEM)] + [whole] * (len(arrays) + 4),
         out_specs=[whole] * len(out_shape),
         scratch_shapes=[pltpu.VMEM((total, 2 * half), F32)],
-        compiler_params=pltpu.CompilerParams(vmem_limit_bytes=16 * MIB),
+        compiler_params=pltpu.CompilerParams(vmem_limit_bytes=10 * MIB),
         cost_estimate=pl.CostEstimate(
             flops=total * width, bytes_accessed=total * width, transcendentals=0
         ),
@@ -244,7 +244,7 @@
             pltpu.VMEM((2, 2, total, tile), BF16),
             pltpu.SemaphoreType.DMA((2, 2, groups)),
         ],
-        compiler_params=pltpu.CompilerParams(vmem_limit_bytes=(28 if total <= 1024 else 48) * MIB),
+        compiler_params=pltpu.CompilerParams(vmem_limit_bytes=(22 if total <= 1024 else 48) * MIB),
         cost_estimate=pl.CostEstimate(
             flops=2 * 3 * total * width * half,
             bytes_accessed=4 * total * width + 6 * width * half,
@@ -273,10 +273,12 @@
     onward, backward = level_route(count, 1), level_route(count, -1)
     both = jnp.concatenate([w_gate, w_up], axis=1)
     weights = [both, w_down, send(both, swap)]
+    weights.append(send(w_down, swap))
     last = levels // 2
+    groups = [(at, -at) if 0 < 2 * at < levels else (at,) for at in range(last + 1)]
 
     ways = {1: (home, None), -1: (home, None)}
-    units, results, planes, arrived, rows, terms = [], [], {}, [], [], []
+    units, results, planes, arrived, far, rows, terms = [], [], {}, [], [], [], []
     done = ()
     for step in range(last + 4):
         ready, done, sent = done, [], ()
@@ -311,29 +313,39 @@
                     else:
                         new[way] = (None, got)
             sent = (mine,)
-            near, beside = pass_on(mine, first), pass_on(mine, second)
+            beside = pass_on(mine, second)
+            near = pass_on(mine if step else after(home, beside, *weights[2:]), first)
             if step == 0:
                 across = send(beside, first)
                 done.append(across)
                 corners = [(across, 0, tok_count)]
                 new = {way: (new[way][0], across) for way in new}
-            if step == 1:
-                weights.append(send(after(w_down, *ready), swap))
-            units.append([[(block, 0, block.shape[0])] for block in (mine, near, beside)] + [corners])
+            own_blocks = [(ways[way][0], 0, tok_count) for way in here] or [(home, 0, tok_count)]
+            units.append([own_blocks] + [[(block, 0, block.shape[0])] for block in (near, beside)] + [corners])
             ways = new
-        if 1 <= step - 2 <= last:
+        if 1 <= step - 3 <= last:
             at = step - 3
-            beside_back = pass_on(add(results[at][2], across_back), second)
-            planes[at] = [results[at][0], near_back, beside_back]
+            plane = sum(part.astype(F32) for part in planes[at]).astype(BF16)
+            for i, shift in enumerate(groups[at]):
+                piece = plane[i * tok_count : (i + 1) * tok_count]
+                arrived.append(pass_on(piece, level_route(count, -shift)))
         if 0 <= step - 2 <= last:
             at = step - 2
-            if at < last:
-                across_back, near_back = pass_on(results[at][3], first), pass_on(results[at][1], first)
-            else:
-                pieces = [pass_on(part, pairs) for part, pairs in zip(results[at][1:], (first, second, corner))]
-                planes[at] = [results[at][0], *pieces]
-            pass_on(rows[2 * at], swap)
-            rows[2 * at + 1] = terms[2 * at + 1] = done[-1]
+            parts = results[at]
+            planes[at] = [parts[0], pass_on(parts[1], first)]
+            if at:
+                planes[at].append(pass_on(parts[2], second))
+            if at == last:
+                planes[at].append(pass_on(parts[3], corner))
+            elif at:
+                for i, shift in enumerate(groups[at]):
+                    piece = parts[3][i * tok_count : (i + 1) * tok_count]
+                    far.append(pass_on(piece, level_route(count, -shift)))
+        if step == last + 3:
+            relayed = pass_on(sum(part.astype(F32) for part in (results[0][3], *far)).astype(BF16), first)
+            arrived += [*planes[0], send(add(results[0][2], relayed), second)]
+        if 3 <= step:
+            rows[2 * step - 5] = terms[2 * step - 5] = send(rows[2 * step - 6], swap)
         if 0 <= step - 1 <= last:
             unit = units[step - 1]
             block, *span = unit[0][0]
@@ -343,17 +355,6 @@
             results.append(parts)
             rows += [kept, None]
             terms += [own, None]
-        back_home = [at for at in planes if planes[at] and (at < last - 1 or step == last + 3)]
-        if step >= 3:
-            for at in back_home:
-                plane = sum(piece.astype(F32) for piece in planes[at]).astype(BF16)
-                planes[at] = None
-                if at == 0:
-                    arrived.append(plane)
-                else:
-                    arrived.append(pass_on(plane[:tok_count], level_route(count, -at)))
-                if plane.shape[0] > tok_count:
-                    arrived.append(pass_on(plane[tok_count:], level_route(count, at)))
 
     grads = weight_grads(rows, terms, width, half)
     arrived[-1] = after(arrived[-1], *grads)

time: 105 us -> 99.6 us (0.949)
  waiting for transfers between devices: 28.6 us -> 17 us
  starting transfers between devices: 32.3 us -> 38.6 us
    ppermute x29 -> x30, waiting for transfers between devices: 28.6 us -> 17 us  [send(): return lax.ppermute(block, 'expert', pairs)]
    ppermute x29 -> x30, starting transfers between devices: 32.3 us -> 38.6 us  [send(): return lax.ppermute(block, 'expert', pairs)]
    pallas_call x3, Pallas kernels: 19.6 us -> 21.5 us  [expert_terms(): pl.pallas_call(functools.partial(terms_body, spans, len(arrays), width, h...]
    unnamed x27 -> x41, local copies, waits for them, and re-layouts: 9.93 us -> 9.01 us
  transfers between devices with their start and end apart: 29 -> 30, of which waited for: 12 -> 9; matrix products, arithmetic and copies ran while one was open for 3% -> 2% of each run, Pallas kernels for 28% -> 30%
where the time goes in v4:
time: 99.6 us; the launch traced here: 99.3 us
  starting transfers between devices  38.6 us (39%)
  Pallas kernels  30 us (30%)
  waiting for transfers between devices  17 us (17%)
  local copies, waits for them, and re-layouts  10.5 us (11%)
  other arithmetic  2.31 us (2%)
    ppermute x30, starting transfers between devices, send(): return lax.ppermute(block, 'expert', pairs)  38.6 us
    pallas_call x3, Pallas kernels, expert_terms(): pl.pallas_call(functools.partial(terms_body, spans, len(arrays), width, h...  21.5 us
    ppermute x30, waiting for transfers between devices, send(): return lax.ppermute(block, 'expert', pairs)  17 us
    unnamed x41, local copies, waits for them, and re-layouts  9.01 us
    pallas_call x1, Pallas kernels, weight_grads(): pl.pallas_call(functools.partial(grads_body, groups, width, half), grid=(...  7.53 us
  transfers between devices with their start and end apart: 30, of which 9 were waited for; matrix products, arithmetic and copies ran while one was open for 2% of the time, Pallas kernels for 30%

profile of v4, /device:TPU:0, one launch (start us, length us, event | category | flops | bytes accessed | tf_op | source)
XLA Modules:
  0.0 99.3 jit_solution(16157417506784207569)
XLA Ops:
  0.6 1.7 %constant_dynamic-update-slice_fusion.1 = bf16[2048,768]{1,0:T(8,128)(2,1)S(1)} fusion(bf16[2048,384]{1,0:T(8,128)(2,1)} %param.11), kind=kLoop, calls=%fused_computation.11 | loop fusion | bytes 3145728
  4.2 2.9 %collective-permute-start.2 = (bf16[32,4224]{1,0:T(8,128)(2,1)S(1)}, bf16[32,4224]{1,0:T(8,128)(2,1)S(1)}, u32[]{:S(2)}, u32[]{:S(2)}) collective-permute-start(bf16[32,4224]{1,0:T(8,128)(2,1)S(1)} %pad_maximum_fusion.refs_0_), channel_id=1, source_target_pairs={{0,4},{1,3},{2,6},{3,1},{4,0},{5,7},{6,2},{7,5},{8,12},{9,11},{10,... | collective-permute-start | bytes 811016 | tf_op jit(solution)/shard_map/ppermute | solution.py:67
  7.2 1.6 %collective-permute-start = (bf16[32,4224]{1,0:T(8,128)(2,1)S(1)}, bf16[32,4224]{1,0:T(8,128)(2,1)S(1)}, u32[]{:S(2)}, u32[]{:S(2)}) collective-permute-start(bf16[32,4224]{1,0:T(8,128)(2,1)S(1)} %pad_maximum_fusion.refs_0_), channel_id=1, source_target_pairs={{0,8},{1,25},{2,10},{3,27},{4,12},{5,29},{6,14},{7,31},{8,16},{9,1... | collective-permute-start | bytes 811016 | tf_op jit(solution)/shard_map/ppermute | solution.py:67
  8.7 2.2 %collective-permute-start.1 = (bf16[32,4224]{1,0:T(8,128)(2,1)S(1)}, bf16[32,4224]{1,0:T(8,128)(2,1)S(1)}, u32[]{:S(2)}, u32[]{:S(2)}) collective-permute-start(bf16[32,4224]{1,0:T(8,128)(2,1)S(1)} %pad_maximum_fusion.refs_0_), channel_id=1, source_target_pairs={{0,24},{1,9},{2,26},{3,11},{4,28},{5,13},{6,30},{7,15},{8,0},{9,17... | collective-permute-start | bytes 811016 | tf_op jit(solution)/shard_map/ppermute | solution.py:67
  11.6 2.0 %collective-permute-start.3 = (bf16[32,4224]{1,0:T(8,128)(2,1)S(1)}, bf16[32,4224]{1,0:T(8,128)(2,1)S(1)}, u32[]{:S(2)}, u32[]{:S(2)}) collective-permute-start(bf16[32,4224]{1,0:T(8,128)(2,1)S(1)} %collective-permute-done.2.refs_2_), channel_id=1, source_target_pairs={{0,2},{1,5},{2,0},{3,7},{4,6},{5,1},{6,4},{7,3},{8,10},{9,13},{10,... | collective-permute-start | bytes 811016 | tf_op jit(solution)/shard_map/ppermute | solution.py:67
  15.0 3.4 %collective-permute-done.refs_0_.refs_2_ = bf16[32,4224]{1,0:T(8,128)(2,1)S(1)} collective-permute-done((bf16[32,4224]{1,0:T(8,128)(2,1)S(1)}, bf16[32,4224]{1,0:T(8,128)(2,1)S(1)}, u32[]{:S(2)}, u32[]{:S(2)}) %collective-permute-start) | collective-permute-done | bytes 270368 | tf_op jit(solution)/shard_map/ppermute | solution.py:67
  18.4 2.2 %collective-permute-done.1.refs_1_ = bf16[32,4224]{1,0:T(8,128)(2,1)S(1)} collective-permute-done((bf16[32,4224]{1,0:T(8,128)(2,1)S(1)}, bf16[32,4224]{1,0:T(8,128)(2,1)S(1)}, u32[]{:S(2)}, u32[]{:S(2)}) %collective-permute-start.1) | collective-permute-done | bytes 270368 | tf_op jit(solution)/shard_map/ppermute | solution.py:67
  22.3 2.0 %collective-permute-start.7 = (bf16[64,4224]{1,0:T(8,128)(2,1)}, bf16[64,4224]{1,0:T(8,128)(2,1)}, u32[]{:S(2)}, u32[]{:S(2)}) collective-permute-start(bf16[64,4224]{1,0:T(8,128)(2,1)} %get-tuple-element.52), channel_id=1, source_target_pairs={{0,8},{1,25},{2,10},{3,27},{4,12},{5,29},{6,14},{7,31},{8,16},{9,1... | collective-permute-start | bytes 1622024 | tf_op jit(solution)/shard_map/ppermute | solution.py:67
  25.4 1.4 %collective-permute-start.10 = (bf16[64,4224]{1,0:T(8,128)(2,1)}, bf16[64,4224]{1,0:T(8,128)(2,1)S(1)}, u32[]{:S(2)}, u32[]{:S(2)}) collective-permute-start(bf16[64,4224]{1,0:T(8,128)(2,1)} %copy-done.10), channel_id=1, source_target_pairs={{0,2},{1,5},{2,0},{3,7},{4,6},{5,1},{6,4},{7,3},{8,10},{9,13},{10,... | collective-permute-start | bytes 1622024 | tf_op jit(solution)/shard_map/ppermute | solution.py:67
  26.8 2.2 %collective-permute-start.8 = (bf16[32,4224]{1,0:T(8,128)(2,1)}, bf16[32,4224]{1,0:T(8,128)(2,1)S(1)}, u32[]{:S(2)}, u32[]{:S(2)}) collective-permute-start(bf16[32,4224]{1,0:T(8,128)(2,1)} %copy-done.4), channel_id=1, source_target_pairs={{0,24},{1,9},{2,26},{3,11},{4,28},{5,13},{6,30},{7,15},{8,0},{9,17... | collective-permute-start | bytes 811016 | tf_op jit(solution)/shard_map/ppermute | solution.py:67
  32.8 6.9 %expert_terms.3 = (bf16[32,2176]{1,0:T(8,128)(2,1)S(1)}, bf16[32,2176]{1,0:T(8,128)(2,1)S(1)}, bf16[32,2176]{1,0:T(8,128)(2,1)S(1)}, bf16[32,2176]{1,0:T(8,128)(...) custom-call(s32[1]{0:T(128)} %bitcast.expert_ref, bf16[32,4224]{1,0:T(8,128)(2,1)S(1)} %copy-done.1, ...), custom_call_target="tpu_custom_call" | custom-call | flops 262144 | bytes 262144 | tf_op jit(solution)/shard_map/expert_terms/pallas_call | solution.py:152
  41.4 2.5 %collective-permute-done.8.refs_5_ = bf16[32,4224]{1,0:T(8,128)(2,1)S(1)} collective-permute-done((bf16[32,4224]{1,0:T(8,128)(2,1)}, bf16[32,4224]{1,0:T(8,128)(2,1)S(1)}, u32[]{:S(2)}, u32[]{:S(2)}) %collective-permute-start.8) | collective-permute-done | bytes 270368 | tf_op jit(solution)/shard_map/ppermute | solution.py:67
  45.1 2.5 %collective-permute-start.12 = (bf16[32,4224]{1,0:T(8,128)(2,1)S(1)}, bf16[32,4224]{1,0:T(8,128)(2,1)S(1)}, u32[]{:S(2)}, u32[]{:S(2)}) collective-permute-start(bf16[32,4224]{1,0:T(8,128)(2,1)S(1)} %get-tuple-element.71.refs_0_), channel_id=1, source_target_pairs={{0,4},{1,3},{2,6},{3,1},{4,0},{5,7},{6,2},{7,5},{8,12},{9,11},{10,... | collective-permute-start | bytes 811016 | tf_op jit(solution)/shard_map/ppermute | solution.py:67
  47.6 2.0 %collective-permute-start.14 = (bf16[32,2176]{1,0:T(8,128)(2,1)S(1)}, bf16[32,2176]{1,0:T(8,128)(2,1)S(1)}, u32[]{:S(2)}, u32[]{:S(2)}) collective-permute-start(bf16[32,2176]{1,0:T(8,128)(2,1)S(1)} %get-tuple-element.64), channel_id=1, source_target_pairs={{0,2},{1,5},{2,0},{3,7},{4,6},{5,1},{6,4},{7,3},{8,10},{9,13},{10,... | collective-permute-start | bytes 417800 | tf_op jit(solution)/shard_map/ppermute | solution.py:67
  49.7 7.8 %expert_terms.4 = (bf16[64,2176]{1,0:T(8,128)(2,1)S(1)}, bf16[64,2176]{1,0:T(8,128)(2,1)S(1)}, bf16[64,2176]{1,0:T(8,128)(2,1)S(1)}, bf16[64,2176]{1,0:T(8,128)(...) custom-call(s32[1]{0:T(128)} %bitcast.expert_ref, ...), custom_call_target="tpu_custom_call" | custom-call | flops 524288 | bytes 524288 | tf_op jit(solution)/shard_map/expert_terms/pallas_call | solution.py:152
  58.9 3.0 %collective-permute-start.17 = (bf16[32,2176]{1,0:T(8,128)(2,1)S(1)}, bf16[32,2176]{1,0:T(8,128)(2,1)S(1)}, u32[]{:S(2)}, u32[]{:S(2)}) collective-permute-start(bf16[32,2176]{1,0:T(8,128)(2,1)S(1)} %get-tuple-element.69), channel_id=1, source_target_pairs={{0,24},{1,9},{2,26},{3,11},{4,28},{5,13},{6,30},{7,15},{8,0},{9,17... | collective-permute-start | bytes 417800 | tf_op jit(solution)/shard_map/ppermute | solution.py:67
  61.8 6.8 %expert_terms.5 = (bf16[32,2176]{1,0:T(8,128)(2,1)S(1)}, bf16[32,2176]{1,0:T(8,128)(2,1)S(1)}, bf16[32,2176]{1,0:T(8,128)(2,1)S(1)}, bf16[32,2176]{1,0:T(8,128)(...) custom-call(s32[1]{0:T(128)} %bitcast.expert_ref, ...), custom_call_target="tpu_custom_call" | custom-call | flops 262144 | bytes 262144 | tf_op jit(solution)/shard_map/expert_terms/pallas_call | solution.py:152
  68.7 2.3 %collective-permute-start.23 = (bf16[32,2176]{1,0:T(8,128)(2,1)S(1)}, bf16[32,2176]{1,0:T(8,128)(2,1)S(1)}, u32[]{:S(2)}, u32[]{:S(2)}) collective-permute-start(bf16[32,2176]{1,0:T(8,128)(2,1)S(1)} %get-tuple-element.80), channel_id=1, source_target_pairs={{0,6},{1,7},{2,4},{3,5},{4,2},{5,3},{6,0},{7,1},{8,14},{9,15},{10,... | collective-permute-start | bytes 417800 | tf_op jit(solution)/shard_map/ppermute | solution.py:67
  72.4 3.9 %collective-permute-start.19 = (bf16[32,2176]{1,0:T(8,128)(2,1)S(1)}, bf16[32,2176]{1,0:T(8,128)(2,1)S(1)}, u32[]{:S(2)}, u32[]{:S(2)}) collective-permute-start(bf16[32,2176]{1,0:T(8,128)(2,1)S(1)} %get-tuple-element.73), channel_id=1, source_target_pairs={{0,24},{1,9},{2,26},{3,11},{4,28},{5,13},{6,30},{7,15},{8,0},{9,17... | collective-permute-start | bytes 417800 | tf_op jit(solution)/shard_map/ppermute | solution.py:67
  79.5 3.7 %collective-permute-done.20 = bf16[32,2176]{1,0:T(8,128)(2,1)S(1)} collective-permute-done((bf16[32,2176]{1,0:T(8,128)(2,1)S(1)}, bf16[32,2176]{1,0:T(8,128)(2,1)S(1)}, u32[]{:S(2)}, u32[]{:S(2)}) %collective-permute-start.20) | collective-permute-done | bytes 139296 | tf_op jit(solution)/shard_map/ppermute | solution.py:67
  84.1 1.5 %collective-permute-start.24 = (bf16[32,2176]{1,0:T(8,128)(2,1)S(1)}, bf16[32,2176]{1,0:T(8,128)(2,1)S(1)}, u32[]{:S(2)}, u32[]{:S(2)}) collective-permute-start(bf16[32,2176]{1,0:T(8,128)(2,1)S(1)} %add_convert_fusion.3), channel_id=1, source_target_pairs={{0,16},{1,17},{2,18},{3,19},{4,20},{5,21},{6,22},{7,23},{8,24},{9,... | collective-permute-start | bytes 417800 | tf_op jit(solution)/shard_map/ppermute | solution.py:67
  85.7 2.6 %collective-permute-done.25 = bf16[32,2176]{1,0:T(8,128)(2,1)S(1)} collective-permute-done((bf16[32,2176]{1,0:T(8,128)(2,1)S(1)}, bf16[32,2176]{1,0:T(8,128)(2,1)S(1)}, u32[]{:S(2)}, u32[]{:S(2)}) %collective-permute-start.25) | collective-permute-done | bytes 139296 | tf_op jit(solution)/shard_map/ppermute | solution.py:67
  89.2 7.5 %weight_grads.1 = (bf16[2048,384]{1,0:T(8,128)(2,1)}, bf16[2048,384]{1,0:T(8,128)(2,1)}, bf16[384,2048]{1,0:T(8,128)(2,1)}) custom-call(bf16[128,5248]{1,0:T(8,128)(2,1)S(1)} %get-tuple-element.85.refs_0_, bf16[128,5248]{1,0:T(8,128)(2,1)S(1)} %collective-permute-done.27.refs_1_.refs_7_, bf16[256,5248]{1,0:T(8,128)(2,1)S(1)} %get-tuple-element.86.refs_2_, ...), custom_call_target="tpu_custom_call" | custom-call | flops 4831838208 | bytes 13107200 | tf_op jit(solution)/shard_map/weight_grads/pallas_call | solution.py:235
  97.7 1.7 %add_convert_fusion.4 = bf16[32,2048]{1,0:T(8,128)(2,1)} fusion(bf16[32,2176]{1,0:T(8,128)(2,1)} %copy-done.14, bf16[32,2176]{1,0:T(8,128)(2,1)S(1)} %collective-permute-done.24, bf16[32,2176]{1,0:T(8,128)(2,1)S(1)} %collective-permute-done.20, bf16[32,2176]{1,0:T(8,128)(2,1)S(1)} %collective-permute-done.19, ...), kind=kLoop, calls=%fused_computation.5 | loop fusion | flops 786432 | bytes 917504 | tf_op jit(solution)/shard_map/convert_element_type | solution.py:362
  (96 shorter events, 22.1 us)
Async XLA Ops:
  2.8 11.5 %collective-permute-start.4 = (bf16[2048,768]{1,0:T(8,128)(2,1)S(1)}, bf16[2048,768]{1,0:T(8,128)(2,1)}, u32[]{:S(2)}, u32[]{:S(2)}) collective-permute-start(bf16[2048,768]{1,0:T(8,128)(2,1)S(1)} %constant_dynamic-update-slice_fusion.refs_4_.refs_6_), channel_id=1, source_target_pairs={{0,1},{1,0},{2,3},{3,2},{4,5},{5,4},{6,7},{7,6},{8,9},{9,8},{10,11... | collective-permute-start | bytes 9437192 | tf_op jit(solution)/shard_map/ppermute | solution.py:67
  3.4 10.9 %collective-permute-start.5 = (bf16[384,2048]{1,0:T(8,128)(2,1)}, bf16[384,2048]{1,0:T(8,128)(2,1)}, u32[]{:S(2)}, u32[]{:S(2)}) collective-permute-start(bf16[384,2048]{1,0:T(8,128)(2,1)} %refs_5_.3), channel_id=1, source_target_pairs={{0,1},{1,0},{2,3},{3,2},{4,5},{5,4},{6,7},{7,6},{8,9},{9,8},{10,11... | collective-permute-start | bytes 4718600 | tf_op jit(solution)/shard_map/ppermute | solution.py:67
  7.2 11.3 %collective-permute-start = (bf16[32,4224]{1,0:T(8,128)(2,1)S(1)}, bf16[32,4224]{1,0:T(8,128)(2,1)S(1)}, u32[]{:S(2)}, u32[]{:S(2)}) collective-permute-start(bf16[32,4224]{1,0:T(8,128)(2,1)S(1)} %pad_maximum_fusion.refs_0_), channel_id=1, source_target_pairs={{0,8},{1,25},{2,10},{3,27},{4,12},{5,29},{6,14},{7,31},{8,16},{9,1... | collective-permute-start | bytes 811016 | tf_op jit(solution)/shard_map/ppermute | solution.py:67
  8.7 11.9 %collective-permute-start.1 = (bf16[32,4224]{1,0:T(8,128)(2,1)S(1)}, bf16[32,4224]{1,0:T(8,128)(2,1)S(1)}, u32[]{:S(2)}, u32[]{:S(2)}) collective-permute-start(bf16[32,4224]{1,0:T(8,128)(2,1)S(1)} %pad_maximum_fusion.refs_0_), channel_id=1, source_target_pairs={{0,24},{1,9},{2,26},{3,11},{4,28},{5,13},{6,30},{7,15},{8,0},{9,17... | collective-permute-start | bytes 811016 | tf_op jit(solution)/shard_map/ppermute | solution.py:67
  11.6 9.0 %collective-permute-start.3 = (bf16[32,4224]{1,0:T(8,128)(2,1)S(1)}, bf16[32,4224]{1,0:T(8,128)(2,1)S(1)}, u32[]{:S(2)}, u32[]{:S(2)}) collective-permute-start(bf16[32,4224]{1,0:T(8,128)(2,1)S(1)} %collective-permute-done.2.refs_2_), channel_id=1, source_target_pairs={{0,2},{1,5},{2,0},{3,7},{4,6},{5,1},{6,4},{7,3},{8,10},{9,13},{10,... | collective-permute-start | bytes 811016 | tf_op jit(solution)/shard_map/ppermute | solution.py:67
  22.3 18.0 %collective-permute-start.7 = (bf16[64,4224]{1,0:T(8,128)(2,1)}, bf16[64,4224]{1,0:T(8,128)(2,1)}, u32[]{:S(2)}, u32[]{:S(2)}) collective-permute-start(bf16[64,4224]{1,0:T(8,128)(2,1)} %get-tuple-element.52), channel_id=1, source_target_pairs={{0,8},{1,25},{2,10},{3,27},{4,12},{5,29},{6,14},{7,31},{8,16},{9,1... | collective-permute-start | bytes 1622024 | tf_op jit(solution)/shard_map/ppermute | solution.py:67
  24.4 19.5 %collective-permute-start.9 = (bf16[64,4224]{1,0:T(8,128)(2,1)}, bf16[64,4224]{1,0:T(8,128)(2,1)S(1)}, u32[]{:S(2)}, u32[]{:S(2)}) collective-permute-start(bf16[64,4224]{1,0:T(8,128)(2,1)} %copy-done.10), channel_id=1, source_target_pairs={{0,4},{1,3},{2,6},{3,1},{4,0},{5,7},{6,2},{7,5},{8,12},{9,11},{10,... | collective-permute-start | bytes 1622024 | tf_op jit(solution)/shard_map/ppermute | solution.py:67
  25.4 18.5 %collective-permute-start.10 = (bf16[64,4224]{1,0:T(8,128)(2,1)}, bf16[64,4224]{1,0:T(8,128)(2,1)S(1)}, u32[]{:S(2)}, u32[]{:S(2)}) collective-permute-start(bf16[64,4224]{1,0:T(8,128)(2,1)} %copy-done.10), channel_id=1, source_target_pairs={{0,2},{1,5},{2,0},{3,7},{4,6},{5,1},{6,4},{7,3},{8,10},{9,13},{10,... | collective-permute-start | bytes 1622024 | tf_op jit(solution)/shard_map/ppermute | solution.py:67
  26.8 17.1 %collective-permute-start.8 = (bf16[32,4224]{1,0:T(8,128)(2,1)}, bf16[32,4224]{1,0:T(8,128)(2,1)S(1)}, u32[]{:S(2)}, u32[]{:S(2)}) collective-permute-start(bf16[32,4224]{1,0:T(8,128)(2,1)} %copy-done.4), channel_id=1, source_target_pairs={{0,24},{1,9},{2,26},{3,11},{4,28},{5,13},{6,30},{7,15},{8,0},{9,17... | collective-permute-start | bytes 811016 | tf_op jit(solution)/shard_map/ppermute | solution.py:67
  43.9 13.6 %collective-permute-start.11 = (bf16[32,4224]{1,0:T(8,128)(2,1)S(1)}, bf16[32,4224]{1,0:T(8,128)(2,1)S(1)}, u32[]{:S(2)}, u32[]{:S(2)}) collective-permute-start(bf16[32,4224]{1,0:T(8,128)(2,1)S(1)} %get-tuple-element.61), channel_id=1, source_target_pairs={{0,8},{1,25},{2,10},{3,27},{4,12},{5,29},{6,14},{7,31},{8,16},{9,1... | collective-permute-start | bytes 811016 | tf_op jit(solution)/shard_map/ppermute | solution.py:67
  45.1 12.4 %collective-permute-start.12 = (bf16[32,4224]{1,0:T(8,128)(2,1)S(1)}, bf16[32,4224]{1,0:T(8,128)(2,1)S(1)}, u32[]{:S(2)}, u32[]{:S(2)}) collective-permute-start(bf16[32,4224]{1,0:T(8,128)(2,1)S(1)} %get-tuple-element.71.refs_0_), channel_id=1, source_target_pairs={{0,4},{1,3},{2,6},{3,1},{4,0},{5,7},{6,2},{7,5},{8,12},{9,11},{10,... | collective-permute-start | bytes 811016 | tf_op jit(solution)/shard_map/ppermute | solution.py:67
  47.6 9.9 %collective-permute-start.13 = (bf16[32,4224]{1,0:T(8,128)(2,1)S(1)}, bf16[32,4224]{1,0:T(8,128)(2,1)S(1)}, u32[]{:S(2)}, u32[]{:S(2)}) collective-permute-start(bf16[32,4224]{1,0:T(8,128)(2,1)S(1)} %get-tuple-element.71.refs_0_), channel_id=1, source_target_pairs={{0,2},{1,5},{2,0},{3,7},{4,6},{5,1},{6,4},{7,3},{8,10},{9,13},{10,... | collective-permute-start | bytes 811016 | tf_op jit(solution)/shard_map/ppermute | solution.py:67
  47.6 9.9 %collective-permute-start.14 = (bf16[32,2176]{1,0:T(8,128)(2,1)S(1)}, bf16[32,2176]{1,0:T(8,128)(2,1)S(1)}, u32[]{:S(2)}, u32[]{:S(2)}) collective-permute-start(bf16[32,2176]{1,0:T(8,128)(2,1)S(1)} %get-tuple-element.64), channel_id=1, source_target_pairs={{0,2},{1,5},{2,0},{3,7},{4,6},{5,1},{6,4},{7,3},{8,10},{9,13},{10,... | collective-permute-start | bytes 417800 | tf_op jit(solution)/shard_map/ppermute | solution.py:67
  57.5 11.2 %collective-permute-start.15 = (bf16[64,2176]{1,0:T(8,128)(2,1)S(1)}, bf16[64,2176]{1,0:T(8,128)(2,1)S(1)}, u32[]{:S(2)}, u32[]{:S(2)}) collective-permute-start(bf16[64,2176]{1,0:T(8,128)(2,1)S(1)} %get-tuple-element.65), channel_id=1, source_target_pairs={{0,2},{1,5},{2,0},{3,7},{4,6},{5,1},{6,4},{7,3},{8,10},{9,13},{10,... | collective-permute-start | bytes 835592 | tf_op jit(solution)/shard_map/ppermute | solution.py:67
  57.6 11.1 %collective-permute-start.16 = (bf16[64,2176]{1,0:T(8,128)(2,1)S(1)}, bf16[64,2176]{1,0:T(8,128)(2,1)S(1)}, u32[]{:S(2)}, u32[]{:S(2)}) collective-permute-start(bf16[64,2176]{1,0:T(8,128)(2,1)S(1)} %get-tuple-element.67), channel_id=1, source_target_pairs={{0,4},{1,3},{2,6},{3,1},{4,0},{5,7},{6,2},{7,5},{8,12},{9,11},{10,... | collective-permute-start | bytes 835592 | tf_op jit(solution)/shard_map/ppermute | solution.py:67
  58.9 9.8 %collective-permute-start.17 = (bf16[32,2176]{1,0:T(8,128)(2,1)S(1)}, bf16[32,2176]{1,0:T(8,128)(2,1)S(1)}, u32[]{:S(2)}, u32[]{:S(2)}) collective-permute-start(bf16[32,2176]{1,0:T(8,128)(2,1)S(1)} %get-tuple-element.69), channel_id=1, source_target_pairs={{0,24},{1,9},{2,26},{3,11},{4,28},{5,13},{6,30},{7,15},{8,0},{9,17... | collective-permute-start | bytes 417800 | tf_op jit(solution)/shard_map/ppermute | solution.py:67
  61.8 27.4 %collective-permute-start.28 = (bf16[256,5248]{1,0:T(8,128)(2,1)S(1)}, bf16[256,5248]{1,0:T(8,128)(2,1)S(1)}, u32[]{:S(2)}, u32[]{:S(2)}) collective-permute-start(bf16[256,5248]{1,0:T(8,128)(2,1)S(1)} %get-tuple-element.86.refs_2_), channel_id=1, source_target_pairs={{0,1},{1,0},{2,3},{3,2},{4,5},{5,4},{6,7},{7,6},{8,9},{9,8},{10,11... | collective-permute-start | bytes 8060936 | tf_op jit(solution)/shard_map/ppermute | solution.py:67
  68.7 7.6 %collective-permute-start.23 = (bf16[32,2176]{1,0:T(8,128)(2,1)S(1)}, bf16[32,2176]{1,0:T(8,128)(2,1)S(1)}, u32[]{:S(2)}, u32[]{:S(2)}) collective-permute-start(bf16[32,2176]{1,0:T(8,128)(2,1)S(1)} %get-tuple-element.80), channel_id=1, source_target_pairs={{0,6},{1,7},{2,4},{3,5},{4,2},{5,3},{6,0},{7,1},{8,14},{9,15},{10,... | collective-permute-start | bytes 417800 | tf_op jit(solution)/shard_map/ppermute | solution.py:67
  71.0 7.7 %collective-permute-start.22 = (bf16[32,2176]{1,0:T(8,128)(2,1)S(1)}, bf16[32,2176]{1,0:T(8,128)(2,1)S(1)}, u32[]{:S(2)}, u32[]{:S(2)}) collective-permute-start(bf16[32,2176]{1,0:T(8,128)(2,1)S(1)} %get-tuple-element.78), channel_id=1, source_target_pairs={{0,4},{1,3},{2,6},{3,1},{4,0},{5,7},{6,2},{7,5},{8,12},{9,11},{10,... | collective-permute-start | bytes 417800 | tf_op jit(solution)/shard_map/ppermute | solution.py:67
  71.1 8.1 %collective-permute-start.21 = (bf16[32,2176]{1,0:T(8,128)(2,1)S(1)}, bf16[32,2176]{1,0:T(8,128)(2,1)S(1)}, u32[]{:S(2)}, u32[]{:S(2)}) collective-permute-start(bf16[32,2176]{1,0:T(8,128)(2,1)S(1)} %get-tuple-element.76), channel_id=1, source_target_pairs={{0,2},{1,5},{2,0},{3,7},{4,6},{5,1},{6,4},{7,3},{8,10},{9,13},{10,... | collective-permute-start | bytes 417800 | tf_op jit(solution)/shard_map/ppermute | solution.py:67
  78.8 10.4 %collective-permute-start.27 = (bf16[128,5248]{1,0:T(8,128)(2,1)S(1)}, bf16[128,5248]{1,0:T(8,128)(2,1)S(1)}, u32[]{:S(2)}, u32[]{:S(2)}) collective-permute-start(bf16[128,5248]{1,0:T(8,128)(2,1)S(1)} %get-tuple-element.85.refs_0_), channel_id=1, source_target_pairs={{0,1},{1,0},{2,3},{3,2},{4,5},{5,4},{6,7},{7,6},{8,9},{9,8},{10,11... | collective-permute-start | bytes 4030472 | tf_op jit(solution)/shard_map/ppermute | solution.py:67
  79.2 10.0 %collective-permute-start.29 = (bf16[128,5248]{1,0:T(8,128)(2,1)S(1)}, bf16[128,5248]{1,0:T(8,128)(2,1)S(1)}, u32[]{:S(2)}, u32[]{:S(2)}) collective-permute-start(bf16[128,5248]{1,0:T(8,128)(2,1)S(1)} %get-tuple-element.87.refs_4_), channel_id=1, source_target_pairs={{0,1},{1,0},{2,3},{3,2},{4,5},{5,4},{6,7},{7,6},{8,9},{9,8},{10,11... | collective-permute-start | bytes 4030472 | tf_op jit(solution)/shard_map/ppermute | solution.py:67
  84.1 12.6 %collective-permute-start.24 = (bf16[32,2176]{1,0:T(8,128)(2,1)S(1)}, bf16[32,2176]{1,0:T(8,128)(2,1)S(1)}, u32[]{:S(2)}, u32[]{:S(2)}) collective-permute-start(bf16[32,2176]{1,0:T(8,128)(2,1)S(1)} %add_convert_fusion.3), channel_id=1, source_target_pairs={{0,16},{1,17},{2,18},{3,19},{4,20},{5,21},{6,22},{7,23},{8,24},{9,... | collective-permute-start | bytes 417800 | tf_op jit(solution)/shard_map/ppermute | solution.py:67
  88.3 8.5 %collective-permute-start.26 = (bf16[32,2176]{1,0:T(8,128)(2,1)S(1)}, bf16[32,2176]{1,0:T(8,128)(2,1)S(1)}, u32[]{:S(2)}, u32[]{:S(2)}) collective-permute-start(bf16[32,2176]{1,0:T(8,128)(2,1)S(1)} %add_convert_fusion.1), channel_id=1, source_target_pairs={{0,4},{1,3},{2,6},{3,1},{4,0},{5,7},{6,2},{7,5},{8,12},{9,11},{10,... | collective-permute-start | bytes 417800 | tf_op jit(solution)/shard_map/ppermute | solution.py:67
  (25 other events, 122.6 us)

commit v5 on v4

--- a/solution.py
+++ b/solution.py
@@ -332,8 +332,9 @@
         if 0 <= step - 2 <= last:
             at = step - 2
             parts = results[at]
-            planes[at] = [parts[0], pass_on(parts[1], first)]
+            planes[at] = [parts[0]]
             if at:
+                planes[at].append(pass_on(parts[1], first))
                 planes[at].append(pass_on(parts[2], second))
             if at == last:
                 planes[at].append(pass_on(parts[3], corner))
@@ -342,10 +343,14 @@
                     piece = parts[3][i * tok_count : (i + 1) * tok_count]
                     far.append(pass_on(piece, level_route(count, -shift)))
         if step == last + 3:
-            relayed = pass_on(sum(part.astype(F32) for part in (results[0][3], *far)).astype(BF16), first)
-            arrived += [*planes[0], send(add(results[0][2], relayed), second)]
-        if 3 <= step:
-            rows[2 * step - 5] = terms[2 * step - 5] = send(rows[2 * step - 6], swap)
+            far = sum(part.astype(F32) for part in (results[0][3], *far)).astype(BF16)
+            arrived += [*planes[0], pass_on(results[0][1], first), pass_on(results[0][2], second), pass_on(far, corner)]
+        if last + 1 < step:
+            for at in range(last + 1) if step == last + 3 else ():
+                block = rows[2 * at]
+                if at in (0, last):
+                    block = after(block, *planes[last][1:2])
+                rows[2 * at + 1] = terms[2 * at + 1] = send(block, swap)
         if 0 <= step - 1 <= last:
             unit = units[step - 1]
             block, *span = unit[0][0]

time: 99.6 us -> 95 us (0.954)
  waiting for transfers between devices: 17 us -> 14.3 us
  starting transfers between devices: 38.6 us -> 37.3 us
    ppermute x30, waiting for transfers between devices: 17 us -> 14.3 us  [send(): return lax.ppermute(block, 'expert', pairs)]
    ppermute x30, starting transfers between devices: 38.6 us -> 37.3 us  [send(): return lax.ppermute(block, 'expert', pairs)]
    unnamed x41 -> x39, local copies, waits for them, and re-layouts: 9.01 us -> 9.02 us
  transfers between devices with their start and end apart: 30 -> 30, of which waited for: 9 -> 8; matrix products, arithmetic and copies ran while one was open for 2% -> 2% of each run, Pallas kernels for 30% -> 32%
where the time goes in v5:
time: 95 us; the launch traced here: 94.4 us
  starting transfers between devices  37.3 us (39%)
  Pallas kernels  30 us (32%)
  waiting for transfers between devices  14.3 us (15%)
  local copies, waits for them, and re-layouts  10.5 us (11%)
  other arithmetic  1.38 us (1%)
    ppermute x30, starting transfers between devices, send(): return lax.ppermute(block, 'expert', pairs)  37.3 us
    pallas_call x3, Pallas kernels, expert_terms(): pl.pallas_call(functools.partial(terms_body, spans, len(arrays), width, h...  21.5 us
    ppermute x30, waiting for transfers between devices, send(): return lax.ppermute(block, 'expert', pairs)  14.3 us
    unnamed x39, local copies, waits for them, and re-layouts  9.02 us
    pallas_call x1, Pallas kernels, weight_grads(): pl.pallas_call(functools.partial(grads_body, groups, width, half), grid=(...  7.47 us
  transfers between devices with their start and end apart: 30, of which 8 were waited for; matrix products, arithmetic and copies ran while one was open for 2% of the time, Pallas kernels for 32%

profile of v5, /device:TPU:0, one launch (start us, length us, event | category | flops | bytes accessed | tf_op | source)
XLA Modules:
  0.0 94.4 jit_solution(12442047341798503655)
XLA Ops:
  0.6 1.7 %constant_dynamic-update-slice_fusion.1 = bf16[2048,768]{1,0:T(8,128)(2,1)S(1)} fusion(bf16[2048,384]{1,0:T(8,128)(2,1)} %param.11), kind=kLoop, calls=%fused_computation.10 | loop fusion | bytes 3145728
  4.2 2.9 %collective-permute-start.2 = (bf16[32,4224]{1,0:T(8,128)(2,1)S(1)}, bf16[32,4224]{1,0:T(8,128)(2,1)S(1)}, u32[]{:S(2)}, u32[]{:S(2)}) collective-permute-start(bf16[32,4224]{1,0:T(8,128)(2,1)S(1)} %pad_maximum_fusion.refs_0_), channel_id=1, source_target_pairs={{0,4},{1,3},{2,6},{3,1},{4,0},{5,7},{6,2},{7,5},{8,12},{9,11},{10,... | collective-permute-start | bytes 811016 | tf_op jit(solution)/shard_map/ppermute | solution.py:67
  7.2 1.6 %collective-permute-start = (bf16[32,4224]{1,0:T(8,128)(2,1)S(1)}, bf16[32,4224]{1,0:T(8,128)(2,1)S(1)}, u32[]{:S(2)}, u32[]{:S(2)}) collective-permute-start(bf16[32,4224]{1,0:T(8,128)(2,1)S(1)} %pad_maximum_fusion.refs_0_), channel_id=1, source_target_pairs={{0,8},{1,25},{2,10},{3,27},{4,12},{5,29},{6,14},{7,31},{8,16},{9,1... | collective-permute-start | bytes 811016 | tf_op jit(solution)/shard_map/ppermute | solution.py:67
  8.7 2.2 %collective-permute-start.1 = (bf16[32,4224]{1,0:T(8,128)(2,1)S(1)}, bf16[32,4224]{1,0:T(8,128)(2,1)S(1)}, u32[]{:S(2)}, u32[]{:S(2)}) collective-permute-start(bf16[32,4224]{1,0:T(8,128)(2,1)S(1)} %pad_maximum_fusion.refs_0_), channel_id=1, source_target_pairs={{0,24},{1,9},{2,26},{3,11},{4,28},{5,13},{6,30},{7,15},{8,0},{9,17... | collective-permute-start | bytes 811016 | tf_op jit(solution)/shard_map/ppermute | solution.py:67
  11.6 2.0 %collective-permute-start.3 = (bf16[32,4224]{1,0:T(8,128)(2,1)S(1)}, bf16[32,4224]{1,0:T(8,128)(2,1)S(1)}, u32[]{:S(2)}, u32[]{:S(2)}) collective-permute-start(bf16[32,4224]{1,0:T(8,128)(2,1)S(1)} %collective-permute-done.2.refs_2_), channel_id=1, source_target_pairs={{0,2},{1,5},{2,0},{3,7},{4,6},{5,1},{6,4},{7,3},{8,10},{9,13},{10,... | collective-permute-start | bytes 811016 | tf_op jit(solution)/shard_map/ppermute | solution.py:67
  15.1 3.4 %collective-permute-done.refs_0_.refs_2_ = bf16[32,4224]{1,0:T(8,128)(2,1)S(1)} collective-permute-done((bf16[32,4224]{1,0:T(8,128)(2,1)S(1)}, bf16[32,4224]{1,0:T(8,128)(2,1)S(1)}, u32[]{:S(2)}, u32[]{:S(2)}) %collective-permute-start) | collective-permute-done | bytes 270368 | tf_op jit(solution)/shard_map/ppermute | solution.py:67
  18.4 2.2 %collective-permute-done.1.refs_1_ = bf16[32,4224]{1,0:T(8,128)(2,1)S(1)} collective-permute-done((bf16[32,4224]{1,0:T(8,128)(2,1)S(1)}, bf16[32,4224]{1,0:T(8,128)(2,1)S(1)}, u32[]{:S(2)}, u32[]{:S(2)}) %collective-permute-start.1) | collective-permute-done | bytes 270368 | tf_op jit(solution)/shard_map/ppermute | solution.py:67
  22.3 2.0 %collective-permute-start.7 = (bf16[64,4224]{1,0:T(8,128)(2,1)}, bf16[64,4224]{1,0:T(8,128)(2,1)}, u32[]{:S(2)}, u32[]{:S(2)}) collective-permute-start(bf16[64,4224]{1,0:T(8,128)(2,1)} %get-tuple-element.55), channel_id=1, source_target_pairs={{0,8},{1,25},{2,10},{3,27},{4,12},{5,29},{6,14},{7,31},{8,16},{9,1... | collective-permute-start | bytes 1622024 | tf_op jit(solution)/shard_map/ppermute | solution.py:67
  25.4 1.3 %collective-permute-start.10 = (bf16[64,4224]{1,0:T(8,128)(2,1)}, bf16[64,4224]{1,0:T(8,128)(2,1)S(1)}, u32[]{:S(2)}, u32[]{:S(2)}) collective-permute-start(bf16[64,4224]{1,0:T(8,128)(2,1)} %copy-done.10), channel_id=1, source_target_pairs={{0,2},{1,5},{2,0},{3,7},{4,6},{5,1},{6,4},{7,3},{8,10},{9,13},{10,... | collective-permute-start | bytes 1622024 | tf_op jit(solution)/shard_map/ppermute | solution.py:67
  26.8 2.2 %collective-permute-start.8 = (bf16[32,4224]{1,0:T(8,128)(2,1)}, bf16[32,4224]{1,0:T(8,128)(2,1)S(1)}, u32[]{:S(2)}, u32[]{:S(2)}) collective-permute-start(bf16[32,4224]{1,0:T(8,128)(2,1)} %copy-done.4), channel_id=1, source_target_pairs={{0,24},{1,9},{2,26},{3,11},{4,28},{5,13},{6,30},{7,15},{8,0},{9,17... | collective-permute-start | bytes 811016 | tf_op jit(solution)/shard_map/ppermute | solution.py:67
  32.8 6.9 %expert_terms.3 = (bf16[32,2176]{1,0:T(8,128)(2,1)S(1)}, bf16[32,2176]{1,0:T(8,128)(2,1)S(1)}, bf16[32,2176]{1,0:T(8,128)(2,1)S(1)}, bf16[32,2176]{1,0:T(8,128)(...) custom-call(s32[1]{0:T(128)} %bitcast.expert_ref, bf16[32,4224]{1,0:T(8,128)(2,1)S(1)} %copy-done.1, ...), custom_call_target="tpu_custom_call" | custom-call | flops 262144 | bytes 262144 | tf_op jit(solution)/shard_map/expert_terms/pallas_call | solution.py:152
  41.3 2.5 %collective-permute-done.8.refs_5_ = bf16[32,4224]{1,0:T(8,128)(2,1)S(1)} collective-permute-done((bf16[32,4224]{1,0:T(8,128)(2,1)}, bf16[32,4224]{1,0:T(8,128)(2,1)S(1)}, u32[]{:S(2)}, u32[]{:S(2)}) %collective-permute-start.8) | collective-permute-done | bytes 270368 | tf_op jit(solution)/shard_map/ppermute | solution.py:67
  45.1 2.5 %collective-permute-start.12 = (bf16[32,4224]{1,0:T(8,128)(2,1)S(1)}, bf16[32,4224]{1,0:T(8,128)(2,1)S(1)}, u32[]{:S(2)}, u32[]{:S(2)}) collective-permute-start(bf16[32,4224]{1,0:T(8,128)(2,1)S(1)} %get-tuple-element.72.refs_0_), channel_id=1, source_target_pairs={{0,4},{1,3},{2,6},{3,1},{4,0},{5,7},{6,2},{7,5},{8,12},{9,11},{10,... | collective-permute-start | bytes 811016 | tf_op jit(solution)/shard_map/ppermute | solution.py:67
  47.6 7.8 %expert_terms.4 = (bf16[64,2176]{1,0:T(8,128)(2,1)S(1)}, bf16[64,2176]{1,0:T(8,128)(2,1)S(1)}, bf16[64,2176]{1,0:T(8,128)(2,1)S(1)}, bf16[64,2176]{1,0:T(8,128)(...) custom-call(s32[1]{0:T(128)} %bitcast.expert_ref, ...), custom_call_target="tpu_custom_call" | custom-call | flops 524288 | bytes 524288 | tf_op jit(solution)/shard_map/expert_terms/pallas_call | solution.py:152
  55.5 1.3 %collective-permute-start.15 = (bf16[64,2176]{1,0:T(8,128)(2,1)S(1)}, bf16[64,2176]{1,0:T(8,128)(2,1)S(1)}, u32[]{:S(2)}, u32[]{:S(2)}) collective-permute-start(bf16[64,2176]{1,0:T(8,128)(2,1)S(1)} %get-tuple-element.68), channel_id=1, source_target_pairs={{0,4},{1,3},{2,6},{3,1},{4,0},{5,7},{6,2},{7,5},{8,12},{9,11},{10,... | collective-permute-start | bytes 835592 | tf_op jit(solution)/shard_map/ppermute | solution.py:67
  57.7 3.0 %collective-permute-start.16 = (bf16[32,2176]{1,0:T(8,128)(2,1)S(1)}, bf16[32,2176]{1,0:T(8,128)(2,1)S(1)}, u32[]{:S(2)}, u32[]{:S(2)}) collective-permute-start(bf16[32,2176]{1,0:T(8,128)(2,1)S(1)} %get-tuple-element.70), channel_id=1, source_target_pairs={{0,24},{1,9},{2,26},{3,11},{4,28},{5,13},{6,30},{7,15},{8,0},{9,17... | collective-permute-start | bytes 417800 | tf_op jit(solution)/shard_map/ppermute | solution.py:67
  60.7 6.8 %expert_terms.5 = (bf16[32,2176]{1,0:T(8,128)(2,1)S(1)}, bf16[32,2176]{1,0:T(8,128)(2,1)S(1)}, bf16[32,2176]{1,0:T(8,128)(2,1)S(1)}, bf16[32,2176]{1,0:T(8,128)(...) custom-call(s32[1]{0:T(128)} %bitcast.expert_ref, ...), custom_call_target="tpu_custom_call" | custom-call | flops 262144 | bytes 262144 | tf_op jit(solution)/shard_map/expert_terms/pallas_call | solution.py:152
  68.9 3.9 %collective-permute-start.18 = (bf16[32,2176]{1,0:T(8,128)(2,1)S(1)}, bf16[32,2176]{1,0:T(8,128)(2,1)S(1)}, u32[]{:S(2)}, u32[]{:S(2)}) collective-permute-start(bf16[32,2176]{1,0:T(8,128)(2,1)S(1)} %get-tuple-element.74), channel_id=1, source_target_pairs={{0,24},{1,9},{2,26},{3,11},{4,28},{5,13},{6,30},{7,15},{8,0},{9,17... | collective-permute-start | bytes 417800 | tf_op jit(solution)/shard_map/ppermute | solution.py:67
  73.7 1.5 %collective-permute-start.22 = (bf16[32,2176]{1,0:T(8,128)(2,1)S(1)}, bf16[32,2176]{1,0:T(8,128)(2,1)S(1)}, u32[]{:S(2)}, u32[]{:S(2)}) collective-permute-start(bf16[32,2176]{1,0:T(8,128)(2,1)S(1)} %get-tuple-element.81), channel_id=1, source_target_pairs={{0,6},{1,7},{2,4},{3,5},{4,2},{5,3},{6,0},{7,1},{8,14},{9,15},{10,... | collective-permute-start | bytes 417800 | tf_op jit(solution)/shard_map/ppermute | solution.py:67
  75.1 1.6 %collective-permute-done.18 = bf16[32,2176]{1,0:T(8,128)(2,1)S(1)} collective-permute-done((bf16[32,2176]{1,0:T(8,128)(2,1)S(1)}, bf16[32,2176]{1,0:T(8,128)(2,1)S(1)}, u32[]{:S(2)}, u32[]{:S(2)}) %collective-permute-start.18) | collective-permute-done | bytes 139296 | tf_op jit(solution)/shard_map/ppermute | solution.py:67
  77.4 3.1 %collective-permute-done.19 = bf16[32,2176]{1,0:T(8,128)(2,1)S(1)} collective-permute-done((bf16[32,2176]{1,0:T(8,128)(2,1)S(1)}, bf16[32,2176]{1,0:T(8,128)(2,1)S(1)}, u32[]{:S(2)}, u32[]{:S(2)}) %collective-permute-start.19) | collective-permute-done | bytes 139296 | tf_op jit(solution)/shard_map/ppermute | solution.py:67
  80.8 1.3 %collective-permute-start.25 = (bf16[32,2176]{1,0:T(8,128)(2,1)S(1)}, bf16[32,2176]{1,0:T(8,128)(2,1)S(1)}, u32[]{:S(2)}, u32[]{:S(2)}) collective-permute-start(bf16[32,2176]{1,0:T(8,128)(2,1)S(1)} %get-tuple-element.86), channel_id=1, source_target_pairs={{0,4},{1,3},{2,6},{3,1},{4,0},{5,7},{6,2},{7,5},{8,12},{9,11},{10,... | collective-permute-start | bytes 417800 | tf_op jit(solution)/shard_map/ppermute | solution.py:67
  82.1 1.5 %collective-permute-start.24 = (bf16[32,2176]{1,0:T(8,128)(2,1)S(1)}, bf16[32,2176]{1,0:T(8,128)(2,1)S(1)}, u32[]{:S(2)}, u32[]{:S(2)}) collective-permute-start(bf16[32,2176]{1,0:T(8,128)(2,1)S(1)} %get-tuple-element.84), channel_id=1, source_target_pairs={{0,2},{1,5},{2,0},{3,7},{4,6},{5,1},{6,4},{7,3},{8,10},{9,13},{10,... | collective-permute-start | bytes 417800 | tf_op jit(solution)/shard_map/ppermute | solution.py:67
  85.2 7.5 %weight_grads.1 = (bf16[2048,384]{1,0:T(8,128)(2,1)}, bf16[2048,384]{1,0:T(8,128)(2,1)}, bf16[384,2048]{1,0:T(8,128)(2,1)}) custom-call(bf16[128,5248]{1,0:T(8,128)(2,1)S(1)} %get-tuple-element.90.refs_0_, bf16[128,5248]{1,0:T(8,128)(2,1)S(1)} %collective-permute-done.27.refs_1_.refs_7_, bf16[256,5248]{1,0:T(8,128)(2,1)S(1)} %get-tuple-element.91.refs_2_, ...), custom_call_target="tpu_custom_call" | custom-call | flops 4831838208 | bytes 13107200 | tf_op jit(solution)/shard_map/weight_grads/pallas_call | solution.py:235
  (93 shorter events, 20.6 us)
Async XLA Ops:
  2.8 11.5 %collective-permute-start.4 = (bf16[2048,768]{1,0:T(8,128)(2,1)S(1)}, bf16[2048,768]{1,0:T(8,128)(2,1)}, u32[]{:S(2)}, u32[]{:S(2)}) collective-permute-start(bf16[2048,768]{1,0:T(8,128)(2,1)S(1)} %constant_dynamic-update-slice_fusion.refs_4_.refs_6_), channel_id=1, source_target_pairs={{0,1},{1,0},{2,3},{3,2},{4,5},{5,4},{6,7},{7,6},{8,9},{9,8},{10,11... | collective-permute-start | bytes 9437192 | tf_op jit(solution)/shard_map/ppermute | solution.py:67
  3.4 11.0 %collective-permute-start.5 = (bf16[384,2048]{1,0:T(8,128)(2,1)}, bf16[384,2048]{1,0:T(8,128)(2,1)}, u32[]{:S(2)}, u32[]{:S(2)}) collective-permute-start(bf16[384,2048]{1,0:T(8,128)(2,1)} %refs_5_.3), channel_id=1, source_target_pairs={{0,1},{1,0},{2,3},{3,2},{4,5},{5,4},{6,7},{7,6},{8,9},{9,8},{10,11... | collective-permute-start | bytes 4718600 | tf_op jit(solution)/shard_map/ppermute | solution.py:67
  4.2 7.4 %collective-permute-start.2 = (bf16[32,4224]{1,0:T(8,128)(2,1)S(1)}, bf16[32,4224]{1,0:T(8,128)(2,1)S(1)}, u32[]{:S(2)}, u32[]{:S(2)}) collective-permute-start(bf16[32,4224]{1,0:T(8,128)(2,1)S(1)} %pad_maximum_fusion.refs_0_), channel_id=1, source_target_pairs={{0,4},{1,3},{2,6},{3,1},{4,0},{5,7},{6,2},{7,5},{8,12},{9,11},{10,... | collective-permute-start | bytes 811016 | tf_op jit(solution)/shard_map/ppermute | solution.py:67
  7.2 11.3 %collective-permute-start = (bf16[32,4224]{1,0:T(8,128)(2,1)S(1)}, bf16[32,4224]{1,0:T(8,128)(2,1)S(1)}, u32[]{:S(2)}, u32[]{:S(2)}) collective-permute-start(bf16[32,4224]{1,0:T(8,128)(2,1)S(1)} %pad_maximum_fusion.refs_0_), channel_id=1, source_target_pairs={{0,8},{1,25},{2,10},{3,27},{4,12},{5,29},{6,14},{7,31},{8,16},{9,1... | collective-permute-start | bytes 811016 | tf_op jit(solution)/shard_map/ppermute | solution.py:67
  8.7 11.9 %collective-permute-start.1 = (bf16[32,4224]{1,0:T(8,128)(2,1)S(1)}, bf16[32,4224]{1,0:T(8,128)(2,1)S(1)}, u32[]{:S(2)}, u32[]{:S(2)}) collective-permute-start(bf16[32,4224]{1,0:T(8,128)(2,1)S(1)} %pad_maximum_fusion.refs_0_), channel_id=1, source_target_pairs={{0,24},{1,9},{2,26},{3,11},{4,28},{5,13},{6,30},{7,15},{8,0},{9,17... | collective-permute-start | bytes 811016 | tf_op jit(solution)/shard_map/ppermute | solution.py:67
  11.6 9.0 %collective-permute-start.3 = (bf16[32,4224]{1,0:T(8,128)(2,1)S(1)}, bf16[32,4224]{1,0:T(8,128)(2,1)S(1)}, u32[]{:S(2)}, u32[]{:S(2)}) collective-permute-start(bf16[32,4224]{1,0:T(8,128)(2,1)S(1)} %collective-permute-done.2.refs_2_), channel_id=1, source_target_pairs={{0,2},{1,5},{2,0},{3,7},{4,6},{5,1},{6,4},{7,3},{8,10},{9,13},{10,... | collective-permute-start | bytes 811016 | tf_op jit(solution)/shard_map/ppermute | solution.py:67
  22.3 18.0 %collective-permute-start.7 = (bf16[64,4224]{1,0:T(8,128)(2,1)}, bf16[64,4224]{1,0:T(8,128)(2,1)}, u32[]{:S(2)}, u32[]{:S(2)}) collective-permute-start(bf16[64,4224]{1,0:T(8,128)(2,1)} %get-tuple-element.55), channel_id=1, source_target_pairs={{0,8},{1,25},{2,10},{3,27},{4,12},{5,29},{6,14},{7,31},{8,16},{9,1... | collective-permute-start | bytes 1622024 | tf_op jit(solution)/shard_map/ppermute | solution.py:67
  24.4 19.5 %collective-permute-start.9 = (bf16[64,4224]{1,0:T(8,128)(2,1)}, bf16[64,4224]{1,0:T(8,128)(2,1)S(1)}, u32[]{:S(2)}, u32[]{:S(2)}) collective-permute-start(bf16[64,4224]{1,0:T(8,128)(2,1)} %copy-done.10), channel_id=1, source_target_pairs={{0,4},{1,3},{2,6},{3,1},{4,0},{5,7},{6,2},{7,5},{8,12},{9,11},{10,... | collective-permute-start | bytes 1622024 | tf_op jit(solution)/shard_map/ppermute | solution.py:67
  25.4 18.5 %collective-permute-start.10 = (bf16[64,4224]{1,0:T(8,128)(2,1)}, bf16[64,4224]{1,0:T(8,128)(2,1)S(1)}, u32[]{:S(2)}, u32[]{:S(2)}) collective-permute-start(bf16[64,4224]{1,0:T(8,128)(2,1)} %copy-done.10), channel_id=1, source_target_pairs={{0,2},{1,5},{2,0},{3,7},{4,6},{5,1},{6,4},{7,3},{8,10},{9,13},{10,... | collective-permute-start | bytes 1622024 | tf_op jit(solution)/shard_map/ppermute | solution.py:67
  26.8 17.1 %collective-permute-start.8 = (bf16[32,4224]{1,0:T(8,128)(2,1)}, bf16[32,4224]{1,0:T(8,128)(2,1)S(1)}, u32[]{:S(2)}, u32[]{:S(2)}) collective-permute-start(bf16[32,4224]{1,0:T(8,128)(2,1)} %copy-done.4), channel_id=1, source_target_pairs={{0,24},{1,9},{2,26},{3,11},{4,28},{5,13},{6,30},{7,15},{8,0},{9,17... | collective-permute-start | bytes 811016 | tf_op jit(solution)/shard_map/ppermute | solution.py:67
  43.9 11.6 %collective-permute-start.11 = (bf16[32,4224]{1,0:T(8,128)(2,1)S(1)}, bf16[32,4224]{1,0:T(8,128)(2,1)S(1)}, u32[]{:S(2)}, u32[]{:S(2)}) collective-permute-start(bf16[32,4224]{1,0:T(8,128)(2,1)S(1)} %get-tuple-element.64), channel_id=1, source_target_pairs={{0,8},{1,25},{2,10},{3,27},{4,12},{5,29},{6,14},{7,31},{8,16},{9,1... | collective-permute-start | bytes 811016 | tf_op jit(solution)/shard_map/ppermute | solution.py:67
  45.1 10.3 %collective-permute-start.12 = (bf16[32,4224]{1,0:T(8,128)(2,1)S(1)}, bf16[32,4224]{1,0:T(8,128)(2,1)S(1)}, u32[]{:S(2)}, u32[]{:S(2)}) collective-permute-start(bf16[32,4224]{1,0:T(8,128)(2,1)S(1)} %get-tuple-element.72.refs_0_), channel_id=1, source_target_pairs={{0,4},{1,3},{2,6},{3,1},{4,0},{5,7},{6,2},{7,5},{8,12},{9,11},{10,... | collective-permute-start | bytes 811016 | tf_op jit(solution)/shard_map/ppermute | solution.py:67
  47.6 7.8 %collective-permute-start.13 = (bf16[32,4224]{1,0:T(8,128)(2,1)S(1)}, bf16[32,4224]{1,0:T(8,128)(2,1)S(1)}, u32[]{:S(2)}, u32[]{:S(2)}) collective-permute-start(bf16[32,4224]{1,0:T(8,128)(2,1)S(1)} %get-tuple-element.72.refs_0_), channel_id=1, source_target_pairs={{0,2},{1,5},{2,0},{3,7},{4,6},{5,1},{6,4},{7,3},{8,10},{9,13},{10,... | collective-permute-start | bytes 811016 | tf_op jit(solution)/shard_map/ppermute | solution.py:67
  55.5 12.1 %collective-permute-start.15 = (bf16[64,2176]{1,0:T(8,128)(2,1)S(1)}, bf16[64,2176]{1,0:T(8,128)(2,1)S(1)}, u32[]{:S(2)}, u32[]{:S(2)}) collective-permute-start(bf16[64,2176]{1,0:T(8,128)(2,1)S(1)} %get-tuple-element.68), channel_id=1, source_target_pairs={{0,4},{1,3},{2,6},{3,1},{4,0},{5,7},{6,2},{7,5},{8,12},{9,11},{10,... | collective-permute-start | bytes 835592 | tf_op jit(solution)/shard_map/ppermute | solution.py:67
  56.8 10.8 %collective-permute-start.14 = (bf16[64,2176]{1,0:T(8,128)(2,1)S(1)}, bf16[64,2176]{1,0:T(8,128)(2,1)S(1)}, u32[]{:S(2)}, u32[]{:S(2)}) collective-permute-start(bf16[64,2176]{1,0:T(8,128)(2,1)S(1)} %get-tuple-element.66), channel_id=1, source_target_pairs={{0,2},{1,5},{2,0},{3,7},{4,6},{5,1},{6,4},{7,3},{8,10},{9,13},{10,... | collective-permute-start | bytes 835592 | tf_op jit(solution)/shard_map/ppermute | solution.py:67
  57.7 9.9 %collective-permute-start.16 = (bf16[32,2176]{1,0:T(8,128)(2,1)S(1)}, bf16[32,2176]{1,0:T(8,128)(2,1)S(1)}, u32[]{:S(2)}, u32[]{:S(2)}) collective-permute-start(bf16[32,2176]{1,0:T(8,128)(2,1)S(1)} %get-tuple-element.70), channel_id=1, source_target_pairs={{0,24},{1,9},{2,26},{3,11},{4,28},{5,13},{6,30},{7,15},{8,0},{9,17... | collective-permute-start | bytes 417800 | tf_op jit(solution)/shard_map/ppermute | solution.py:67
  60.7 24.5 %collective-permute-start.28 = (bf16[256,5248]{1,0:T(8,128)(2,1)S(1)}, bf16[256,5248]{1,0:T(8,128)(2,1)S(1)}, u32[]{:S(2)}, u32[]{:S(2)}) collective-permute-start(bf16[256,5248]{1,0:T(8,128)(2,1)S(1)} %get-tuple-element.91.refs_2_), channel_id=1, source_target_pairs={{0,1},{1,0},{2,3},{3,2},{4,5},{5,4},{6,7},{7,6},{8,9},{9,8},{10,11... | collective-permute-start | bytes 8060936 | tf_op jit(solution)/shard_map/ppermute | solution.py:67
  68.9 7.9 %collective-permute-start.18 = (bf16[32,2176]{1,0:T(8,128)(2,1)S(1)}, bf16[32,2176]{1,0:T(8,128)(2,1)S(1)}, u32[]{:S(2)}, u32[]{:S(2)}) collective-permute-start(bf16[32,2176]{1,0:T(8,128)(2,1)S(1)} %get-tuple-element.74), channel_id=1, source_target_pairs={{0,24},{1,9},{2,26},{3,11},{4,28},{5,13},{6,30},{7,15},{8,0},{9,17... | collective-permute-start | bytes 417800 | tf_op jit(solution)/shard_map/ppermute | solution.py:67
  72.8 7.7 %collective-permute-start.19 = (bf16[32,2176]{1,0:T(8,128)(2,1)S(1)}, bf16[32,2176]{1,0:T(8,128)(2,1)S(1)}, u32[]{:S(2)}, u32[]{:S(2)}) collective-permute-start(bf16[32,2176]{1,0:T(8,128)(2,1)S(1)} %get-tuple-element.75), channel_id=1, source_target_pairs={{0,8},{1,25},{2,10},{3,27},{4,12},{5,29},{6,14},{7,31},{8,16},{9,1... | collective-permute-start | bytes 417800 | tf_op jit(solution)/shard_map/ppermute | solution.py:67
  72.8 8.0 %collective-permute-start.21 = (bf16[32,2176]{1,0:T(8,128)(2,1)S(1)}, bf16[32,2176]{1,0:T(8,128)(2,1)S(1)}, u32[]{:S(2)}, u32[]{:S(2)}) collective-permute-start(bf16[32,2176]{1,0:T(8,128)(2,1)S(1)} %get-tuple-element.79), channel_id=1, source_target_pairs={{0,4},{1,3},{2,6},{3,1},{4,0},{5,7},{6,2},{7,5},{8,12},{9,11},{10,... | collective-permute-start | bytes 417800 | tf_op jit(solution)/shard_map/ppermute | solution.py:67
  80.8 11.8 %collective-permute-start.25 = (bf16[32,2176]{1,0:T(8,128)(2,1)S(1)}, bf16[32,2176]{1,0:T(8,128)(2,1)S(1)}, u32[]{:S(2)}, u32[]{:S(2)}) collective-permute-start(bf16[32,2176]{1,0:T(8,128)(2,1)S(1)} %get-tuple-element.86), channel_id=1, source_target_pairs={{0,4},{1,3},{2,6},{3,1},{4,0},{5,7},{6,2},{7,5},{8,12},{9,11},{10,... | collective-permute-start | bytes 417800 | tf_op jit(solution)/shard_map/ppermute | solution.py:67
  82.1 10.6 %collective-permute-start.24 = (bf16[32,2176]{1,0:T(8,128)(2,1)S(1)}, bf16[32,2176]{1,0:T(8,128)(2,1)S(1)}, u32[]{:S(2)}, u32[]{:S(2)}) collective-permute-start(bf16[32,2176]{1,0:T(8,128)(2,1)S(1)} %get-tuple-element.84), channel_id=1, source_target_pairs={{0,2},{1,5},{2,0},{3,7},{4,6},{5,1},{6,4},{7,3},{8,10},{9,13},{10,... | collective-permute-start | bytes 417800 | tf_op jit(solution)/shard_map/ppermute | solution.py:67
  83.8 8.9 %collective-permute-start.23 = (bf16[32,2176]{1,0:T(8,128)(2,1)S(1)}, bf16[32,2176]{1,0:T(8,128)(2,1)S(1)}, u32[]{:S(2)}, u32[]{:S(2)}) collective-permute-start(bf16[32,2176]{1,0:T(8,128)(2,1)S(1)} %add_convert_fusion.2), channel_id=1, source_target_pairs={{0,16},{1,17},{2,18},{3,19},{4,20},{5,21},{6,22},{7,23},{8,24},{9,... | collective-permute-start | bytes 417800 | tf_op jit(solution)/shard_map/ppermute | solution.py:67
  84.5 8.1 %collective-permute-start.26 = (bf16[32,2176]{1,0:T(8,128)(2,1)S(1)}, bf16[32,2176]{1,0:T(8,128)(2,1)S(1)}, u32[]{:S(2)}, u32[]{:S(2)}) collective-permute-start(bf16[32,2176]{1,0:T(8,128)(2,1)S(1)} %add_convert_fusion.1), channel_id=1, source_target_pairs={{0,6},{1,7},{2,4},{3,5},{4,2},{5,3},{6,0},{7,1},{8,14},{9,15},{10,... | collective-permute-start | bytes 417800 | tf_op jit(solution)/shard_map/ppermute | solution.py:67
  (24 other events, 79.2 us)

commit v6 on v5

--- a/solution.py
+++ b/solution.py
@@ -117,7 +117,7 @@
     lane = lax.broadcasted_iota(jnp.int32, gates.shape, 1)
     gate_lanes = jnp.where(lane == expert, gate_grad, 0.0).astype(BF16)
     scatter(gate_lanes, parts, slice(width, None))
-    tile = 512 if width % 512 == 0 else width
+    tile = 1024 if width % 1024 == 0 else width
     for low in range(0, width, tile):
         span = slice(low, low + tile)
         token = 0.0
@@ -348,7 +348,9 @@
         if last + 1 < step:
             for at in range(last + 1) if step == last + 3 else ():
                 block = rows[2 * at]
-                if at in (0, last):
+                if at == 0:
+                    block = after(block, *planes[1][1:2])
+                if at == last:
                     block = after(block, *planes[last][1:2])
                 rows[2 * at + 1] = terms[2 * at + 1] = send(block, swap)
         if 0 <= step - 1 <= last:

time: 95 us -> 95 us (level)
  no operation moved by 1% of the time
where the time goes in v6:
time: 95 us; the launch traced here: 94.4 us
  starting transfers between devices  37.3 us (39%)
  Pallas kernels  30 us (32%)
  waiting for transfers between devices  14.4 us (15%)
  local copies, waits for them, and re-layouts  10.5 us (11%)
  other arithmetic  1.38 us (1%)
    ppermute x30, starting transfers between devices, send(): return lax.ppermute(block, 'expert', pairs)  37.3 us
    pallas_call x3, Pallas kernels, expert_terms(): pl.pallas_call(functools.partial(terms_body, spans, len(arrays), width, h...  21.6 us
    ppermute x30, waiting for transfers between devices, send(): return lax.ppermute(block, 'expert', pairs)  14.4 us
    unnamed x39, local copies, waits for them, and re-layouts  9.02 us
    pallas_call x1, Pallas kernels, weight_grads(): pl.pallas_call(functools.partial(grads_body, groups, width, half), grid=(...  7.47 us
  transfers between devices with their start and end apart: 30, of which 8 were waited for; matrix products, arithmetic and copies ran while one was open for 2% of the time, Pallas kernels for 32%

profile of v6, /device:TPU:0, one launch (start us, length us, event | category | flops | bytes accessed | tf_op | source)
XLA Modules:
  0.0 94.4 jit_solution(14010054291654110328)
XLA Ops:
  0.6 1.7 %constant_dynamic-update-slice_fusion.1 = bf16[2048,768]{1,0:T(8,128)(2,1)S(1)} fusion(bf16[2048,384]{1,0:T(8,128)(2,1)} %param.11), kind=kLoop, calls=%fused_computation.10 | loop fusion | bytes 3145728
  4.2 2.9 %collective-permute-start.2 = (bf16[32,4224]{1,0:T(8,128)(2,1)S(1)}, bf16[32,4224]{1,0:T(8,128)(2,1)S(1)}, u32[]{:S(2)}, u32[]{:S(2)}) collective-permute-start(bf16[32,4224]{1,0:T(8,128)(2,1)S(1)} %pad_maximum_fusion.refs_0_), channel_id=1, source_target_pairs={{0,4},{1,3},{2,6},{3,1},{4,0},{5,7},{6,2},{7,5},{8,12},{9,11},{10,... | collective-permute-start | bytes 811016 | tf_op jit(solution)/shard_map/ppermute | solution.py:67
  7.2 1.6 %collective-permute-start = (bf16[32,4224]{1,0:T(8,128)(2,1)S(1)}, bf16[32,4224]{1,0:T(8,128)(2,1)S(1)}, u32[]{:S(2)}, u32[]{:S(2)}) collective-permute-start(bf16[32,4224]{1,0:T(8,128)(2,1)S(1)} %pad_maximum_fusion.refs_0_), channel_id=1, source_target_pairs={{0,8},{1,25},{2,10},{3,27},{4,12},{5,29},{6,14},{7,31},{8,16},{9,1... | collective-permute-start | bytes 811016 | tf_op jit(solution)/shard_map/ppermute | solution.py:67
  8.7 2.2 %collective-permute-start.1 = (bf16[32,4224]{1,0:T(8,128)(2,1)S(1)}, bf16[32,4224]{1,0:T(8,128)(2,1)S(1)}, u32[]{:S(2)}, u32[]{:S(2)}) collective-permute-start(bf16[32,4224]{1,0:T(8,128)(2,1)S(1)} %pad_maximum_fusion.refs_0_), channel_id=1, source_target_pairs={{0,24},{1,9},{2,26},{3,11},{4,28},{5,13},{6,30},{7,15},{8,0},{9,17... | collective-permute-start | bytes 811016 | tf_op jit(solution)/shard_map/ppermute | solution.py:67
  11.6 2.0 %collective-permute-start.3 = (bf16[32,4224]{1,0:T(8,128)(2,1)S(1)}, bf16[32,4224]{1,0:T(8,128)(2,1)S(1)}, u32[]{:S(2)}, u32[]{:S(2)}) collective-permute-start(bf16[32,4224]{1,0:T(8,128)(2,1)S(1)} %collective-permute-done.2.refs_2_), channel_id=1, source_target_pairs={{0,2},{1,5},{2,0},{3,7},{4,6},{5,1},{6,4},{7,3},{8,10},{9,13},{10,... | collective-permute-start | bytes 811016 | tf_op jit(solution)/shard_map/ppermute | solution.py:67
  15.1 3.4 %collective-permute-done.refs_0_.refs_2_ = bf16[32,4224]{1,0:T(8,128)(2,1)S(1)} collective-permute-done((bf16[32,4224]{1,0:T(8,128)(2,1)S(1)}, bf16[32,4224]{1,0:T(8,128)(2,1)S(1)}, u32[]{:S(2)}, u32[]{:S(2)}) %collective-permute-start) | collective-permute-done | bytes 270368 | tf_op jit(solution)/shard_map/ppermute | solution.py:67
  18.4 2.2 %collective-permute-done.1.refs_1_ = bf16[32,4224]{1,0:T(8,128)(2,1)S(1)} collective-permute-done((bf16[32,4224]{1,0:T(8,128)(2,1)S(1)}, bf16[32,4224]{1,0:T(8,128)(2,1)S(1)}, u32[]{:S(2)}, u32[]{:S(2)}) %collective-permute-start.1) | collective-permute-done | bytes 270368 | tf_op jit(solution)/shard_map/ppermute | solution.py:67
  22.3 2.0 %collective-permute-start.7 = (bf16[64,4224]{1,0:T(8,128)(2,1)}, bf16[64,4224]{1,0:T(8,128)(2,1)}, u32[]{:S(2)}, u32[]{:S(2)}) collective-permute-start(bf16[64,4224]{1,0:T(8,128)(2,1)} %get-tuple-element.55), channel_id=1, source_target_pairs={{0,8},{1,25},{2,10},{3,27},{4,12},{5,29},{6,14},{7,31},{8,16},{9,1... | collective-permute-start | bytes 1622024 | tf_op jit(solution)/shard_map/ppermute | solution.py:67
  25.4 1.3 %collective-permute-start.10 = (bf16[64,4224]{1,0:T(8,128)(2,1)}, bf16[64,4224]{1,0:T(8,128)(2,1)S(1)}, u32[]{:S(2)}, u32[]{:S(2)}) collective-permute-start(bf16[64,4224]{1,0:T(8,128)(2,1)} %copy-done.10), channel_id=1, source_target_pairs={{0,2},{1,5},{2,0},{3,7},{4,6},{5,1},{6,4},{7,3},{8,10},{9,13},{10,... | collective-permute-start | bytes 1622024 | tf_op jit(solution)/shard_map/ppermute | solution.py:67
  26.8 2.2 %collective-permute-start.8 = (bf16[32,4224]{1,0:T(8,128)(2,1)}, bf16[32,4224]{1,0:T(8,128)(2,1)S(1)}, u32[]{:S(2)}, u32[]{:S(2)}) collective-permute-start(bf16[32,4224]{1,0:T(8,128)(2,1)} %copy-done.4), channel_id=1, source_target_pairs={{0,24},{1,9},{2,26},{3,11},{4,28},{5,13},{6,30},{7,15},{8,0},{9,17... | collective-permute-start | bytes 811016 | tf_op jit(solution)/shard_map/ppermute | solution.py:67
  32.8 6.9 %expert_terms.3 = (bf16[32,2176]{1,0:T(8,128)(2,1)S(1)}, bf16[32,2176]{1,0:T(8,128)(2,1)S(1)}, bf16[32,2176]{1,0:T(8,128)(2,1)S(1)}, bf16[32,2176]{1,0:T(8,128)(...) custom-call(s32[1]{0:T(128)} %bitcast.expert_ref, bf16[32,4224]{1,0:T(8,128)(2,1)S(1)} %copy-done.1, ...), custom_call_target="tpu_custom_call" | custom-call | flops 262144 | bytes 262144 | tf_op jit(solution)/shard_map/expert_terms/pallas_call | solution.py:152
  41.3 2.5 %collective-permute-done.8.refs_5_ = bf16[32,4224]{1,0:T(8,128)(2,1)S(1)} collective-permute-done((bf16[32,4224]{1,0:T(8,128)(2,1)}, bf16[32,4224]{1,0:T(8,128)(2,1)S(1)}, u32[]{:S(2)}, u32[]{:S(2)}) %collective-permute-start.8) | collective-permute-done | bytes 270368 | tf_op jit(solution)/shard_map/ppermute | solution.py:67
  45.1 2.5 %collective-permute-start.12 = (bf16[32,4224]{1,0:T(8,128)(2,1)S(1)}, bf16[32,4224]{1,0:T(8,128)(2,1)S(1)}, u32[]{:S(2)}, u32[]{:S(2)}) collective-permute-start(bf16[32,4224]{1,0:T(8,128)(2,1)S(1)} %get-tuple-element.72.refs_0_), channel_id=1, source_target_pairs={{0,4},{1,3},{2,6},{3,1},{4,0},{5,7},{6,2},{7,5},{8,12},{9,11},{10,... | collective-permute-start | bytes 811016 | tf_op jit(solution)/shard_map/ppermute | solution.py:67
  47.6 7.8 %expert_terms.4 = (bf16[64,2176]{1,0:T(8,128)(2,1)S(1)}, bf16[64,2176]{1,0:T(8,128)(2,1)S(1)}, bf16[64,2176]{1,0:T(8,128)(2,1)S(1)}, bf16[64,2176]{1,0:T(8,128)(...) custom-call(s32[1]{0:T(128)} %bitcast.expert_ref, ...), custom_call_target="tpu_custom_call" | custom-call | flops 524288 | bytes 524288 | tf_op jit(solution)/shard_map/expert_terms/pallas_call | solution.py:152
  55.5 1.3 %collective-permute-start.15 = (bf16[64,2176]{1,0:T(8,128)(2,1)S(1)}, bf16[64,2176]{1,0:T(8,128)(2,1)S(1)}, u32[]{:S(2)}, u32[]{:S(2)}) collective-permute-start(bf16[64,2176]{1,0:T(8,128)(2,1)S(1)} %get-tuple-element.68), channel_id=1, source_target_pairs={{0,4},{1,3},{2,6},{3,1},{4,0},{5,7},{6,2},{7,5},{8,12},{9,11},{10,... | collective-permute-start | bytes 835592 | tf_op jit(solution)/shard_map/ppermute | solution.py:67
  57.7 3.0 %collective-permute-start.16 = (bf16[32,2176]{1,0:T(8,128)(2,1)S(1)}, bf16[32,2176]{1,0:T(8,128)(2,1)S(1)}, u32[]{:S(2)}, u32[]{:S(2)}) collective-permute-start(bf16[32,2176]{1,0:T(8,128)(2,1)S(1)} %get-tuple-element.70), channel_id=1, source_target_pairs={{0,24},{1,9},{2,26},{3,11},{4,28},{5,13},{6,30},{7,15},{8,0},{9,17... | collective-permute-start | bytes 417800 | tf_op jit(solution)/shard_map/ppermute | solution.py:67
  60.7 6.8 %expert_terms.5 = (bf16[32,2176]{1,0:T(8,128)(2,1)S(1)}, bf16[32,2176]{1,0:T(8,128)(2,1)S(1)}, bf16[32,2176]{1,0:T(8,128)(2,1)S(1)}, bf16[32,2176]{1,0:T(8,128)(...) custom-call(s32[1]{0:T(128)} %bitcast.expert_ref, ...), custom_call_target="tpu_custom_call" | custom-call | flops 262144 | bytes 262144 | tf_op jit(solution)/shard_map/expert_terms/pallas_call | solution.py:152
  68.9 3.9 %collective-permute-start.18 = (bf16[32,2176]{1,0:T(8,128)(2,1)S(1)}, bf16[32,2176]{1,0:T(8,128)(2,1)S(1)}, u32[]{:S(2)}, u32[]{:S(2)}) collective-permute-start(bf16[32,2176]{1,0:T(8,128)(2,1)S(1)} %get-tuple-element.74), channel_id=1, source_target_pairs={{0,24},{1,9},{2,26},{3,11},{4,28},{5,13},{6,30},{7,15},{8,0},{9,17... | collective-permute-start | bytes 417800 | tf_op jit(solution)/shard_map/ppermute | solution.py:67
  73.7 1.5 %collective-permute-start.22 = (bf16[32,2176]{1,0:T(8,128)(2,1)S(1)}, bf16[32,2176]{1,0:T(8,128)(2,1)S(1)}, u32[]{:S(2)}, u32[]{:S(2)}) collective-permute-start(bf16[32,2176]{1,0:T(8,128)(2,1)S(1)} %get-tuple-element.81), channel_id=1, source_target_pairs={{0,6},{1,7},{2,4},{3,5},{4,2},{5,3},{6,0},{7,1},{8,14},{9,15},{10,... | collective-permute-start | bytes 417800 | tf_op jit(solution)/shard_map/ppermute | solution.py:67
  75.2 1.7 %collective-permute-done.18 = bf16[32,2176]{1,0:T(8,128)(2,1)S(1)} collective-permute-done((bf16[32,2176]{1,0:T(8,128)(2,1)S(1)}, bf16[32,2176]{1,0:T(8,128)(2,1)S(1)}, u32[]{:S(2)}, u32[]{:S(2)}) %collective-permute-start.18) | collective-permute-done | bytes 139296 | tf_op jit(solution)/shard_map/ppermute | solution.py:67
  77.4 3.1 %collective-permute-done.19 = bf16[32,2176]{1,0:T(8,128)(2,1)S(1)} collective-permute-done((bf16[32,2176]{1,0:T(8,128)(2,1)S(1)}, bf16[32,2176]{1,0:T(8,128)(2,1)S(1)}, u32[]{:S(2)}, u32[]{:S(2)}) %collective-permute-start.19) | collective-permute-done | bytes 139296 | tf_op jit(solution)/shard_map/ppermute | solution.py:67
  80.9 1.3 %collective-permute-start.25 = (bf16[32,2176]{1,0:T(8,128)(2,1)S(1)}, bf16[32,2176]{1,0:T(8,128)(2,1)S(1)}, u32[]{:S(2)}, u32[]{:S(2)}) collective-permute-start(bf16[32,2176]{1,0:T(8,128)(2,1)S(1)} %get-tuple-element.86), channel_id=1, source_target_pairs={{0,4},{1,3},{2,6},{3,1},{4,0},{5,7},{6,2},{7,5},{8,12},{9,11},{10,... | collective-permute-start | bytes 417800 | tf_op jit(solution)/shard_map/ppermute | solution.py:67
  82.1 1.5 %collective-permute-start.24 = (bf16[32,2176]{1,0:T(8,128)(2,1)S(1)}, bf16[32,2176]{1,0:T(8,128)(2,1)S(1)}, u32[]{:S(2)}, u32[]{:S(2)}) collective-permute-start(bf16[32,2176]{1,0:T(8,128)(2,1)S(1)} %get-tuple-element.84), channel_id=1, source_target_pairs={{0,2},{1,5},{2,0},{3,7},{4,6},{5,1},{6,4},{7,3},{8,10},{9,13},{10,... | collective-permute-start | bytes 417800 | tf_op jit(solution)/shard_map/ppermute | solution.py:67
  85.2 7.5 %weight_grads.1 = (bf16[2048,384]{1,0:T(8,128)(2,1)}, bf16[2048,384]{1,0:T(8,128)(2,1)}, bf16[384,2048]{1,0:T(8,128)(2,1)}) custom-call(bf16[128,5248]{1,0:T(8,128)(2,1)S(1)} %get-tuple-element.90.refs_0_, bf16[128,5248]{1,0:T(8,128)(2,1)S(1)} %collective-permute-done.27.refs_1_.refs_7_, bf16[256,5248]{1,0:T(8,128)(2,1)S(1)} %get-tuple-element.91.refs_2_, ...), custom_call_target="tpu_custom_call" | custom-call | flops 4831838208 | bytes 13107200 | tf_op jit(solution)/shard_map/weight_grads/pallas_call | solution.py:235
  (93 shorter events, 20.7 us)
Async XLA Ops:
  2.8 11.5 %collective-permute-start.4 = (bf16[2048,768]{1,0:T(8,128)(2,1)S(1)}, bf16[2048,768]{1,0:T(8,128)(2,1)}, u32[]{:S(2)}, u32[]{:S(2)}) collective-permute-start(bf16[2048,768]{1,0:T(8,128)(2,1)S(1)} %constant_dynamic-update-slice_fusion.refs_4_.refs_6_), channel_id=1, source_target_pairs={{0,1},{1,0},{2,3},{3,2},{4,5},{5,4},{6,7},{7,6},{8,9},{9,8},{10,11... | collective-permute-start | bytes 9437192 | tf_op jit(solution)/shard_map/ppermute | solution.py:67
  3.4 11.0 %collective-permute-start.5 = (bf16[384,2048]{1,0:T(8,128)(2,1)}, bf16[384,2048]{1,0:T(8,128)(2,1)}, u32[]{:S(2)}, u32[]{:S(2)}) collective-permute-start(bf16[384,2048]{1,0:T(8,128)(2,1)} %refs_5_.3), channel_id=1, source_target_pairs={{0,1},{1,0},{2,3},{3,2},{4,5},{5,4},{6,7},{7,6},{8,9},{9,8},{10,11... | collective-permute-start | bytes 4718600 | tf_op jit(solution)/shard_map/ppermute | solution.py:67
  4.2 7.4 %collective-permute-start.2 = (bf16[32,4224]{1,0:T(8,128)(2,1)S(1)}, bf16[32,4224]{1,0:T(8,128)(2,1)S(1)}, u32[]{:S(2)}, u32[]{:S(2)}) collective-permute-start(bf16[32,4224]{1,0:T(8,128)(2,1)S(1)} %pad_maximum_fusion.refs_0_), channel_id=1, source_target_pairs={{0,4},{1,3},{2,6},{3,1},{4,0},{5,7},{6,2},{7,5},{8,12},{9,11},{10,... | collective-permute-start | bytes 811016 | tf_op jit(solution)/shard_map/ppermute | solution.py:67
  7.2 11.3 %collective-permute-start = (bf16[32,4224]{1,0:T(8,128)(2,1)S(1)}, bf16[32,4224]{1,0:T(8,128)(2,1)S(1)}, u32[]{:S(2)}, u32[]{:S(2)}) collective-permute-start(bf16[32,4224]{1,0:T(8,128)(2,1)S(1)} %pad_maximum_fusion.refs_0_), channel_id=1, source_target_pairs={{0,8},{1,25},{2,10},{3,27},{4,12},{5,29},{6,14},{7,31},{8,16},{9,1... | collective-permute-start | bytes 811016 | tf_op jit(solution)/shard_map/ppermute | solution.py:67
  8.7 11.9 %collective-permute-start.1 = (bf16[32,4224]{1,0:T(8,128)(2,1)S(1)}, bf16[32,4224]{1,0:T(8,128)(2,1)S(1)}, u32[]{:S(2)}, u32[]{:S(2)}) collective-permute-start(bf16[32,4224]{1,0:T(8,128)(2,1)S(1)} %pad_maximum_fusion.refs_0_), channel_id=1, source_target_pairs={{0,24},{1,9},{2,26},{3,11},{4,28},{5,13},{6,30},{7,15},{8,0},{9,17... | collective-permute-start | bytes 811016 | tf_op jit(solution)/shard_map/ppermute | solution.py:67
  11.6 9.0 %collective-permute-start.3 = (bf16[32,4224]{1,0:T(8,128)(2,1)S(1)}, bf16[32,4224]{1,0:T(8,128)(2,1)S(1)}, u32[]{:S(2)}, u32[]{:S(2)}) collective-permute-start(bf16[32,4224]{1,0:T(8,128)(2,1)S(1)} %collective-permute-done.2.refs_2_), channel_id=1, source_target_pairs={{0,2},{1,5},{2,0},{3,7},{4,6},{5,1},{6,4},{7,3},{8,10},{9,13},{10,... | collective-permute-start | bytes 811016 | tf_op jit(solution)/shard_map/ppermute | solution.py:67
  22.3 18.0 %collective-permute-start.7 = (bf16[64,4224]{1,0:T(8,128)(2,1)}, bf16[64,4224]{1,0:T(8,128)(2,1)}, u32[]{:S(2)}, u32[]{:S(2)}) collective-permute-start(bf16[64,4224]{1,0:T(8,128)(2,1)} %get-tuple-element.55), channel_id=1, source_target_pairs={{0,8},{1,25},{2,10},{3,27},{4,12},{5,29},{6,14},{7,31},{8,16},{9,1... | collective-permute-start | bytes 1622024 | tf_op jit(solution)/shard_map/ppermute | solution.py:67
  24.4 19.5 %collective-permute-start.9 = (bf16[64,4224]{1,0:T(8,128)(2,1)}, bf16[64,4224]{1,0:T(8,128)(2,1)S(1)}, u32[]{:S(2)}, u32[]{:S(2)}) collective-permute-start(bf16[64,4224]{1,0:T(8,128)(2,1)} %copy-done.10), channel_id=1, source_target_pairs={{0,4},{1,3},{2,6},{3,1},{4,0},{5,7},{6,2},{7,5},{8,12},{9,11},{10,... | collective-permute-start | bytes 1622024 | tf_op jit(solution)/shard_map/ppermute | solution.py:67
  25.4 18.5 %collective-permute-start.10 = (bf16[64,4224]{1,0:T(8,128)(2,1)}, bf16[64,4224]{1,0:T(8,128)(2,1)S(1)}, u32[]{:S(2)}, u32[]{:S(2)}) collective-permute-start(bf16[64,4224]{1,0:T(8,128)(2,1)} %copy-done.10), channel_id=1, source_target_pairs={{0,2},{1,5},{2,0},{3,7},{4,6},{5,1},{6,4},{7,3},{8,10},{9,13},{10,... | collective-permute-start | bytes 1622024 | tf_op jit(solution)/shard_map/ppermute | solution.py:67
  26.8 17.1 %collective-permute-start.8 = (bf16[32,4224]{1,0:T(8,128)(2,1)}, bf16[32,4224]{1,0:T(8,128)(2,1)S(1)}, u32[]{:S(2)}, u32[]{:S(2)}) collective-permute-start(bf16[32,4224]{1,0:T(8,128)(2,1)} %copy-done.4), channel_id=1, source_target_pairs={{0,24},{1,9},{2,26},{3,11},{4,28},{5,13},{6,30},{7,15},{8,0},{9,17... | collective-permute-start | bytes 811016 | tf_op jit(solution)/shard_map/ppermute | solution.py:67
  43.9 11.6 %collective-permute-start.11 = (bf16[32,4224]{1,0:T(8,128)(2,1)S(1)}, bf16[32,4224]{1,0:T(8,128)(2,1)S(1)}, u32[]{:S(2)}, u32[]{:S(2)}) collective-permute-start(bf16[32,4224]{1,0:T(8,128)(2,1)S(1)} %get-tuple-element.64), channel_id=1, source_target_pairs={{0,8},{1,25},{2,10},{3,27},{4,12},{5,29},{6,14},{7,31},{8,16},{9,1... | collective-permute-start | bytes 811016 | tf_op jit(solution)/shard_map/ppermute | solution.py:67
  45.1 10.4 %collective-permute-start.12 = (bf16[32,4224]{1,0:T(8,128)(2,1)S(1)}, bf16[32,4224]{1,0:T(8,128)(2,1)S(1)}, u32[]{:S(2)}, u32[]{:S(2)}) collective-permute-start(bf16[32,4224]{1,0:T(8,128)(2,1)S(1)} %get-tuple-element.72.refs_0_), channel_id=1, source_target_pairs={{0,4},{1,3},{2,6},{3,1},{4,0},{5,7},{6,2},{7,5},{8,12},{9,11},{10,... | collective-permute-start | bytes 811016 | tf_op jit(solution)/shard_map/ppermute | solution.py:67
  47.6 7.9 %collective-permute-start.13 = (bf16[32,4224]{1,0:T(8,128)(2,1)S(1)}, bf16[32,4224]{1,0:T(8,128)(2,1)S(1)}, u32[]{:S(2)}, u32[]{:S(2)}) collective-permute-start(bf16[32,4224]{1,0:T(8,128)(2,1)S(1)} %get-tuple-element.72.refs_0_), channel_id=1, source_target_pairs={{0,2},{1,5},{2,0},{3,7},{4,6},{5,1},{6,4},{7,3},{8,10},{9,13},{10,... | collective-permute-start | bytes 811016 | tf_op jit(solution)/shard_map/ppermute | solution.py:67
  55.5 12.1 %collective-permute-start.15 = (bf16[64,2176]{1,0:T(8,128)(2,1)S(1)}, bf16[64,2176]{1,0:T(8,128)(2,1)S(1)}, u32[]{:S(2)}, u32[]{:S(2)}) collective-permute-start(bf16[64,2176]{1,0:T(8,128)(2,1)S(1)} %get-tuple-element.68), channel_id=1, source_target_pairs={{0,4},{1,3},{2,6},{3,1},{4,0},{5,7},{6,2},{7,5},{8,12},{9,11},{10,... | collective-permute-start | bytes 835592 | tf_op jit(solution)/shard_map/ppermute | solution.py:67
  56.8 10.8 %collective-permute-start.14 = (bf16[64,2176]{1,0:T(8,128)(2,1)S(1)}, bf16[64,2176]{1,0:T(8,128)(2,1)S(1)}, u32[]{:S(2)}, u32[]{:S(2)}) collective-permute-start(bf16[64,2176]{1,0:T(8,128)(2,1)S(1)} %get-tuple-element.66), channel_id=1, source_target_pairs={{0,2},{1,5},{2,0},{3,7},{4,6},{5,1},{6,4},{7,3},{8,10},{9,13},{10,... | collective-permute-start | bytes 835592 | tf_op jit(solution)/shard_map/ppermute | solution.py:67
  57.7 9.9 %collective-permute-start.16 = (bf16[32,2176]{1,0:T(8,128)(2,1)S(1)}, bf16[32,2176]{1,0:T(8,128)(2,1)S(1)}, u32[]{:S(2)}, u32[]{:S(2)}) collective-permute-start(bf16[32,2176]{1,0:T(8,128)(2,1)S(1)} %get-tuple-element.70), channel_id=1, source_target_pairs={{0,24},{1,9},{2,26},{3,11},{4,28},{5,13},{6,30},{7,15},{8,0},{9,17... | collective-permute-start | bytes 417800 | tf_op jit(solution)/shard_map/ppermute | solution.py:67
  60.7 24.5 %collective-permute-start.28 = (bf16[256,5248]{1,0:T(8,128)(2,1)S(1)}, bf16[256,5248]{1,0:T(8,128)(2,1)S(1)}, u32[]{:S(2)}, u32[]{:S(2)}) collective-permute-start(bf16[256,5248]{1,0:T(8,128)(2,1)S(1)} %get-tuple-element.91.refs_2_), channel_id=1, source_target_pairs={{0,1},{1,0},{2,3},{3,2},{4,5},{5,4},{6,7},{7,6},{8,9},{9,8},{10,11... | collective-permute-start | bytes 8060936 | tf_op jit(solution)/shard_map/ppermute | solution.py:67
  68.9 7.9 %collective-permute-start.18 = (bf16[32,2176]{1,0:T(8,128)(2,1)S(1)}, bf16[32,2176]{1,0:T(8,128)(2,1)S(1)}, u32[]{:S(2)}, u32[]{:S(2)}) collective-permute-start(bf16[32,2176]{1,0:T(8,128)(2,1)S(1)} %get-tuple-element.74), channel_id=1, source_target_pairs={{0,24},{1,9},{2,26},{3,11},{4,28},{5,13},{6,30},{7,15},{8,0},{9,17... | collective-permute-start | bytes 417800 | tf_op jit(solution)/shard_map/ppermute | solution.py:67
  72.8 7.7 %collective-permute-start.19 = (bf16[32,2176]{1,0:T(8,128)(2,1)S(1)}, bf16[32,2176]{1,0:T(8,128)(2,1)S(1)}, u32[]{:S(2)}, u32[]{:S(2)}) collective-permute-start(bf16[32,2176]{1,0:T(8,128)(2,1)S(1)} %get-tuple-element.75), channel_id=1, source_target_pairs={{0,8},{1,25},{2,10},{3,27},{4,12},{5,29},{6,14},{7,31},{8,16},{9,1... | collective-permute-start | bytes 417800 | tf_op jit(solution)/shard_map/ppermute | solution.py:67
  72.8 8.0 %collective-permute-start.21 = (bf16[32,2176]{1,0:T(8,128)(2,1)S(1)}, bf16[32,2176]{1,0:T(8,128)(2,1)S(1)}, u32[]{:S(2)}, u32[]{:S(2)}) collective-permute-start(bf16[32,2176]{1,0:T(8,128)(2,1)S(1)} %get-tuple-element.79), channel_id=1, source_target_pairs={{0,4},{1,3},{2,6},{3,1},{4,0},{5,7},{6,2},{7,5},{8,12},{9,11},{10,... | collective-permute-start | bytes 417800 | tf_op jit(solution)/shard_map/ppermute | solution.py:67
  80.9 11.8 %collective-permute-start.25 = (bf16[32,2176]{1,0:T(8,128)(2,1)S(1)}, bf16[32,2176]{1,0:T(8,128)(2,1)S(1)}, u32[]{:S(2)}, u32[]{:S(2)}) collective-permute-start(bf16[32,2176]{1,0:T(8,128)(2,1)S(1)} %get-tuple-element.86), channel_id=1, source_target_pairs={{0,4},{1,3},{2,6},{3,1},{4,0},{5,7},{6,2},{7,5},{8,12},{9,11},{10,... | collective-permute-start | bytes 417800 | tf_op jit(solution)/shard_map/ppermute | solution.py:67
  82.1 10.6 %collective-permute-start.24 = (bf16[32,2176]{1,0:T(8,128)(2,1)S(1)}, bf16[32,2176]{1,0:T(8,128)(2,1)S(1)}, u32[]{:S(2)}, u32[]{:S(2)}) collective-permute-start(bf16[32,2176]{1,0:T(8,128)(2,1)S(1)} %get-tuple-element.84), channel_id=1, source_target_pairs={{0,2},{1,5},{2,0},{3,7},{4,6},{5,1},{6,4},{7,3},{8,10},{9,13},{10,... | collective-permute-start | bytes 417800 | tf_op jit(solution)/shard_map/ppermute | solution.py:67
  83.8 9.0 %collective-permute-start.23 = (bf16[32,2176]{1,0:T(8,128)(2,1)S(1)}, bf16[32,2176]{1,0:T(8,128)(2,1)S(1)}, u32[]{:S(2)}, u32[]{:S(2)}) collective-permute-start(bf16[32,2176]{1,0:T(8,128)(2,1)S(1)} %add_convert_fusion.2), channel_id=1, source_target_pairs={{0,16},{1,17},{2,18},{3,19},{4,20},{5,21},{6,22},{7,23},{8,24},{9,... | collective-permute-start | bytes 417800 | tf_op jit(solution)/shard_map/ppermute | solution.py:67
  84.5 8.2 %collective-permute-start.26 = (bf16[32,2176]{1,0:T(8,128)(2,1)S(1)}, bf16[32,2176]{1,0:T(8,128)(2,1)S(1)}, u32[]{:S(2)}, u32[]{:S(2)}) collective-permute-start(bf16[32,2176]{1,0:T(8,128)(2,1)S(1)} %add_convert_fusion.1), channel_id=1, source_target_pairs={{0,6},{1,7},{2,4},{3,5},{4,2},{5,3},{6,0},{7,1},{8,14},{9,15},{10,... | collective-permute-start | bytes 417800 | tf_op jit(solution)/shard_map/ppermute | solution.py:67
  (24 other events, 79.2 us)
